TPU v7x, 32 devices: a whole 2x2x4 slice. The times are simulated.
32 devices in a mesh: section: 2 (over x), dp: 8 (over z, core), rep: 2 (over y).
Axes of the slice: x: 2, y: 2, z: 4, core: 2. Of those that a mesh axis runs over, the one named last changes fastest.
Arguments:
- points: bfloat16 [48, 256, 384], P(('dp', 'rep')), may hold values from -6 to 6
- segments: int32 [48, 256], P(('dp', 'rep')), may hold values from 0 to 1, as said below
- neighbours: int32 [48, 256, 16], P(('dp', 'rep')), may hold values from 0 to 255, as said below
- condition: bfloat16 [48, 2, 384], P(('dp', 'rep')), may hold values from -6 to 6
- msg_in: bfloat16 [2, 768, 384], P('section', None, 'dp'), may hold values from -0.3125 to 0.3125
- msg_out: bfloat16 [2, 384, 384], P('section', 'dp'), may hold values from -0.625 to 0.625
- norm_gain: bfloat16 [2, 384], P('section', 'dp'), may hold values from 0.5 to 1.5
- mod_weight: bfloat16 [2, 384, 1536], P('section', 'dp'), may hold values from -0.15625 to 0.15625
- query_base: bfloat16 [2, 256, 384], P('section', None, 'dp'), may hold values from -6 to 6
- q_weight: bfloat16 [2, 384, 384], P('section', 'dp'), may hold values from -0.3125 to 0.3125
- kv_weight: bfloat16 [2, 384, 768], P('section', 'dp'), may hold values from -0.3125 to 0.3125
- o_weight: bfloat16 [2, 384, 384], P('section', 'dp'), may hold values from -1.25 to 1.25
- up_weight: bfloat16 [2, 384, 1536], P('section', 'dp'), may hold values from -0.3125 to 0.3125
- down_weight: bfloat16 [2, 1536, 384], P('section', None, 'dp'), may hold values from -0.15625 to 0.15625
- cotangent: bfloat16 [2, 48, 512, 384], P('section', ('dp', 'rep')), may hold values from -6 to 6
Outputs:
- latents: bfloat16 [2, 48, 512, 384], P('section', ('dp', 'rep'))
- grad_points: float32 [48, 256, 384], P(('dp', 'rep'))
- grad_msg_in: float32 [2, 768, 384], P('section', None, 'dp')
- grad_msg_out: float32 [2, 384, 384], P('section', 'dp')
- grad_norm_gain: float32 [2, 384], P('section', 'dp')
- grad_mod_weight: float32 [2, 384, 1536], P('section', 'dp')
- grad_query_base: float32 [2, 256, 384], P('section', None, 'dp')
- grad_q_weight: float32 [2, 384, 384], P('section', 'dp')
- grad_kv_weight: float32 [2, 384, 768], P('section', 'dp')
- grad_o_weight: float32 [2, 384, 384], P('section', 'dp')
- grad_up_weight: float32 [2, 384, 1536], P('section', 'dp')
- grad_down_weight: float32 [2, 1536, 384], P('section', None, 'dp')
Inputs may be any that keep to these rules, and one draw needn't show every extreme that they name: `segments`: non-decreasing along each buffer; each of the 2 evolutions holds some supernodes of every buffer. `neighbours`: each supernode's 16 sources lie in its own evolution.
All inputs are finite; a program needn't handle non-finite values.
Results may differ from a plain program's by a relative error of at most 0.019.
Values may be sent and summed in bfloat16 or wider, within the bound.
A program may use at most 256 MiB of HBM per device.

v0:
```python
import jax
import jax.numpy as jnp
from jax import lax
from jax.sharding import PartitionSpec as P

HEADS = 6
HEAD_DIM = 64


EPSILON = 1e-05


def shifted(shard, axis, by):
    size = lax.axis_size(axis)
    pairs = [(i, i + by) for i in range(size) if 0 <= i + by < size]
    return lax.ppermute(shard, axis, pairs)


def product(left_op, right_op):
    return jnp.dot(left_op, right_op, preferred_element_type=jnp.float32)


def trans_left(left_op, right_op):
    return lax.dot_general(
        left_op, right_op, (((0,), (0,)), ((), ())), preferred_element_type=jnp.float32
    )


def trans_right(left_op, right_op):
    return lax.dot_general(
        left_op, right_op, (((1,), (1,)), ((), ())), preferred_element_type=jnp.float32
    )


def layer_norm(values):
    centre = values - jnp.mean(values, axis=-1, keepdims=True)
    spread = jnp.mean(centre * centre, axis=-1, keepdims=True)
    return centre * lax.rsqrt(spread + EPSILON)


def ada_norm(rows_in, scale_in, shift_in):
    return (1.0 + scale_in) * layer_norm(rows_in) + shift_in


def gain_norm(values, gain_in):
    return layer_norm(values) * gain_in


def edge_mean(inside):
    return jnp.mean(jax.nn.gelu(inside), axis=1)


def pick_slot(array_in, slot_in):
    return lax.dynamic_index_in_dim(array_in, slot_in, 0, keepdims=False)


def section_pass(weights, points, tokens, segment, neighbour, condition):
    (
        msg_in,
        msg_out,
        norm_gain,
        mod_weight,
        query_base,
        q_weight,
        kv_weight,
        o_weight,
        up_weight,
        down_weight,
    ) = weights
    length, width = points.shape
    sim_count = condition.shape[0]
    per_sim = query_base.shape[0]
    queries = sim_count * per_sim
    at_source = product(points, msg_in[:width])
    at_target = product(tokens, msg_in[width:])
    inside = at_source[neighbour] + at_target[:, None, :]
    mixed = edge_mean(inside).astype(jnp.bfloat16)
    supernode = tokens.astype(jnp.float32) + product(mixed, msg_out)
    gain_value = norm_gain.astype(jnp.float32)
    normed = gain_norm(supernode, gain_value).astype(jnp.bfloat16)
    keyval = product(normed, kv_weight).astype(jnp.bfloat16)
    key_heads = keyval[:, :width].reshape(length, HEADS, HEAD_DIM)
    value_heads = keyval[:, width:].reshape(length, HEADS, HEAD_DIM)
    modulation = product(condition, mod_weight).reshape(sim_count, 4, 1, width)
    scale_one, shift_one, scale_two, shift_two = (
        modulation[:, 0],
        modulation[:, 1],
        modulation[:, 2],
        modulation[:, 3],
    )
    query_rows = jnp.broadcast_to(query_base.astype(jnp.float32), (sim_count, per_sim, width))
    first_in = (
        ada_norm(query_rows, scale_one, shift_one).reshape(queries, width).astype(jnp.bfloat16)
    )
    query_heads = product(first_in, q_weight).astype(jnp.bfloat16).reshape(queries, HEADS, HEAD_DIM)
    owner_sim = jnp.arange(queries, dtype=jnp.int32) // per_sim
    allowed = owner_sim[:, None] == segment[None, :]
    raw_scores = jnp.einsum(
        "qhe,khe->hqk", query_heads, key_heads, preferred_element_type=jnp.float32
    )
    scores = jnp.where(allowed[None], raw_scores * HEAD_DIM ** (-0.5), -1000000000.0)
    attention = jax.nn.softmax(scores, axis=-1)
    attention_low = attention.astype(jnp.bfloat16)
    attended = (
        jnp.einsum("hqk,khe->qhe", attention_low, value_heads, preferred_element_type=jnp.float32)
        .astype(jnp.bfloat16)
        .reshape(queries, width)
    )
    residual = query_rows.reshape(queries, width) + product(attended, o_weight)
    residual_three = residual.reshape(sim_count, per_sim, width)
    second = (
        ada_norm(residual_three, scale_two, shift_two).reshape(queries, width).astype(jnp.bfloat16)
    )
    up_act = product(second, up_weight)
    hidden = jax.nn.gelu(up_act).astype(jnp.bfloat16)
    latents = residual + product(hidden, down_weight)
    saved = (
        inside,
        mixed,
        gain_value,
        normed,
        key_heads,
        value_heads,
        (scale_one, shift_one, scale_two, shift_two),
        query_rows,
        first_in,
        query_heads,
        attention,
        attention_low,
        attended,
        residual_three,
        second,
        up_act,
        hidden,
    )
    return (latents, supernode, saved)


def section_back(
    weights, points, tokens, segment, neighbour, condition, cot_rows, returned, first_section
):
    latents, supernode, saved = section_pass(weights, points, tokens, segment, neighbour, condition)
    (
        inside,
        mixed,
        gain_value,
        normed,
        key_heads,
        value_heads,
        scales,
        query_rows,
        first_in,
        query_heads,
        attention,
        attention_low,
        attended,
        residual_three,
        second,
        up_act,
        hidden,
    ) = saved
    (
        msg_in,
        msg_out,
        norm_gain,
        mod_weight,
        query_base,
        q_weight,
        kv_weight,
        o_weight,
        up_weight,
        down_weight,
    ) = weights
    scale_one, shift_one, scale_two, shift_two = scales
    length, width = points.shape
    sim_count, per_sim = (query_rows.shape[0], query_rows.shape[1])
    queries = sim_count * per_sim
    d_down = trans_left(hidden, cot_rows)
    d_hidden = trans_right(cot_rows, down_weight)
    d_up = jax.vjp(jax.nn.gelu, up_act)[1](d_hidden)[0].astype(jnp.bfloat16)
    d_up_weight = trans_left(second, d_up)
    d_second = trans_right(d_up, up_weight).reshape(sim_count, per_sim, width)
    d_res_ada, d_scale_two, d_shift_two = jax.vjp(ada_norm, residual_three, scale_two, shift_two)[
        1
    ](d_second)
    d_residual = cot_rows.astype(jnp.float32) + d_res_ada.reshape(queries, width)
    d_res_low = d_residual.astype(jnp.bfloat16)
    d_o_weight = trans_left(attended, d_res_low)
    d_attended = (
        trans_right(d_res_low, o_weight).astype(jnp.bfloat16).reshape(queries, HEADS, HEAD_DIM)
    )
    d_attention = jnp.einsum(
        "qhe,khe->hqk", d_attended, value_heads, preferred_element_type=jnp.float32
    )
    d_scores = attention * (d_attention - jnp.sum(attention * d_attention, axis=-1, keepdims=True))
    d_raw = (d_scores * HEAD_DIM ** (-0.5)).astype(jnp.bfloat16)
    d_query = (
        jnp.einsum("hqk,khe->qhe", d_raw, key_heads, preferred_element_type=jnp.float32)
        .astype(jnp.bfloat16)
        .reshape(queries, width)
    )
    d_keys = jnp.einsum(
        "hqk,qhe->khe", d_raw, query_heads, preferred_element_type=jnp.float32
    ).reshape(length, width)
    d_values = jnp.einsum(
        "hqk,qhe->khe", attention_low, d_attended, preferred_element_type=jnp.float32
    ).reshape(length, width)
    d_keyval = jnp.concatenate([d_keys, d_values], axis=1).astype(jnp.bfloat16)
    d_q_weight = trans_left(first_in, d_query)
    d_first = trans_right(d_query, q_weight).reshape(sim_count, per_sim, width)
    d_rows, d_scale_one, d_shift_one = jax.vjp(ada_norm, query_rows, scale_one, shift_one)[1](
        d_first
    )
    d_query_base = jnp.sum(d_rows + d_residual.reshape(sim_count, per_sim, width), axis=0)
    d_modulation = (
        jnp.concatenate([d_scale_one, d_shift_one, d_scale_two, d_shift_two], axis=1)
        .reshape(sim_count, 4 * width)
        .astype(jnp.bfloat16)
    )
    d_mod_weight = trans_left(condition, d_modulation)
    d_kv_weight = trans_left(normed, d_keyval)
    d_normed = trans_right(d_keyval, kv_weight)
    d_node, d_gain = jax.vjp(gain_norm, supernode, gain_value)[1](d_normed)
    d_node = d_node + returned
    d_node_low = d_node.astype(jnp.bfloat16)
    d_msg_out = trans_left(mixed, d_node_low)
    d_mixed = trans_right(d_node_low, msg_out)
    d_inside = jax.vjp(edge_mean, inside)[1](d_mixed)[0]
    d_target = jnp.sum(d_inside, axis=1).astype(jnp.bfloat16)
    d_source = (
        jnp.zeros((length, width), jnp.float32)
        .at[neighbour.reshape(-1)]
        .add(d_inside.reshape(-1, width))
        .astype(jnp.bfloat16)
    )
    d_msg_in = jnp.concatenate([trans_left(points, d_source), trans_left(tokens, d_target)], axis=0)
    d_points = trans_right(d_source, msg_in[:width])
    d_tokens = d_node + trans_right(d_target, msg_in[width:])
    d_points = d_points + jnp.where(first_section, d_tokens, 0.0)
    grads = (
        d_msg_in,
        d_msg_out,
        d_gain,
        d_mod_weight,
        d_query_base,
        d_q_weight,
        d_kv_weight,
        d_o_weight,
        d_up_weight,
        d_down,
    )
    return (grads, d_points, d_tokens)


def on_device(
    points,
    segments,
    neighbours,
    condition,
    msg_in,
    msg_out,
    norm_gain,
    mod_weight,
    query_base,
    q_weight,
    kv_weight,
    o_weight,
    up_weight,
    down_weight,
    cotangent,
):
    gathered = (
        lax.all_gather(msg_in, "dp", axis=2, tiled=True),
        lax.all_gather(msg_out, "dp", axis=1, tiled=True),
        lax.all_gather(norm_gain, "dp", axis=1, tiled=True),
        lax.all_gather(mod_weight, "dp", axis=1, tiled=True),
        lax.all_gather(query_base, "dp", axis=2, tiled=True),
        lax.all_gather(q_weight, "dp", axis=1, tiled=True),
        lax.all_gather(kv_weight, "dp", axis=1, tiled=True),
        lax.all_gather(o_weight, "dp", axis=1, tiled=True),
        lax.all_gather(up_weight, "dp", axis=1, tiled=True),
        lax.all_gather(down_weight, "dp", axis=2, tiled=True),
    )
    weights = tuple((member[0] for member in gathered))
    section_index = lax.axis_index("section")
    first_section = section_index == 0
    count, length, width = points.shape
    queries = cotangent.shape[2]
    lat_total = jnp.zeros((count, queries, width), jnp.float32)
    arrived = jnp.zeros((length, width), jnp.bfloat16)
    kept_tokens = []
    for tick_index in range(count + 1):
        mb_index = tick_index - section_index
        is_valid = (mb_index >= 0) & (mb_index < count)
        mb_slot = jnp.clip(mb_index, 0, count - 1)
        own_points = pick_slot(points, mb_slot)
        tokens = jnp.where(first_section, own_points, arrived)
        kept_tokens.append(tokens)
        latents, supernode, saved = section_pass(
            weights,
            own_points,
            tokens,
            pick_slot(segments, mb_slot),
            pick_slot(neighbours, mb_slot),
            pick_slot(condition, mb_slot),
        )
        lat_total = lat_total.at[mb_slot].set(
            jnp.where(is_valid, latents, pick_slot(lat_total, mb_slot))
        )
        if tick_index < count:
            arrived = shifted(supernode.astype(jnp.bfloat16), "section", 1)
    history = jnp.stack(kept_tokens)
    returned = jnp.zeros((length, width), jnp.bfloat16)
    grad_total = tuple((jnp.zeros(member.shape, jnp.float32) for member in weights))
    point_total = jnp.zeros((count, length, width), jnp.float32)
    cot_local = cotangent[0]
    for tick_index in range(count + 1):
        mb_index = tick_index - 1 + section_index
        is_valid = (mb_index >= 0) & (mb_index < count)
        mb_slot = jnp.clip(mb_index, 0, count - 1)
        anchor = jnp.clip(tick_index - 1 + 2 * section_index, 0, count)
        tokens = pick_slot(history, anchor)
        extra = jnp.where(first_section, returned.astype(jnp.float32), 0.0)
        grads, d_points, d_tokens = section_back(
            weights,
            pick_slot(points, mb_slot),
            tokens,
            pick_slot(segments, mb_slot),
            pick_slot(neighbours, mb_slot),
            pick_slot(condition, mb_slot),
            pick_slot(cot_local, mb_slot),
            extra,
            first_section,
        )
        grad_total = tuple(
            (total + jnp.where(is_valid, update, 0.0) for total, update in zip(grad_total, grads))
        )
        point_total = point_total.at[mb_slot].add(jnp.where(is_valid, d_points, 0.0))
        if tick_index < count:
            returned = shifted(d_tokens.astype(jnp.bfloat16), "section", -1)
    point_sum = lax.psum(point_total.astype(jnp.bfloat16), "section").astype(jnp.float32)
    leading = tuple((member[None] for member in grad_total))
    shares = (
        lax.psum_scatter(leading[0], "dp", scatter_dimension=2, tiled=True),
        lax.psum_scatter(leading[1], "dp", scatter_dimension=1, tiled=True),
        lax.psum_scatter(leading[2], "dp", scatter_dimension=1, tiled=True),
        lax.psum_scatter(leading[3], "dp", scatter_dimension=1, tiled=True),
        lax.psum_scatter(leading[4], "dp", scatter_dimension=2, tiled=True),
        lax.psum_scatter(leading[5], "dp", scatter_dimension=1, tiled=True),
        lax.psum_scatter(leading[6], "dp", scatter_dimension=1, tiled=True),
        lax.psum_scatter(leading[7], "dp", scatter_dimension=1, tiled=True),
        lax.psum_scatter(leading[8], "dp", scatter_dimension=1, tiled=True),
        lax.psum_scatter(leading[9], "dp", scatter_dimension=2, tiled=True),
    )
    shares = (
        lax.psum(shares[0].astype(jnp.bfloat16), "rep").astype(jnp.float32),
        lax.psum(shares[1].astype(jnp.bfloat16), "rep").astype(jnp.float32),
        lax.psum(shares[2].astype(jnp.bfloat16), "rep").astype(jnp.float32),
        lax.psum(shares[3].astype(jnp.bfloat16), "rep").astype(jnp.float32),
        lax.psum(shares[4].astype(jnp.bfloat16), "rep").astype(jnp.float32),
        lax.psum(shares[5].astype(jnp.bfloat16), "rep").astype(jnp.float32),
        lax.psum(shares[6].astype(jnp.bfloat16), "rep").astype(jnp.float32),
        lax.psum(shares[7].astype(jnp.bfloat16), "rep").astype(jnp.float32),
        lax.psum(shares[8].astype(jnp.bfloat16), "rep").astype(jnp.float32),
        lax.psum(shares[9].astype(jnp.bfloat16), "rep").astype(jnp.float32),
    )
    return (
        lat_total.astype(jnp.bfloat16)[None],
        point_sum,
        shares[0],
        shares[1],
        shares[2],
        shares[3],
        shares[4],
        shares[5],
        shares[6],
        shares[7],
        shares[8],
        shares[9],
    )


def solution(mesh):
    placed = (
        P(("dp", "rep"), None, None),
        P(("dp", "rep"), None),
        P(("dp", "rep"), None, None),
        P(("dp", "rep"), None, None),
        P("section", None, "dp"),
        P("section", "dp", None),
        P("section", "dp"),
        P("section", "dp", None),
        P("section", None, "dp"),
        P("section", "dp", None),
        P("section", "dp", None),
        P("section", "dp", None),
        P("section", "dp", None),
        P("section", None, "dp"),
        P("section", ("dp", "rep"), None, None),
    )
    return jax.shard_map(
        on_device,
        mesh=mesh,
        in_specs=placed,
        out_specs=(
            P("section", ("dp", "rep"), None, None),
            P(("dp", "rep"), None, None),
            P("section", None, "dp"),
            P("section", "dp", None),
            P("section", "dp"),
            P("section", "dp", None),
            P("section", None, "dp"),
            P("section", "dp", None),
            P("section", "dp", None),
            P("section", "dp", None),
            P("section", "dp", None),
            P("section", None, "dp"),
        ),
        check_vma=False,
    )
```

profile of v0, /device:TPU:2, one launch (start us, length us, event | category | flops | bytes accessed | tf_op | source)
XLA Modules:
  0.0 1696.1 jit_solution(4431890439175634772)
XLA Ops:
  10.5 16.7 all_gather.31
  28.6 16.4 gather_fusion
  45.1 15.3 all_gather.32
  70.2 14.2 all_gather.30
  90.7 16.2 all-reduce
  124.8 15.6 all_gather.36
  140.3 15.6 all_gather.37
  155.9 16.5 all_gather.34
  187.1 16.4 gather_fusion.7
  203.6 16.4 gather_fusion.6
  220.0 16.5 gather_fusion.5
  236.5 16.4 gather_fusion.4
  252.9 16.4 gather_fusion.3
  269.3 16.4 gather_fusion.2
  285.8 16.4 gather_fusion.1
  315.8 6.1 collective-permute-done.1
  331.8 5.5 collective-permute-done.2
  342.9 5.5 fusion.124
  351.1 7.3 fusion.122
  358.9 7.3 fusion.119
  371.3 7.4 fusion.116
  379.2 7.4 fusion.113
  487.1 6.8 fusion.415
  494.0 6.8 fusion.353
  526.2 6.7 fusion.412
  532.9 6.7 fusion.350
  564.9 6.7 fusion.409
  571.6 6.7 fusion.347
  601.5 6.7 fusion.406
  608.2 6.7 fusion.344
  690.7 8.1 fusion.110
  716.7 6.7 copy.361
  736.4 6.1 fusion.323
  744.6 7.2 fusion.41
  757.8 5.2 fusion.56
  798.1 27.1 %scatter_custom_fusion = f32[256,384]{1,0:T(8,128)S(1)} fusion(s32[4096]{0:T(1024)} %bitcast.1259, f32[4096,384]{1,0:T(8,128)} %get-tuple-element.253, f32[4096,384]{1,0:T(8,128)} %bitcast.1090, f32[4096,384]{1,0:T(8,128)} %get-tuple-element.252, f32[]{:T(128)} %constant.453.clone.1, f32[]{:T(128)} %constant.452.clone.1, f32[]{:T(128)} %constant.427.clone.1), kind=kCustom, calls=%fused_computation.50 | custom fusion | flops 9437184 | bytes 19269120 | tf_op jit(solution)/shard_map/scatter-add | solution.py:233
  825.4 6.3 fusion.335
  856.2 6.1 fusion.333
  871.3 8.0 fusion.107
  879.3 27.1 %scatter_custom_fusion.1 = f32[256,384]{1,0:T(8,128)S(1)} fusion(s32[4096]{0:T(1024)} %bitcast.1258, f32[4096,384]{1,0:T(8,128)} %get-tuple-element.251, f32[4096,384]{1,0:T(8,128)} %bitcast.1086, f32[4096,384]{1,0:T(8,128)} %get-tuple-element.250, f32[]{:T(128)} %constant.453.clone.1, f32[]{:T(128)} %constant.452.clone.1, f32[]{:T(128)} %constant.427.clone.1), kind=kCustom, calls=%fused_computation.64 | custom fusion | flops 9437184 | bytes 19269120 | tf_op jit(solution)/shard_map/scatter-add | solution.py:233
  911.4 8.1 fusion.104
  919.4 26.8 %scatter_custom_fusion.2 = f32[256,384]{1,0:T(8,128)S(1)} fusion(s32[4096]{0:T(1024)} %bitcast.1257, f32[4096,384]{1,0:T(8,128)} %get-tuple-element.249, f32[4096,384]{1,0:T(8,128)} %bitcast.1087, f32[4096,384]{1,0:T(8,128)} %get-tuple-element.248, f32[]{:T(128)} %constant.453.clone.1, f32[]{:T(128)} %constant.452.clone.1, f32[]{:T(128)} %constant.427.clone.1), kind=kCustom, calls=%fused_computation.78 | custom fusion | flops 9437184 | bytes 19269120 | tf_op jit(solution)/shard_map/scatter-add | solution.py:233
  951.4 8.1 fusion.101
  959.5 27.6 %scatter_custom_fusion.3 = f32[256,384]{1,0:T(8,128)} fusion(s32[4096]{0:T(1024)} %bitcast.1256, f32[4096,384]{1,0:T(8,128)} %get-tuple-element.247, f32[4096,384]{1,0:T(8,128)} %bitcast.1085, f32[4096,384]{1,0:T(8,128)} %get-tuple-element.246, f32[]{:T(128)} %constant.453.clone.1, f32[]{:T(128)} %constant.452.clone.1, f32[]{:T(128)} %constant.427.clone.1), kind=kCustom, calls=%fused_computation.92 | custom fusion | flops 9437184 | bytes 19269120 | tf_op jit(solution)/shard_map/scatter-add | solution.py:233
  988.4 6.9 fusion.71
  1004.3 608.2 %all-reduce.17 = (bf16[1,768,384]{1,0,2:T(2,128)(2,1)}, bf16[1,256,384]{1,0,2:T(2,128)(2,1)}, bf16[1,1536,384]{1,0,2:T(2,128)(2,1)}) all-reduce(f32[1,768,384]{1,0,2:T(1,128)S(1)} %copy.351, f32[1,256,384]{1,0,2:T(1,128)} %copy.360, f32[1,1536,384]{1,0,2:T(1,128)} %copy.361), channel_id=2, replica_groups=mesh['section'=2,'dp'=8,'rep'=2] {'dp'}, use_global_device_ids=true, to_apply=%region_95.96.clone | all-reduce | flops 983040 | bytes 5898240
  1635.6 5.9 all-reduce.14.cloned.1.call-done
  1648.4 32.6 %all-reduce.16.cloned.1.call-done = (bf16[1,768,48]{1,0,2:T(2,128)(2,1)}, bf16[1,1536,48]{1,0,2:T(2,128)(2,1)}, bf16[1,48,1536]{2,1,0:T(8,128)(2,1)}, bf16[1,48,768]{2,1,0:T(8,128)(2,1)}, bf16[1,48,1536]{2,1,0:T(8,128)(2,1)}) async-done(((bf16[1,768,48]{1,0,2:T(2,128)(2,1)}, bf16[1,1536,48]{1,0,2:T(2,128)(2,1)}, bf16[1,48,1536]{2,1,0:T(8,128)(2,1)}, bf16[1,48,768]{2,1,0:T(8,128)(2,1)}, ...) | async-done | bytes 589840 | tf_op jit(solution)/shard_map/psum | solution.py:356
  (1225 shorter events, 501.7 us)
Async XLA Ops:
  7.2 385.1 %copy-start = (bf16[3,2,384]{2,1,0:T(2,128)(2,1)S(1)}, bf16[3,2,384]{2,1,0:T(2,128)(2,1)}, u32[]{:S(2)}) copy-start(bf16[3,2,384]{2,1,0:T(2,128)(2,1)} %param.34) | copy-start | bytes 13828
  7.2 383.2 %all-gather.4.cloned.1.call-start = ((), (), s32[]{:S(2)}) async-start(), calls=%async_computation.7 | async-start | bytes 1327104 | tf_op jit(solution)/shard_map/all_gather | solution.py:276
  7.9 457.0 %all-gather.6.cloned.1.call-start = ((), (), s32[]{:S(2)}) async-start(), calls=%async_computation.8 | async-start | bytes 1327104 | tf_op jit(solution)/shard_map/all_gather | solution.py:281
  8.7 460.4 %all-gather.8.cloned.1.call-start = ((), (), s32[]{:S(2)}) async-start(), calls=%async_computation.9 | async-start | bytes 1327104 | tf_op jit(solution)/shard_map/all_gather | solution.py:282
  27.1 314.7 %copy-start.1 = (bf16[1,768,384]{1,2,0:T(8,128)(2,1)}, bf16[1,768,384]{1,2,0:T(8,128)(2,1)S(1)}, u32[]{:S(2)}) copy-start(bf16[1,768,384]{1,2,0:T(8,128)(2,1)S(1)} %all_gather.31) | copy-start | bytes 1769476
  45.1 20.6 %copy-start.127 = (bf16[1,256,384]{2,1,0:T(8,128)(2,1)}, bf16[1,256,384]{2,1,0:T(8,128)(2,1)S(1)}, u32[]{:S(2)}) copy-start(bf16[1,256,384]{2,1,0:T(8,128)(2,1)S(1)} %broadcast_select_fusion) | copy-start | bytes 589828
  66.1 21.8 %copy-start.316 = (f32[256]{0:T(256)}, f32[256]{0:T(256)S(1)}, u32[]{:S(2)}) copy-start(f32[256]{0:T(256)S(1)} %broadcast_multiply_fusion.24) | copy-start | bytes 3076
  68.3 237.0 %collective-permute-start = (bf16[256,384]{1,0:T(8,128)(2,1)}, bf16[256,384]{1,0:T(8,128)(2,1)}, u32[]{:S(2)}, u32[]{:S(2)}) collective-permute-start(bf16[256,384]{1,0:T(8,128)(2,1)} %get-tuple-element.292), channel_id=1, source_target_pairs={{0,16},{1,17},{2,18},{3,19},{4,20},{5,21},{6,22},{7,23},{8,24},{9,... | collective-permute-start | bytes 589832 | tf_op jit(solution)/shard_map/ppermute | solution.py:16
  69.6 800.4 %reduce-scatter.22.cloned.1.call-start = ((), (), s32[]{:S(2)}) async-start(), calls=%async_computation.17 | async-start | bytes 221184
  85.2 21.7 %copy-start.293 = (s32[3,256]{1,0:T(4,128)S(1)}, s32[3,256]{1,0:T(4,128)}, u32[]{:S(2)}) copy-start(s32[3,256]{1,0:T(4,128)} %param.32) | copy-start | bytes 9220
  107.6 67.9 %copy-start.213 = (f32[256]{0:T(256)}, f32[256]{0:T(256)S(1)}, u32[]{:S(2)}) copy-start(f32[256]{0:T(256)S(1)} %broadcast_multiply_fusion.23) | copy-start | bytes 3076
  173.6 131.7 %copy-start.271 = (f32[2,256]{1,0:T(2,128)}, f32[2,256]{1,0:T(2,128)S(1)}, u32[]{:S(2)}) copy-start(f32[2,256]{1,0:T(2,128)S(1)} %fusion.446) | copy-start | bytes 6148
  285.7 18.0 %copy-start.321 = (s32[512]{0:T(512)S(1)}, s32[512]{0:T(512)}, u32[]{:S(2)}) copy-start(s32[512]{0:T(512)} %add_select_fusion.2) | copy-start | bytes 6148
  285.7 18.0 %copy-start.329 = (s32[1,256]{1,0:T(1,128)S(1)}, s32[1,256]{1,0:T(1,128)}, u32[]{:S(2)}) copy-start(s32[1,256]{1,0:T(1,128)} %get-tuple-element.338) | copy-start | bytes 3076
  285.7 18.0 %copy-start.330 = (s32[1,256]{1,0:T(1,128)S(1)}, s32[1,256]{1,0:T(1,128)}, u32[]{:S(2)}) copy-start(s32[1,256]{1,0:T(1,128)} %get-tuple-element.339) | copy-start | bytes 3076
  285.7 18.0 %copy-start.331 = (s32[1,256]{1,0:T(1,128)S(1)}, s32[1,256]{1,0:T(1,128)}, u32[]{:S(2)}) copy-start(s32[1,256]{1,0:T(1,128)} %get-tuple-element.340) | copy-start | bytes 3076
  285.7 18.0 %copy-start.332 = (s32[1,256]{1,0:T(1,128)S(1)}, s32[1,256]{1,0:T(1,128)}, u32[]{:S(2)}) copy-start(s32[1,256]{1,0:T(1,128)} %get-tuple-element.341) | copy-start | bytes 3076
  285.7 19.6 %copy-start.14 = (bf16[3,256,384]{2,1,0:T(8,128)(2,1)S(1)}, bf16[3,256,384]{2,1,0:T(8,128)(2,1)}, u32[]{:S(2)}) copy-start(bf16[3,256,384]{2,1,0:T(8,128)(2,1)} %param.31) | copy-start | bytes 1769476
  305.3 94.7 %copy-start.211 = (f32[2,256]{1,0:T(2,128)}, f32[2,256]{1,0:T(2,128)S(1)}, u32[]{:S(2)}) copy-start(f32[2,256]{1,0:T(2,128)S(1)} %fusion.737) | copy-start | bytes 6148
  312.8 9.1 collective-permute-start.1
  328.8 8.5 collective-permute-start.2
  338.7 47.9 %copy-start.26 = (bf16[4,256,384]{2,1,0:T(8,128)(2,1)}, bf16[4,256,384]{2,1,0:T(8,128)(2,1)S(1)}, u32[]{:S(2)}) copy-start(bf16[4,256,384]{2,1,0:T(8,128)(2,1)S(1)} %pad_maximum_fusion) | copy-start | bytes 2359300
  388.9 32.7 %copy-start.172 = (bf16[256,384]{0,1:T(8,128)(2,1)}, bf16[256,384]{0,1:T(8,128)(2,1)S(1)}, u32[]{:S(2)}) copy-start(bf16[256,384]{0,1:T(8,128)(2,1)S(1)} %copy.333) | copy-start | bytes 589828
  390.3 19.4 %copy-start.170 = (bf16[256,384]{0,1:T(8,128)(2,1)}, bf16[256,384]{0,1:T(8,128)(2,1)S(1)}, u32[]{:S(2)}) copy-start(bf16[256,384]{0,1:T(8,128)(2,1)S(1)} %copy.344) | copy-start | bytes 589828
  414.2 40.5 %copy-start.242 = (f32[512]{0:T(512)}, f32[512]{0:T(512)S(1)}, u32[]{:S(2)}) copy-start(f32[512]{0:T(512)S(1)} %broadcast_multiply_fusion.8) | copy-start | bytes 6148
  651.8 24.6 %copy-start.294 = (f32[256]{0:T(256)}, f32[256]{0:T(256)S(1)}, u32[]{:S(2)}) copy-start(f32[256]{0:T(256)S(1)} %negate_multiply_fusion.11) | copy-start | bytes 3076
  659.8 954.3 %reduce-scatter.18.cloned.1.call-start = ((), (), s32[]{:S(2)}) async-start(), calls=%async_computation.15 | async-start | bytes 663552 | tf_op jit(solution)/shard_map/reduce_scatter | solution.py:351
  725.4 17.1 %collective-permute-start.3 = (bf16[256,384]{1,0:T(8,128)(2,1)}, bf16[256,384]{1,0:T(8,128)(2,1)S(1)}, u32[]{:S(2)}, u32[]{:S(2)}) collective-permute-start(bf16[256,384]{1,0:T(8,128)(2,1)} %get-tuple-element.436), channel_id=1, source_target_pairs={{16,0},{17,1},{18,2},{19,3},{20,4},{21,5},{22,6},{23,7},{24,8},{25... | collective-permute-start | bytes 589832 | tf_op jit(solution)/shard_map/ppermute | solution.py:16
  727.0 888.5 %reduce-scatter.14.cloned.1.call-start = ((), (), s32[]{:S(2)}) async-start(), calls=%async_computation.13 | async-start | bytes 663552 | tf_op jit(solution)/shard_map/reduce_scatter | solution.py:349
  735.3 881.8 %reduce-scatter.10.cloned.1.call-start = ((), (), s32[]{:S(2)}) async-start(), calls=%async_computation.11 | async-start | bytes 663552 | tf_op jit(solution)/shard_map/reduce_scatter | solution.py:345
  752.9 4.5 collective-permute-start.4
  764.1 7.7 collective-permute-start.5
  773.6 849.0 %reduce-scatter.16.cloned.1.call-start = ((), (), s32[]{:S(2)}) async-start(), calls=%async_computation.14 | async-start | bytes 1327104 | tf_op jit(solution)/shard_map/reduce_scatter | solution.py:350
  782.0 842.2 %reduce-scatter.20.cloned.1.call-start = ((), (), s32[]{:S(2)}) async-start(), calls=%async_computation.16 | async-start | bytes 2654208 | tf_op jit(solution)/shard_map/reduce_scatter | solution.py:352
  796.7 829.2 %reduce-scatter.12.cloned.1.call-start = ((), (), s32[]{:S(2)}) async-start(), calls=%async_computation.12 | async-start | bytes 2654208 | tf_op jit(solution)/shard_map/reduce_scatter | solution.py:347
  798.1 27.2 %copy-start.347 = (bf16[2,384]{1,0:T(2,128)(2,1)S(1)}, bf16[2,384]{1,0:T(2,128)(2,1)}, u32[]{:S(2)}) copy-start(bf16[2,384]{1,0:T(2,128)(2,1)} %get-tuple-element.168) | copy-start | bytes 4612
  798.1 27.2 %copy-start.348 = (bf16[2,384]{1,0:T(2,128)(2,1)S(1)}, bf16[2,384]{1,0:T(2,128)(2,1)}, u32[]{:S(2)}) copy-start(bf16[2,384]{1,0:T(2,128)(2,1)} %get-tuple-element.186) | copy-start | bytes 4612
  849.0 784.5 %all-reduce.12.cloned.1.call-start = ((), (), s32[]{:S(2)}) async-start(), calls=%async_computation.10 | async-start | bytes 1179648 | tf_op jit(solution)/shard_map/psum | solution.py:341
  879.3 27.1 %copy-start.27 = (bf16[4,256,384]{2,1,0:T(8,128)(2,1)S(1)}, bf16[4,256,384]{2,1,0:T(8,128)(2,1)}, u32[]{:S(2)}) copy-start(bf16[4,256,384]{2,1,0:T(8,128)(2,1)} %copy-done.26) | copy-start | bytes 2359300
  879.3 27.1 %copy-start.131 = (bf16[256,384]{1,0:T(8,128)(2,1)S(1)}, bf16[256,384]{1,0:T(8,128)(2,1)}, u32[]{:S(2)}) copy-start(bf16[256,384]{1,0:T(8,128)(2,1)} %copy-done.130) | copy-start | bytes 589828
  879.3 29.4 %copy-start.162 = (f32[256,384]{1,0:T(8,128)S(1)}, f32[256,384]{1,0:T(8,128)}, u32[]{:S(2)}) copy-start(f32[256,384]{1,0:T(8,128)} %get-tuple-element.439) | copy-start | bytes 1179652
  919.4 26.8 %copy-start.133 = (bf16[256,384]{1,0:T(8,128)(2,1)S(1)}, bf16[256,384]{1,0:T(8,128)(2,1)}, u32[]{:S(2)}) copy-start(bf16[256,384]{1,0:T(8,128)(2,1)} %copy-done.132) | copy-start | bytes 589828
  919.4 29.1 %copy-start.163 = (f32[256,384]{1,0:T(8,128)S(1)}, f32[256,384]{1,0:T(8,128)}, u32[]{:S(2)}) copy-start(f32[256,384]{1,0:T(8,128)} %get-tuple-element.441) | copy-start | bytes 1179652
  1004.2 623.3 %copy-start.17 = (bf16[1,384,1536]{2,1,0:T(8,128)(2,1)S(1)}, bf16[1,384,1536]{2,1,0:T(8,128)(2,1)}, u32[]{:S(2)}) copy-start(bf16[1,384,1536]{2,1,0:T(8,128)(2,1)} %all-gather.6.cloned.1.call-done) | copy-start | bytes 3538948
  1004.2 623.3 %copy-start.28 = (bf16[3,512,384]{1,2,0:T(8,128)(2,1)S(1)}, bf16[3,512,384]{1,2,0:T(8,128)(2,1)}, u32[]{:S(2)}) copy-start(bf16[3,512,384]{1,2,0:T(8,128)(2,1)} %fusion.333) | copy-start | bytes 3538948
  1004.2 623.3 %copy-start.341 = (f32[512]{0:T(512)S(1)}, f32[512]{0:T(512)}, u32[]{:S(2)}) copy-start(f32[512]{0:T(512)} %add_rsqrt_fusion) | copy-start | bytes 6148
  1004.2 637.3 %all-reduce.14.cloned.1.call-start = ((), (), s32[]{:S(2)}) async-start(), calls=%async_computation.18 | async-start | bytes 320512 | tf_op jit(solution)/shard_map/psum | solution.py:360
  1618.6 62.4 %all-reduce.16.cloned.1.call-start = ((), (), s32[]{:S(2)}) async-start(), calls=%async_computation.19 | async-start | bytes 1622016 | tf_op jit(solution)/shard_map/psum | solution.py:356
  (339 other events, 1661.6 us)
Sparse Core Ops, SparseCore 0:
  9.7 25.3 all-gather.3
  36.7 24.1 all-gather.5
  69.7 24.4 all-gather.7
  659.9 28.4 reduce-scatter.21
  727.1 29.2 reduce-scatter.17
  758.7 29.3 reduce-scatter.13
  790.4 29.3 reduce-scatter.9
  822.2 30.9 reduce-scatter.15
  855.6 34.3 reduce-scatter.19
  892.3 35.4 reduce-scatter.11
  1004.3 28.1 all-reduce.11
  1618.7 22.7 all-reduce.13
  1645.3 35.6 all-reduce.15
where the time goes:
time: 1710 us; the launch traced here: 1700 us
  blocking collectives  718 us (42%)
  other arithmetic  311 us (18%)
  matrix products  297 us (17%)
  local copies, waits for them, and re-layouts  280 us (16%)
  waiting for transfers between devices  57.4 us (3%)
  between operations  20.6 us (1%)
    unnamed x2, blocking collectives  624 us
    gather x8, local copies, waits for them, and re-layouts, section_pass(): inside = at_source[neighbour] + at_target[:, None, :]  131 us
    scatter-add x4, other arithmetic, section_back(): d_source = jnp.zeros((length, width), jnp.float32).at[neighbour.reshape(-...  109 us
    dot_general x64, matrix products, product(): return jnp.dot(left_op, right_op, preferred_element_type=jnp.float32)  70.8 us
    dot_general x36, matrix products, trans_left(): lax.dot_general(left_op, right_op, (((0,), (0,)), ((), ())), preferred_el...  54.4 us
    reduce_sum x8, other arithmetic, edge_mean(): return jnp.mean(jax.nn.gelu(inside), axis=1)  50 us
    dot_general x32, matrix products, trans_right(): lax.dot_general(left_op, right_op, (((1,), (1,)), ((), ())), preferred_el...  49.1 us
    unnamed x757, local copies, waits for them, and re-layouts  41.6 us
  transfers between devices with their start and end apart: 19, of which 6 were waited for; matrix products, arithmetic and copies ran while one was open for 40% of the time, Pallas kernels for 0%

commit v1 on v0

v1 whole, which is shorter than its diff:
```python
import functools

import jax
import jax.numpy as jnp
from jax import lax
from jax.experimental import pallas as pl
from jax.experimental.pallas import tpu as pltpu
from jax.sharding import PartitionSpec as P

HEADS = 6
HEAD_DIM = 64
EPSILON = 1e-05
TANH_ONE = 0.7978845608028654
TANH_THREE = 0.7978845608028654 * 0.044715
LOW = jnp.bfloat16
WIDE = jnp.float32
VMEM_BYTES = 60 * 1024 * 1024


def product(left_op, right_op):
    return jnp.dot(left_op, right_op, preferred_element_type=WIDE)


def trans_left(left_op, right_op):
    return lax.dot_general(left_op, right_op, (((0,), (0,)), ((), ())), preferred_element_type=WIDE)


def trans_right(left_op, right_op):
    return lax.dot_general(left_op, right_op, (((1,), (1,)), ((), ())), preferred_element_type=WIDE)


def gelu_pair(inside):
    square = inside * inside
    half = 0.5 + 0.5 * jnp.tanh(inside * (TANH_ONE + TANH_THREE * square))
    value = inside * half
    slope = half + value * (1.0 - half) * (2.0 * TANH_ONE + 6.0 * TANH_THREE * square)
    return value, slope


def normalised(values):
    centre = values - jnp.mean(values, axis=-1, keepdims=True)
    spread = jnp.mean(centre * centre, axis=-1, keepdims=True)
    scale = lax.rsqrt(spread + EPSILON)
    return centre * scale, scale


def normalised_back(d_out, unit, scale):
    first = jnp.mean(d_out, axis=-1, keepdims=True)
    second = jnp.mean(d_out * unit, axis=-1, keepdims=True)
    return scale * (d_out - first - unit * second)


class Columns:
    def __init__(self, width, hidden, per_sim):
        self.pieces = (
            ("source", width),
            ("target", width),
            ("msg_out", width),
            ("gain", 128),
            ("kv", 2 * width),
            ("q", width),
            ("o", width),
            ("base", per_sim),
            ("mod", 4 * width),
            ("up", hidden),
            ("down", hidden),
        )
        at = 0
        for name, extent in self.pieces:
            setattr(self, name, slice(at, at + extent))
            at += extent
        self.total = at


def message_forward(b, cols, packed, points, tokens, neighbours, source, target, mixed, slope, slope_sum, node):
    width = points.shape[-1]
    length = points.shape[1]
    count = neighbours.shape[-1]
    rows = 32
    source[...] = trans_right(points[b], packed[:, cols.source]).astype(LOW)
    target[...] = trans_right(tokens[b], packed[:, cols.target])

    def step(at, carry):
        here = pl.ds(pl.multiple_of(at * rows, rows), rows)
        near = neighbours[b, here, :]
        lane = lax.broadcasted_iota(jnp.int32, (rows, length), 1)
        picks = [jnp.where(near[:, k : k + 1] == lane, 1.0, 0.0).astype(LOW) for k in range(count)]
        inside = product(jnp.concatenate(picks, axis=0), source[...])
        inside = inside.reshape(count, rows, width) + target[here, :][None]
        value, steep = gelu_pair(inside)
        mixed[b, here, :] = (jnp.sum(value, axis=0) * (1.0 / count)).astype(LOW)
        slope_sum[b, here, :] = jnp.sum(steep, axis=0)
        slope[b, :, here, :] = steep.astype(LOW)
        return carry

    lax.fori_loop(0, length // rows, step, 0)
    node[b] = tokens[b].astype(WIDE) + product(mixed[b], packed[:, cols.msg_out])


def message_back(
    b, cols, packed, points, tokens, neighbours_t, mixed, slope, slope_sum, d_node, grads, d_points, d_tokens, total
):
    length = points.shape[1]
    count = neighbours_t.shape[1]
    node_low = d_node.astype(LOW)
    grads[:, cols.msg_out] += trans_left(mixed[b], node_low)
    d_mixed = trans_right(node_low, packed[:, cols.msg_out]) * (1.0 / count)
    d_target = (d_mixed * slope_sum[b]).astype(LOW)
    mixed_low = d_mixed.astype(LOW)
    group = 4
    total[...] = jnp.zeros_like(total)
    for at in range(0, count, group):
        spot = lax.broadcasted_iota(jnp.int32, (length, length), 0)
        picks = [
            jnp.where(neighbours_t[b, k : k + 1, :] == spot, 1.0, 0.0).astype(LOW) for k in range(at, at + group)
        ]
        inside = [slope[b, k] * mixed_low for k in range(at, at + group)]
        total[...] += product(jnp.concatenate(picks, axis=1), jnp.concatenate(inside, axis=0))
    d_source = total[...].astype(LOW)
    grads[:, cols.source] += trans_left(d_source, points[b])
    grads[:, cols.target] += trans_left(d_target, tokens[b])
    d_points[b] = product(d_source, packed[:, cols.source])
    d_tokens[b] = d_node + product(d_target, packed[:, cols.target])


def perceiver(
    b,
    cols,
    packed,
    node,
    segments,
    modulation,
    base_unit,
    base_rows,
    gain_row,
    cotangent,
    latents,
    grads,
    d_node,
    d_gain,
    d_base_unit,
    d_base,
    d_mod,
    scr,
):
    length, width = node.shape[1:]
    per_sim = base_rows.shape[0]
    queries = 2 * per_sim
    pairs = HEADS // 2
    block = 2 * HEAD_DIM
    unit, node_scale = normalised(node[b])
    gain = gain_row[...]
    normed = (unit * gain).astype(LOW)
    keyval = product(normed, packed[:, cols.kv]).astype(LOW)
    keyval_t = scr["keyval_t"]
    keyval_t[...] = keyval.T
    second_count = jnp.sum(segments[b], axis=1, keepdims=True)
    first_count = length - second_count
    own_col = (lax.broadcasted_iota(jnp.int32, (length, 1), 0) < first_count).astype(WIDE)
    own_row = (lax.broadcasted_iota(jnp.int32, (1, length), 1) < first_count).astype(WIDE)
    low_col = (own_col.astype(LOW), (1.0 - own_col).astype(LOW))
    low_row = (own_row.astype(LOW), (1.0 - own_row).astype(LOW))
    lane = lax.broadcasted_iota(jnp.int32, (1, block), 1)
    half = ((lane < HEAD_DIM).astype(WIDE).astype(LOW), (lane >= HEAD_DIM).astype(WIDE).astype(LOW))
    scale_one, shift_one, scale_two, shift_two = (
        [modulation[b, s : s + 1, width * n : width * (n + 1)] for s in range(2)] for n in range(4)
    )

    first_in, query = scr["first_in"], scr["query"]
    for s in range(2):
        first_in[s * per_sim : (s + 1) * per_sim, :] = (
            (1.0 + scale_one[s]) * base_unit[...] + shift_one[s]
        ).astype(LOW)
    query[...] = (product(first_in[...], packed[:, cols.q]).astype(LOW) * 0.125).astype(LOW)

    def spread_heads(values):
        return [
            jnp.concatenate([values * low_col[0] * half[h], values * low_col[1] * half[h]], axis=1) for h in range(2)
        ]

    def by_sim(rows_in, pair):
        here = slice(pair * block, (pair + 1) * block)
        return jnp.concatenate([rows_in[:per_sim, here], rows_in[per_sim:, here]], axis=1)

    weights_t = scr["weights_t"]
    attended_t = scr["attended_t"]
    mask = own_col > 0.5
    for pair in range(pairs):
        keys = spread_heads(keyval[:, pair * block : (pair + 1) * block])
        query_pair = by_sim(query, pair)
        for h in range(2):
            head = 2 * pair + h
            raw = trans_right(keys[h], query_pair)
            top_first = jnp.max(jnp.where(mask, raw, -3e38), axis=0, keepdims=True)
            top_second = jnp.max(jnp.where(mask, -3e38, raw), axis=0, keepdims=True)
            grown = jnp.exp(raw - jnp.where(mask, top_first, top_second))
            sum_first = jnp.sum(jnp.where(mask, grown, 0.0), axis=0, keepdims=True)
            sum_second = jnp.sum(jnp.where(mask, 0.0, grown), axis=0, keepdims=True)
            share = (grown * jnp.where(mask, 1.0 / sum_first, 1.0 / sum_second)).astype(LOW)
            weights_t[head] = share
            value_t = keyval_t[width + head * HEAD_DIM : width + (head + 1) * HEAD_DIM, :]
            value_sims = jnp.concatenate([value_t * low_row[0], value_t * low_row[1]], axis=0)
            out_t = product(value_sims, share).astype(LOW)
            here = slice(head * HEAD_DIM, (head + 1) * HEAD_DIM)
            attended_t[here, :per_sim] = out_t[:HEAD_DIM]
            attended_t[here, per_sim:] = out_t[HEAD_DIM:]

    residual = trans_left(attended_t[...], packed[:, cols.o])
    residual = residual + jnp.concatenate([base_rows[...]] * 2, axis=0)
    res_unit, res_scale = normalised(residual)
    second = jnp.concatenate(
        [(1.0 + scale_two[s]) * res_unit[s * per_sim : (s + 1) * per_sim] + shift_two[s] for s in range(2)], axis=0
    ).astype(LOW)
    cot = cotangent[b]
    second_t, cot_t = scr["second_t"], scr["cot_t"]
    second_t[...] = second.T
    cot_t[...] = cot.T
    lat = None
    d_second = None
    hidden_width = cols.up.stop - cols.up.start
    chunk = 512
    for at in range(0, hidden_width, chunk):
        up = slice(cols.up.start + at, cols.up.start + at + chunk)
        down = slice(cols.down.start + at, cols.down.start + at + chunk)
        value, steep = gelu_pair(product(second, packed[:, up]))
        hidden = value.astype(LOW)
        d_up = (product(cot, packed[:, down]) * steep).astype(LOW)
        part = trans_right(hidden, packed[:, down])
        lat = part if lat is None else lat + part
        part = trans_right(d_up, packed[:, up])
        d_second = part if d_second is None else d_second + part
        grads[:, down] += product(cot_t[...], hidden)
        grads[:, up] += product(second_t[...], d_up)
    latents[b] = (residual + lat).astype(LOW)

    d_res = []
    mod_rows = [[], []]
    for s in range(2):
        rows_at = slice(s * per_sim, (s + 1) * per_sim)
        d_sim = d_second[rows_at]
        unit_sim = res_unit[rows_at]
        mod_rows[s] = [
            jnp.sum(d_sim * unit_sim, axis=0, keepdims=True),
            jnp.sum(d_sim, axis=0, keepdims=True),
        ]
        d_res.append(
            cot[rows_at].astype(WIDE)
            + normalised_back(d_sim * (1.0 + scale_two[s]), unit_sim, res_scale[rows_at])
        )
    d_base[...] += d_res[0] + d_res[1]
    res_low = jnp.concatenate(d_res, axis=0).astype(LOW)
    grads[:, cols.o] += product(attended_t[...], res_low)
    d_att = trans_right(packed[:, cols.o], res_low).astype(LOW)
    d_query_t = scr["query_t"]
    d_keyval = scr["d_keyval"]
    left_half = lane < HEAD_DIM
    for pair in range(pairs):
        values = spread_heads(keyval[:, width + pair * block : width + (pair + 1) * block])
        query_pair = by_sim(query, pair)
        here = slice(pair * block, (pair + 1) * block)
        d_att_pair = jnp.concatenate([d_att[here, :per_sim], d_att[here, per_sim:]], axis=0)
        d_keys, d_values = [], []
        for h in range(2):
            head = 2 * pair + h
            there = slice(head * HEAD_DIM, (head + 1) * HEAD_DIM)
            both = d_att[there, :].astype(WIDE) * attended_t[there, :].astype(WIDE)
            both = jnp.sum(both, axis=0, keepdims=True)
            share = weights_t[head]
            d_share = product(values[h], d_att_pair)
            d_raw = (
                share.astype(WIDE) * (d_share - jnp.where(mask, both[:, :per_sim], both[:, per_sim:]))
            ).astype(LOW)
            key_t = keyval_t[there, :]
            key_sims = jnp.concatenate([key_t * low_row[0], key_t * low_row[1]], axis=0)
            d_q = (product(key_sims, d_raw) * 0.125).astype(LOW)
            d_query_t[there, :per_sim] = d_q[:HEAD_DIM]
            d_query_t[there, per_sim:] = d_q[HEAD_DIM:]
            full = trans_right(share, d_att_pair)
            d_values.append(jnp.where(mask, full[:, :block], full[:, block:]))
            full = product(d_raw, query_pair)
            d_keys.append(jnp.where(mask, full[:, :block], full[:, block:]))
        d_keyval[:, here] = jnp.where(left_half, d_keys[0], d_keys[1]).astype(LOW)
        d_keyval[:, width + here.start : width + here.stop] = jnp.where(
            left_half, d_values[0], d_values[1]
        ).astype(LOW)

    d_query = d_query_t[...].T
    grads[:, cols.q] += trans_left(first_in[...], d_query)
    d_first = trans_right(d_query, packed[:, cols.q])
    for s in range(2):
        d_sim = d_first[s * per_sim : (s + 1) * per_sim]
        mod_rows[s] = [
            jnp.sum(d_sim * base_unit[...], axis=0, keepdims=True),
            jnp.sum(d_sim, axis=0, keepdims=True),
        ] + mod_rows[s]
        d_base_unit[...] += d_sim * (1.0 + scale_one[s])
        d_mod[b, s : s + 1, :] = jnp.concatenate(mod_rows[s], axis=1)

    d_kv = d_keyval[...]
    grads[:, cols.kv] += trans_left(normed, d_kv)
    d_normed = trans_right(d_kv, packed[:, cols.kv])
    d_gain[...] += jnp.sum(d_normed * unit, axis=0, keepdims=True)
    d_node[b] = normalised_back(d_normed * gain, unit, node_scale)


def perceiver_scratch(length, width, per_sim):
    queries = 2 * per_sim
    return {
        "keyval_t": pltpu.VMEM((2 * width, length), LOW),
        "first_in": pltpu.VMEM((queries, width), LOW),
        "query": pltpu.VMEM((queries, width), LOW),
        "weights_t": pltpu.VMEM((HEADS, length, per_sim), LOW),
        "attended_t": pltpu.VMEM((width, queries), LOW),
        "second_t": pltpu.VMEM((width, queries), LOW),
        "cot_t": pltpu.VMEM((width, queries), LOW),
        "query_t": pltpu.VMEM((width, queries), LOW),
        "d_keyval": pltpu.VMEM((length, 2 * width), LOW),
    }


def whole_call(body, outs, scratch, flops, **named):
    spec = pl.BlockSpec(memory_space=pltpu.VMEM)
    return pl.pallas_call(
        body,
        out_shape=outs,
        in_specs=[spec] * len(named["args"]),
        out_specs=[spec] * len(outs),
        scratch_shapes=scratch,
        compiler_params=pltpu.CompilerParams(vmem_limit_bytes=VMEM_BYTES),
        cost_estimate=pl.CostEstimate(flops=flops, bytes_accessed=1 << 23, transcendentals=0),
        name=named["name"],
    )(*named["args"])


def forward_call(cols, packed, points, tokens, neighbours):
    count, length, width = points.shape
    near = neighbours.shape[-1]

    def body(packed, points, tokens, neighbours, mixed, slope, slope_sum, node, source, target):
        def step(b, carry):
            message_forward(
                b, cols, packed, points, tokens, neighbours, source, target, mixed, slope, slope_sum, node
            )
            return carry

        lax.fori_loop(0, count, step, 0)

    shape = jax.ShapeDtypeStruct
    return whole_call(
        body,
        [
            shape((count, length, width), LOW),
            shape((count, near, length, width), LOW),
            shape((count, length, width), WIDE),
            shape((count, length, width), WIDE),
        ],
        [pltpu.VMEM((length, width), LOW), pltpu.VMEM((length, width), WIDE)],
        10**9,
        args=(packed, points, tokens, neighbours),
        name="message_forward",
    )


def perceiver_call(cols, packed, node, segments, condition, cotangent):
    count, length, width = node.shape
    per_sim = cols.base.stop - cols.base.start
    names = list(perceiver_scratch(length, width, per_sim))

    def body(packed, node, segments, condition, cotangent, latents, grads, d_node, *rest):
        modulation, base_unit, base_rows, base_scale, gain_row, d_gain, d_base_unit, d_base, d_mod = rest[:9]
        scr = dict(zip(names, rest[9:]))
        grads[...] = jnp.zeros_like(grads)
        base = packed[:, cols.base].astype(WIDE).T
        base_rows[...] = base
        unit, scale = normalised(base)
        base_unit[...] = unit
        base_scale[...] = scale
        gain_row[...] = packed[:, cols.gain].astype(WIDE).T[:1]
        for b in range(count):
            modulation[b] = product(condition[b], packed[:, cols.mod])
        d_gain[...] = jnp.zeros_like(d_gain)
        d_base_unit[...] = jnp.zeros_like(d_base_unit)
        d_base[...] = jnp.zeros_like(d_base)

        def step(b, carry):
            perceiver(
                b, cols, packed, node, segments, modulation, base_unit, base_rows, gain_row, cotangent,
                latents, grads, d_node, d_gain, d_base_unit, d_base, d_mod, scr,
            )
            return carry

        lax.fori_loop(0, count, step, 0)
        d_rows = normalised_back(d_base_unit[...], base_unit[...], base_scale[...]) + d_base[...]
        grads[:, cols.base] = d_rows.T
        grads[:, cols.gain] = jnp.broadcast_to(d_gain[...], (128, width)).T
        for b in range(count):
            grads[:, cols.mod] += trans_left(condition[b], d_mod[b].astype(LOW))

    shape = jax.ShapeDtypeStruct
    return whole_call(
        body,
        [
            shape((count, 2 * per_sim, width), LOW),
            shape((width, cols.total), WIDE),
            shape((count, length, width), WIDE),
        ],
        [
            pltpu.VMEM((count, 2, 4 * width), WIDE),
            pltpu.VMEM((per_sim, width), WIDE),
            pltpu.VMEM((per_sim, width), WIDE),
            pltpu.VMEM((per_sim, 1), WIDE),
            pltpu.VMEM((1, width), WIDE),
            pltpu.VMEM((1, width), WIDE),
            pltpu.VMEM((per_sim, width), WIDE),
            pltpu.VMEM((per_sim, width), WIDE),
            pltpu.VMEM((count, 2, 4 * width), WIDE),
        ]
        + list(perceiver_scratch(length, width, per_sim).values()),
        10**10,
        args=(packed, node, segments, condition, cotangent),
        name="perceiver",
    )


def backward_call(cols, packed, points, tokens, neighbours_t, mixed, slope, slope_sum, d_node):
    count, length, width = points.shape

    def body(packed, points, tokens, neighbours_t, mixed, slope, slope_sum, d_node, grads, d_points, d_tokens, total):
        grads[...] = jnp.zeros_like(grads)

        def step(b, carry):
            message_back(
                b, cols, packed, points, tokens, neighbours_t, mixed, slope, slope_sum, d_node[b], grads,
                d_points, d_tokens, total,
            )
            return carry

        lax.fori_loop(0, count, step, 0)

    shape = jax.ShapeDtypeStruct
    return whole_call(
        body,
        [
            shape((width, cols.msg_out.stop), WIDE),
            shape((count, length, width), WIDE),
            shape((count, length, width), WIDE),
        ],
        [pltpu.VMEM((length, width), WIDE)],
        10**9,
        args=(packed, points, tokens, neighbours_t, mixed, slope, slope_sum, d_node),
        name="message_back",
    )


def on_device(
    points,
    segments,
    neighbours,
    condition,
    msg_in,
    msg_out,
    norm_gain,
    mod_weight,
    query_base,
    q_weight,
    kv_weight,
    o_weight,
    up_weight,
    down_weight,
    cotangent,
):
    count, length, width = points.shape
    per = q_weight.shape[1]
    hidden = up_weight.shape[2]
    per_sim = query_base.shape[1]
    cols = Columns(width, hidden, per_sim)
    turned = msg_in[0].T
    own = jnp.concatenate(
        [
            turned[:, :width],
            turned[:, width:],
            msg_out[0],
            jnp.broadcast_to(norm_gain[0][:, None], (per, 128)),
            kv_weight[0],
            q_weight[0],
            o_weight[0],
            query_base[0].T,
            mod_weight[0],
            up_weight[0],
            down_weight[0].T,
        ],
        axis=1,
    )
    packed = lax.all_gather(own, "dp", axis=0, tiled=True)
    first_section = lax.axis_index("section") == 0
    section_size = lax.axis_size("section")
    forth = [(i, i + 1) for i in range(section_size - 1)]
    back = [(i + 1, i) for i in range(section_size - 1)]
    neighbours_t = jnp.transpose(neighbours, (0, 2, 1))
    seg_rows = segments.reshape(count, 1, length)
    _, _, _, node = forward_call(cols, packed, points, points, neighbours)
    arrived = lax.ppermute(node.astype(LOW), "section", forth)
    tokens = jnp.where(first_section, points, arrived)
    mixed, slope, slope_sum, node = forward_call(cols, packed, points, tokens, neighbours)
    latents, grads, d_node = perceiver_call(cols, packed, node, seg_rows, condition, cotangent[0])
    _, _, d_tokens = backward_call(
        cols, packed, points, tokens, neighbours_t, mixed, slope, slope_sum, d_node
    )
    returned = lax.ppermute(d_tokens.astype(LOW), "section", back)
    d_node = d_node + jnp.where(first_section, returned.astype(WIDE), 0.0)
    grads_msg, d_points, d_tokens = backward_call(
        cols, packed, points, tokens, neighbours_t, mixed, slope, slope_sum, d_node
    )
    d_points = d_points + jnp.where(first_section, d_tokens, 0.0)
    point_sum = lax.psum(d_points.astype(LOW), "section").astype(WIDE)
    grads = jnp.concatenate([grads_msg, grads[:, cols.msg_out.stop :]], axis=1)
    share = lax.psum_scatter(grads, "dp", scatter_dimension=0, tiled=True)
    share = lax.psum(share.astype(LOW), "rep").astype(WIDE)
    return (
        latents[None],
        point_sum,
        share[:, : 2 * width].T[None],
        share[None, :, cols.msg_out],
        share[None, :, cols.gain.start],
        share[None, :, cols.mod],
        share[:, cols.base].T[None],
        share[None, :, cols.q],
        share[None, :, cols.kv],
        share[None, :, cols.o],
        share[None, :, cols.up],
        share[:, cols.down].T[None],
    )


def solution(mesh):
    placed = (
        P(("dp", "rep"), None, None),
        P(("dp", "rep"), None),
        P(("dp", "rep"), None, None),
        P(("dp", "rep"), None, None),
        P("section", None, "dp"),
        P("section", "dp", None),
        P("section", "dp"),
        P("section", "dp", None),
        P("section", None, "dp"),
        P("section", "dp", None),
        P("section", "dp", None),
        P("section", "dp", None),
        P("section", "dp", None),
        P("section", None, "dp"),
        P("section", ("dp", "rep"), None, None),
    )
    return jax.shard_map(
        on_device,
        mesh=mesh,
        in_specs=placed,
        out_specs=(
            P("section", ("dp", "rep"), None, None),
            P(("dp", "rep"), None, None),
            P("section", None, "dp"),
            P("section", "dp", None),
            P("section", "dp"),
            P("section", "dp", None),
            P("section", None, "dp"),
            P("section", "dp", None),
            P("section", "dp", None),
            P("section", "dp", None),
            P("section", "dp", None),
            P("section", None, "dp"),
        ),
        check_vma=False,
    )
```

time: 1710 us -> 454 us (0.27)
  blocking collectives: 718 us -> 0 us
  matrix products: 297 us -> 0 us
  other arithmetic: 311 us -> 21 us
  local copies, waits for them, and re-layouts: 280 us -> 23.4 us
  waiting for transfers between devices: 57.4 us -> 263 us
  Pallas kernels: 0 us -> 128 us
    unnamed x2 -> x0, blocking collectives: 624 us -> none
    dot_general x156 -> x0, matrix products: 263 us -> none  [the longest x64 70.8 us: product(): return jnp.dot(left_op, right_op, preferred_element_type=jnp.float32)]
    gather x8 -> x0, local copies, waits for them, and re-layouts: 131 us -> none  [section_pass(): inside = at_source[neighbour] + at_target[:, None, :]]
    pallas_call x0 -> x5, Pallas kernels: none -> 128 us  [whole_call(): pl.pallas_call(body, out_shape=outs, in_specs=[spec] * len(named['args'])...]
    reduce_scatter x6 -> x1, waiting for transfers between devices: 0.01 us -> 119 us  [on_device(): share = lax.psum_scatter(grads, 'dp', scatter_dimension=0, tiled=True)]
    scatter-add x4 -> x0, other arithmetic: 109 us -> none  [section_back(): d_source = jnp.zeros((length, width), jnp.float32).at[neighbour.reshape(-...]
    reduce_sum x35 -> x0, other arithmetic: 103 us -> none  [the longest x8 50 us: edge_mean(): return jnp.mean(jax.nn.gelu(inside), axis=1)]
    all_gather x6 -> x0, blocking collectives: 93.8 us -> none  [the longest x1 16.7 us: on_device(): lax.all_gather(msg_in, 'dp', axis=2, tiled=True)]
  transfers between devices with their start and end apart: 19 -> 6, of which waited for: 6 -> 6; matrix products, arithmetic and copies ran while one was open for 40% -> 3% of each run, Pallas kernels for 0% -> 0%
where the time goes in v1:
time: 454 us; the launch traced here: 452 us
  waiting for transfers between devices  263 us (58%)
  Pallas kernels  128 us (28%)
  local copies, waits for them, and re-layouts  23.4 us (5%)
  other arithmetic  21 us (5%)
  between operations  13.9 us (3%)
    pallas_call x5, Pallas kernels, whole_call(): pl.pallas_call(body, out_shape=outs, in_specs=[spec] * len(named['args'])...  128 us
    reduce_scatter x1, waiting for transfers between devices, on_device(): share = lax.psum_scatter(grads, 'dp', scatter_dimension=0, tiled=True)  119 us
    all_gather x1, waiting for transfers between devices, on_device(): packed = lax.all_gather(own, 'dp', axis=0, tiled=True)  61.9 us
    psum x1, waiting for transfers between devices, on_device(): share = lax.psum(share.astype(LOW), 'rep').astype(WIDE)  34.5 us
    psum x1, waiting for transfers between devices, on_device(): point_sum = lax.psum(d_points.astype(LOW), 'section').astype(WIDE)  27.8 us
    ppermute x1, waiting for transfers between devices, on_device(): arrived = lax.ppermute(node.astype(LOW), 'section', forth)  15.5 us
    unnamed x26, local copies, waits for them, and re-layouts  10.8 us
    concatenate x1, other arithmetic, on_device(): grads = jnp.concatenate([grads_msg, grads[:, cols.msg_out.stop:]], axis=1)  9.58 us
  transfers between devices with their start and end apart: 6, of which 6 were waited for; matrix products, arithmetic and copies ran while one was open for 3% of the time, Pallas kernels for 0%

profile of v1, /device:TPU:2, one launch (start us, length us, event | category | flops | bytes accessed | tf_op | source)
XLA Modules:
  0.0 451.6 jit_solution(18367712882469976740)
XLA Ops:
  7.2 0.0 all-gather.2.cloned.1.call-start
  7.2 0.9 bitcast_dynamic-update-slice_fusion.3
  8.2 0.8 bitcast_dynamic-update-slice_fusion.7
  8.9 0.7 constant_dynamic-update-slice_fusion
  9.7 0.9 bitcast_dynamic-update-slice_fusion.4
  10.6 0.8 bitcast_dynamic-update-slice_fusion.6
  11.3 0.8 bitcast_dynamic-update-slice_fusion.5
  12.1 0.7 bitcast_dynamic-update-slice_fusion.8
  12.9 0.9 bitcast_dynamic-update-slice_fusion.2
  13.8 0.9 bitcast_dynamic-update-slice_fusion.1
  14.8 0.9 copy-done.4
  15.6 0.0 reduce-scatter.2.cloned.1.call-start
  15.7 0.9 copy.29.neighbours
  16.6 61.9 %all-gather.2.cloned.1.call-done.packed = bf16[384,7680]{1,0:T(8,128)(2,1)} async-done(((bf16[48,7680]{1,0:T(8,128)(2,1)}), bf16[384,7680]{1,0:T(8,128)(2,1)}) %all-gather.2.cloned.1.call-update) | async-done | bytes 5898256 | tf_op jit(solution)/shard_map/all_gather | solution.py:494
  78.5 25.7 %message_forward.2 = (bf16[3,256,384]{2,1,0:T(8,128)(2,1)}, bf16[3,16,256,384]{3,2,1,0:T(8,128)(2,1)}, f32[3,256,384]{2,1,0:T(8,128)}, f32[3,256,384]{2,1,0:T(8,128)}) custom-call(bf16[384,7680]{1,0:T(8,128)(2,1)} %all-gather.2.cloned.1.call-done.packed, bf16[3,256,384]{2,1,0:T(8,128)(2,1)} %points.7, bf16[3,256,384]{2,1,0:T(8,128)(2,1)} %points.7, ...), custom_call_target="tpu_custom_call" | custom-call | flops 1000000000 | bytes 8388608 | tf_op jit(solution)/shard_map/message_forward/pallas_call | solution.py:323
  104.2 1.4 convert_element_type.21
  105.6 1.3 collective-permute-start
  106.9 0.6 reshape.28.segments
  107.5 15.5 %collective-permute-done = bf16[3,256,384]{2,1,0:T(8,128)(2,1)S(1)} collective-permute-done((bf16[3,256,384]{2,1,0:T(8,128)(2,1)S(1)}, bf16[3,256,384]{2,1,0:T(8,128)(2,1)S(1)}, u32[]{:S(2)}, u32[]{:S(2)}) %collective-permute-start) | collective-permute-done | bytes 589856 | tf_op jit(solution)/shard_map/ppermute | solution.py:502
  123.0 0.9 broadcast_select_fusion.tokens
  123.9 25.7 %message_forward.3 = (bf16[3,256,384]{2,1,0:T(8,128)(2,1)}, bf16[3,16,256,384]{3,2,1,0:T(8,128)(2,1)}, f32[3,256,384]{2,1,0:T(8,128)}, f32[3,256,384]{2,1,0:T(8,128)}) custom-call(bf16[384,7680]{1,0:T(8,128)(2,1)} %all-gather.2.cloned.1.call-done.packed, bf16[3,256,384]{2,1,0:T(8,128)(2,1)} %points.7, bf16[3,256,384]{2,1,0:T(8,128)(2,1)} %broadcast_select_fusion.tokens, ...), custom_call_target="tpu_custom_call" | custom-call | flops 1000000000 | bytes 8388608 | tf_op jit(solution)/shard_map/message_forward/pallas_call | solution.py:323
  149.6 45.6 %perceiver.1 = (bf16[3,512,384]{2,1,0:T(8,128)(2,1)}, f32[384,7680]{1,0:T(8,128)}, f32[3,256,384]{2,1,0:T(8,128)}) custom-call(bf16[384,7680]{1,0:T(8,128)(2,1)} %all-gather.2.cloned.1.call-done.packed, f32[3,256,384]{2,1,0:T(8,128)} %get-tuple-element.25.node, s32[3,1,256]{2,1,0:T(1,128)} %reshape.28.segments, bf16[3,2,384]{2,1,0:T(2,128)(2,1)} %condition.1, ...), custom_call_target="tpu_custom_call" | custom-call | flops 10000000000 | bytes 8388608 | tf_op jit(solution)/shard_map/perceiver/pallas_call | solution.py:323
  195.1 15.5 %message_back.2 = (f32[384,1152]{1,0:T(8,128)}, f32[3,256,384]{2,1,0:T(8,128)}, f32[3,256,384]{2,1,0:T(8,128)}) custom-call(bf16[384,7680]{1,0:T(8,128)(2,1)} %all-gather.2.cloned.1.call-done.packed, bf16[3,256,384]{2,1,0:T(8,128)(2,1)} %points.7, bf16[3,256,384]{2,1,0:T(8,128)(2,1)} %broadcast_select_fusion.tokens, s32[3,16,256]{2,1,0:T(8,128)} %bitcast.53, ...), custom_call_target="tpu_custom_call" | custom-call | flops 1000000000 | bytes 8388608 | tf_op jit(solution)/shard_map/message_back/pallas_call | solution.py:323
  210.6 1.3 convert_element_type.22
  211.9 1.5 collective-permute-start.1
  213.4 8.4 %slice.36 = f32[384,6528]{1,0:T(8,128)} slice(f32[384,7680]{1,0:T(8,128)} %get-tuple-element.35), slice={[0:384], [1152:7680]} | slice | bytes 20054016 | tf_op jit(solution)/shard_map/slice | solution.py:516
  221.8 3.8 collective-permute-done.1
  225.7 1.1 select_add_fusion.d_node
  226.8 15.3 %message_back.3 = (f32[384,1152]{1,0:T(8,128)}, f32[3,256,384]{2,1,0:T(8,128)}, f32[3,256,384]{2,1,0:T(8,128)}) custom-call(bf16[384,7680]{1,0:T(8,128)(2,1)} %all-gather.2.cloned.1.call-done.packed, bf16[3,256,384]{2,1,0:T(8,128)(2,1)} %points.7, bf16[3,256,384]{2,1,0:T(8,128)(2,1)} %broadcast_select_fusion.tokens, s32[3,16,256]{2,1,0:T(8,128)} %bitcast.54, ...), custom_call_target="tpu_custom_call" | custom-call | flops 1000000000 | bytes 8388608 | tf_op jit(solution)/shard_map/message_back/pallas_call | solution.py:323
  242.1 9.6 %pad_maximum_fusion = f32[384,7680]{1,0:T(8,128)} fusion(f32[384,6528]{1,0:T(8,128)} %slice.36, f32[384,1152]{1,0:T(8,128)} %get-tuple-element.34), kind=kLoop, calls=%fused_computation | loop fusion | flops 2949120 | bytes 23592960 | tf_op jit(solution)/shard_map/concatenate | solution.py:516
  251.7 0.0 reduce-scatter.2.cloned.1.call-update
  251.7 0.0 all-reduce.3.cloned.1.call-start
  251.8 1.2 copy-done.2
  253.0 0.4 copy-done.3
  253.3 0.9 add_convert_fusion
  254.3 0.0 all-reduce.3.cloned.1.call-update
  254.3 0.0 all-reduce.5.cloned.1.call-start
  254.3 119.0 %reduce-scatter.2.cloned.1.call-done = f32[48,7680]{1,0:T(8,128)} async-done(((f32[384,7680]{1,0:T(8,128)}), f32[48,7680]{1,0:T(8,128)}) %reduce-scatter.2.cloned.1.call-update) | async-done | bytes 1474576 | tf_op jit(solution)/shard_map/reduce_scatter | solution.py:517
  373.4 2.3 convert_element_type.26
  375.7 27.8 %all-reduce.3.cloned.1.call-done = bf16[3,256,384]{2,1,0:T(8,128)(2,1)} async-done(((bf16[3,256,384]{2,1,0:T(8,128)(2,1)}), bf16[3,256,384]{2,1,0:T(8,128)(2,1)}) %all-reduce.3.cloned.1.call-update) | async-done | bytes 589840 | tf_op jit(solution)/shard_map/psum | solution.py:515
  403.5 2.2 convert_element_type.25
  405.7 34.5 %all-reduce.5.cloned.1.call-done = bf16[48,7680]{1,0:T(8,128)(2,1)} async-done(((bf16[48,7680]{1,0:T(8,128)(2,1)}), bf16[48,7680]{1,0:T(8,128)(2,1)}) %all-reduce.5.cloned.1.call-update) | async-done | bytes 737296 | tf_op jit(solution)/shard_map/psum | solution.py:518
  440.2 1.2 convert_element_type.27
  441.4 0.6 slice_reduce_fusion
  442.1 0.6 slice_bitcast_fusion.8
  442.7 0.7 slice_bitcast_fusion.5
  443.4 0.7 slice_bitcast_fusion.3
  444.1 0.9 slice_bitcast_fusion
  (16 shorter events, 0.1 us)
Async XLA Ops:
  7.2 7.5 %copy-start.6 = (bf16[1,1536,48]{1,2,0:T(8,128)(2,1)S(1)}, bf16[1,1536,48]{1,2,0:T(8,128)(2,1)}, u32[]{:S(2)}) copy-start(bf16[1,1536,48]{1,2,0:T(8,128)(2,1)} %param.28) | copy-start | bytes 442372
  7.2 8.5 %copy-start.5 = (s32[3,256,16]{1,2,0:T(8,128)S(1)}, s32[3,256,16]{1,2,0:T(8,128)}, u32[]{:S(2)}) copy-start(s32[3,256,16]{1,2,0:T(8,128)} %param.17) | copy-start | bytes 147460
  7.2 71.3 %all-gather.2.cloned.1.call-start = ((), (), s32[]{:S(2)}) async-start(), calls=%async_computation.1 | async-start | bytes 6635520 | tf_op jit(solution)/shard_map/all_gather | solution.py:494
  14.7 0.9 copy-start.4
  15.6 357.7 %reduce-scatter.2.cloned.1.call-start = ((), (), s32[]{:S(2)}) async-start(), calls=%async_computation.3 | async-start | bytes 13271040 | tf_op jit(solution)/shard_map/reduce_scatter | solution.py:517
  104.2 2.7 copy-start.7
  104.2 18.8 %copy-start = (bf16[3,256,384]{2,1,0:T(8,128)(2,1)S(1)}, bf16[3,256,384]{2,1,0:T(8,128)(2,1)}, u32[]{:S(2)}) copy-start(bf16[3,256,384]{2,1,0:T(8,128)(2,1)} %points.7) | copy-start | bytes 1769476
  105.6 17.4 %collective-permute-start = (bf16[3,256,384]{2,1,0:T(8,128)(2,1)S(1)}, bf16[3,256,384]{2,1,0:T(8,128)(2,1)S(1)}, u32[]{:S(2)}, u32[]{:S(2)}) collective-permute-start(bf16[3,256,384]{2,1,0:T(8,128)(2,1)S(1)} %convert_element_type.21), channel_id=1, source_target_pairs={{0,16},{1,17},{2,18},{3,19},{4,20},{5,21},{6,22},{7,23},{8,24},{9,... | collective-permute-start | bytes 1769480 | tf_op jit(solution)/shard_map/ppermute | solution.py:502
  211.9 13.7 %collective-permute-start.1 = (bf16[3,256,384]{2,1,0:T(8,128)(2,1)S(1)}, bf16[3,256,384]{2,1,0:T(8,128)(2,1)S(1)}, u32[]{:S(2)}, u32[]{:S(2)}) collective-permute-start(bf16[3,256,384]{2,1,0:T(8,128)(2,1)S(1)} %convert_element_type.22), channel_id=1, source_target_pairs={{16,0},{17,1},{18,2},{19,3},{20,4},{21,5},{22,6},{23,7},{24,8},{25... | collective-permute-start | bytes 1769480 | tf_op jit(solution)/shard_map/ppermute | solution.py:509
  213.4 12.2 %copy-start.1 = (f32[3,256,384]{2,1,0:T(8,128)S(1)}, f32[3,256,384]{2,1,0:T(8,128)}, u32[]{:S(2)}) copy-start(f32[3,256,384]{2,1,0:T(8,128)} %get-tuple-element.30.d_node) | copy-start | bytes 3538948
  251.7 1.3 copy-start.2
  251.7 1.6 copy-start.3
  251.7 151.8 %all-reduce.3.cloned.1.call-start = ((), (), s32[]{:S(2)}) async-start(), calls=%async_computation.2 | async-start | bytes 1179648 | tf_op jit(solution)/shard_map/psum | solution.py:515
  254.3 185.9 %all-reduce.5.cloned.1.call-start = ((), (), s32[]{:S(2)}) async-start(), calls=%async_computation.4 | async-start | bytes 1474560 | tf_op jit(solution)/shard_map/psum | solution.py:518
Sparse Core Ops, SparseCore 0:
  15.8 62.7 all-gather.1
  251.9 121.4 reduce-scatter.1
  376.2 27.2 all-reduce.2
  405.8 34.3 all-reduce.4

commit v2 on v1

v2 whole, which is shorter than its diff:
```python
import types

import jax
import jax.numpy as jnp
from jax import lax
from jax.experimental import pallas as pl
from jax.experimental.pallas import tpu as pltpu
from jax.sharding import PartitionSpec as P

HEADS = 6
HEAD_DIM = 64
EPSILON = 1e-05
TANH_ONE = 0.7978845608028654
TANH_THREE = 0.7978845608028654 * 0.044715
CUBE = TANH_THREE ** (1.0 / 3.0)
SECTION, DP, REP = "section", "dp", "rep"
LOW = jnp.bfloat16
WIDE = jnp.float32
VMEM_BYTES = 63 * 1024 * 1024


def product(left_op, right_op):
    return jnp.dot(left_op, right_op, preferred_element_type=WIDE)


def trans_left(left_op, right_op):
    return lax.dot_general(left_op, right_op, (((0,), (0,)), ((), ())), preferred_element_type=WIDE)


def trans_right(left_op, right_op):
    return lax.dot_general(left_op, right_op, (((1,), (1,)), ((), ())), preferred_element_type=WIDE)


def gelu_pair(inside):
    square = inside * inside
    half = 0.5 + 0.5 * jnp.tanh(inside * (TANH_ONE + TANH_THREE * square))
    value = inside * half
    slope = half + value * (1.0 - half) * (2.0 * TANH_ONE + 6.0 * TANH_THREE * square)
    return value, slope


def gelu_cubed(inside):
    kind = inside.dtype
    square = inside * inside
    bend = jnp.tanh(inside * (square + jnp.asarray(TANH_ONE / CUBE, kind)))
    upper = bend + jnp.asarray(1.0, kind)
    value = inside * upper
    steep = value * (jnp.asarray(1.0, kind) - bend) * (square + jnp.asarray(TANH_ONE / (3.0 * CUBE), kind))
    return value, upper * jnp.asarray(1.0 / 3.0, kind) + steep


def normalised(values):
    centre = values - jnp.mean(values, axis=-1, keepdims=True)
    spread = jnp.mean(centre * centre, axis=-1, keepdims=True)
    scale = lax.rsqrt(spread + EPSILON)
    return centre * scale, scale


def normalised_back(d_out, unit, scale):
    first = jnp.mean(d_out, axis=-1, keepdims=True)
    second = jnp.mean(d_out * unit, axis=-1, keepdims=True)
    return scale * (d_out - first - unit * second)


class Columns:
    def __init__(self, width, hidden, per_sim):
        self.pieces = (
            ("source", width),
            ("gain", 128),
            ("target", width),
            ("msg_out", width),
            ("kv", 2 * width),
            ("q", width),
            ("o", width),
            ("base", per_sim),
            ("up", hidden),
            ("down", hidden),
            ("mod", 4 * width),
        )
        at = 0
        for name, extent in self.pieces:
            setattr(self, name, slice(at, at + extent))
            at += extent
        self.total = at


def evolution_masks(b, segments, length):
    second_count = jnp.sum(segments[pl.ds(b, 1), :], axis=1, keepdims=True)
    first_count = length - second_count
    own_col = (lax.broadcasted_iota(jnp.int32, (length, 1), 0) < first_count).astype(WIDE)
    own_row = (lax.broadcasted_iota(jnp.int32, (1, length), 1) < first_count).astype(WIDE)
    return own_col, own_row


def spread_heads(values, own_col):
    lane = lax.broadcasted_iota(jnp.int32, (1, values.shape[1]), 1)
    sims = (own_col.astype(LOW), (1.0 - own_col).astype(LOW))
    halves = ((lane < HEAD_DIM).astype(WIDE).astype(LOW), (lane >= HEAD_DIM).astype(WIDE).astype(LOW))
    return [jnp.concatenate([values * sims[0] * half, values * sims[1] * half], axis=1) for half in halves]


def by_sim(rows_in, pair):
    block = 2 * HEAD_DIM
    per_sim = rows_in.shape[0] // 2
    here = slice(pair * block, (pair + 1) * block)
    return jnp.concatenate([rows_in[:per_sim, here], rows_in[per_sim:, here]], axis=1)


def mod_rows(b, scr, width):
    return (
        [scr.modulation[pl.ds(2 * b + s, 1), width * n : width * (n + 1)] for s in range(2)] for n in range(4)
    )


def first_rows(b, scr, width):
    scale_one, shift_one, _, _ = mod_rows(b, scr, width)
    rows = [(1.0 + scale_one[s]) * scr.base_unit[...] + shift_one[s] for s in range(2)]
    return jnp.concatenate(rows, axis=0).astype(LOW)


def attend(b, cols, packed, segments, scr):
    length, width = scr.node.shape[1:]
    per_sim = scr.base_rows.shape[0]
    block = 2 * HEAD_DIM
    unit, _ = normalised(scr.node[b])
    normed = (unit * scr.gain_row[...]).astype(LOW)
    keyval = product(normed, packed[:, cols.kv]).astype(LOW)
    scr.keyval[b] = keyval
    scr.keyval_t[b] = keyval.T
    own_col, own_row = evolution_masks(b, segments, length)
    low_row = (own_row.astype(LOW), (1.0 - own_row).astype(LOW))
    query = (product(first_rows(b, scr, width), packed[:, cols.q]).astype(LOW) * 0.125).astype(LOW)
    scr.query[b] = query
    mask = own_col > 0.5
    for pair in range(HEADS // 2):
        keys = spread_heads(keyval[:, pair * block : (pair + 1) * block], own_col)
        query_pair = by_sim(query, pair)
        for h in range(2):
            head = 2 * pair + h
            raw = trans_right(keys[h], query_pair)
            top_first = jnp.max(jnp.where(mask, raw, -3e38), axis=0, keepdims=True)
            top_second = jnp.max(jnp.where(mask, -3e38, raw), axis=0, keepdims=True)
            grown = jnp.exp(raw - jnp.where(mask, top_first, top_second))
            sum_first = jnp.sum(jnp.where(mask, grown, 0.0), axis=0, keepdims=True)
            sum_second = jnp.sum(jnp.where(mask, 0.0, grown), axis=0, keepdims=True)
            share = (grown * jnp.where(mask, 1.0 / sum_first, 1.0 / sum_second)).astype(LOW)
            scr.weights_t[b, head] = share
            here = slice(head * HEAD_DIM, (head + 1) * HEAD_DIM)
            value_t = scr.keyval_t[b, width + here.start : width + here.stop, :]
            value_sims = jnp.concatenate([value_t * low_row[0], value_t * low_row[1]], axis=0)
            out_t = product(value_sims, share).astype(LOW)
            scr.attended_t[b, here, :per_sim] = out_t[:HEAD_DIM]
            scr.attended_t[b, here, per_sim:] = out_t[HEAD_DIM:]


def feed_forward(b, cols, packed, cotangent, latents, grads, scr):
    width = scr.node.shape[-1]
    per_sim = scr.base_rows.shape[0]
    _, _, scale_two, shift_two = mod_rows(b, scr, width)
    attended_t = scr.attended_t[b]
    residual = trans_left(attended_t, packed[:, cols.o])
    residual = residual + jnp.concatenate([scr.base_rows[...]] * 2, axis=0)
    res_unit, res_scale = normalised(residual)
    second = jnp.concatenate(
        [(1.0 + scale_two[s]) * res_unit[s * per_sim : (s + 1) * per_sim] + shift_two[s] for s in range(2)], axis=0
    ).astype(LOW)
    cot = cotangent[b]
    scr.second_t[...] = second.T
    scr.cot_t[...] = cot.T
    lat = None
    d_second = None
    chunk = 512
    for at in range(0, cols.up.stop - cols.up.start, chunk):
        up = slice(cols.up.start + at, cols.up.start + at + chunk)
        down = slice(cols.down.start + at, cols.down.start + at + chunk)
        value, steep = gelu_cubed((product(second, packed[:, up]) * CUBE).astype(LOW))
        hidden = value * jnp.asarray(0.5 / CUBE, LOW)
        d_up = (product(cot, packed[:, down]) * 1.5).astype(LOW) * steep
        part = trans_right(hidden, packed[:, down])
        lat = part if lat is None else lat + part
        part = trans_right(d_up, packed[:, up])
        d_second = part if d_second is None else d_second + part
        grads[:, down] += product(scr.cot_t[...], hidden)
        grads[:, up] += product(scr.second_t[...], d_up)
    out_copy = pltpu.make_async_copy(scr.lat_buf, latents.at[b], scr.lat_sem)

    @pl.when(b > 0)
    def _():
        out_copy.wait()

    scr.lat_buf[...] = (residual + lat).astype(LOW)
    out_copy.start()
    d_res = []
    for s in range(2):
        rows_at = slice(s * per_sim, (s + 1) * per_sim)
        d_sim = d_second[rows_at]
        unit_sim = res_unit[rows_at]
        scr.d_mod[pl.ds(2 * b + s, 1), 2 * width : 3 * width] = jnp.sum(d_sim * unit_sim, axis=0, keepdims=True)
        scr.d_mod[pl.ds(2 * b + s, 1), 3 * width :] = jnp.sum(d_sim, axis=0, keepdims=True)
        d_res.append(
            cot[rows_at].astype(WIDE)
            + normalised_back(d_sim * (1.0 + scale_two[s]), unit_sim, res_scale[rows_at])
        )
    scr.d_base[...] += d_res[0] + d_res[1]
    res_low = jnp.concatenate(d_res, axis=0).astype(LOW)
    grads[:, cols.o] += product(attended_t, res_low)
    d_att = trans_right(packed[:, cols.o], res_low).astype(LOW)
    both = d_att.astype(WIDE) * attended_t.astype(WIDE)
    for head in range(HEADS):
        scr.overlap[b, head : head + 1, :] = jnp.sum(
            both[head * HEAD_DIM : (head + 1) * HEAD_DIM], axis=0, keepdims=True
        )
    scr.attended_t[b] = d_att


def attend_back(b, cols, packed, segments, grads, scr):
    length, width = scr.node.shape[1:]
    per_sim = scr.base_rows.shape[0]
    block = 2 * HEAD_DIM
    own_col, own_row = evolution_masks(b, segments, length)
    low_row = (own_row.astype(LOW), (1.0 - own_row).astype(LOW))
    mask = own_col > 0.5
    left_half = lax.broadcasted_iota(jnp.int32, (1, block), 1) < HEAD_DIM
    keyval = scr.keyval[b]
    query = scr.query[b]
    d_att = scr.attended_t[b]
    for pair in range(HEADS // 2):
        values = spread_heads(keyval[:, width + pair * block : width + (pair + 1) * block], own_col)
        query_pair = by_sim(query, pair)
        here = slice(pair * block, (pair + 1) * block)
        d_att_pair = jnp.concatenate([d_att[here, :per_sim], d_att[here, per_sim:]], axis=0)
        d_keys, d_values = [], []
        for h in range(2):
            head = 2 * pair + h
            there = slice(head * HEAD_DIM, (head + 1) * HEAD_DIM)
            both = scr.overlap[b, head : head + 1, :]
            share = scr.weights_t[b, head]
            d_share = product(values[h], d_att_pair)
            d_raw = (
                share.astype(WIDE) * (d_share - jnp.where(mask, both[:, :per_sim], both[:, per_sim:]))
            ).astype(LOW)
            key_t = scr.keyval_t[b, there, :]
            key_sims = jnp.concatenate([key_t * low_row[0], key_t * low_row[1]], axis=0)
            d_q = (product(key_sims, d_raw) * 0.125).astype(LOW)
            scr.query_t[there, :per_sim] = d_q[:HEAD_DIM]
            scr.query_t[there, per_sim:] = d_q[HEAD_DIM:]
            full = trans_right(share, d_att_pair)
            d_values.append(jnp.where(mask, full[:, :block], full[:, block:]))
            full = product(d_raw, query_pair)
            d_keys.append(jnp.where(mask, full[:, :block], full[:, block:]))
        scr.d_keyval[:, here] = jnp.where(left_half, d_keys[0], d_keys[1]).astype(LOW)
        scr.d_keyval[:, width + here.start : width + here.stop] = jnp.where(
            left_half, d_values[0], d_values[1]
        ).astype(LOW)

    scale_one, shift_one, _, _ = mod_rows(b, scr, width)
    d_query = scr.query_t[...].T
    grads[:, cols.q] += trans_left(first_rows(b, scr, width), d_query)
    d_first = trans_right(d_query, packed[:, cols.q])
    for s in range(2):
        d_sim = d_first[s * per_sim : (s + 1) * per_sim]
        scr.d_mod[pl.ds(2 * b + s, 1), :width] = jnp.sum(d_sim * scr.base_unit[...], axis=0, keepdims=True)
        scr.d_mod[pl.ds(2 * b + s, 1), width : 2 * width] = jnp.sum(d_sim, axis=0, keepdims=True)
        scr.d_base_unit[...] += d_sim * (1.0 + scale_one[s])

    unit, node_scale = normalised(scr.node[b])
    gain = scr.gain_row[...]
    d_kv = scr.d_keyval[...]
    grads[:, cols.kv] += trans_left((unit * gain).astype(LOW), d_kv)
    d_normed = trans_right(d_kv, packed[:, cols.kv])
    scr.d_gain[...] += jnp.sum(d_normed * unit, axis=0, keepdims=True)
    scr.node[b] = normalised_back(d_normed * gain, unit, node_scale)


def perceiver_scratch(count, length, width, per_sim):
    queries = 2 * per_sim
    return dict(
        keyval=pltpu.VMEM((count, length, 2 * width), LOW),
        keyval_t=pltpu.VMEM((count, 2 * width, length), LOW),
        query=pltpu.VMEM((count, queries, width), LOW),
        weights_t=pltpu.VMEM((count, HEADS, length, per_sim), LOW),
        attended_t=pltpu.VMEM((count, width, queries), LOW),
        overlap=pltpu.VMEM((count, 8, queries), WIDE),
        second_t=pltpu.VMEM((width, queries), LOW),
        cot_t=pltpu.VMEM((width, queries), LOW),
        query_t=pltpu.VMEM((width, queries), LOW),
        d_keyval=pltpu.VMEM((length, 2 * width), LOW),
    )


def one_hot(near_t, edges, columns, length):
    picks = []
    for k in edges:
        row = near_t[k : k + 1, columns].astype(jnp.int16)
        spot = lax.broadcasted_iota(jnp.int16, (length, row.shape[1]), 0)
        picks.append(jnp.where(row == spot, jnp.asarray(1.0, LOW), jnp.asarray(0.0, LOW)))
    return jnp.concatenate(picks, axis=1)


def message_half(b, half, cols, packed, points, tokens, neighbours, scr):
    length, width = points.shape[1:]
    count = neighbours.shape[1]
    part = length // 2
    here = slice(half * part, (half + 1) * part)
    if half == 0:
        scr.source_t[...] = (trans_right(packed[:, cols.source], points[b]) * CUBE).astype(LOW)
    target = (trans_right(packed[:, cols.target], tokens[b, here, :]) * CUBE).astype(LOW)
    target = jnp.concatenate([target, target], axis=1)
    near_t = neighbours[b]
    group = 8
    for at in range(0, count, group):
        value, steep = None, None
        for k in range(at, at + group, 2):
            inside = product(scr.source_t[...], one_hot(near_t, (k, k + 1), here, length)).astype(LOW) + target
            v, t = gelu_cubed(inside)
            scr.slope[b, k, :, here] = t[:, :part]
            scr.slope[b, k + 1, :, here] = t[:, part:]
            v, t = v[:, :part] + v[:, part:], t[:, :part] + t[:, part:]
            value, steep = (v, t) if value is None else (value + v, steep + t)
        if at == 0:
            scr.value_sum[...] = value.astype(WIDE)
            scr.slope_sum[b, :, here] = steep.astype(WIDE)
        else:
            scr.value_sum[...] += value.astype(WIDE)
            scr.slope_sum[b, :, here] += steep.astype(WIDE)
    mixed = (scr.value_sum[...] * (0.5 / (count * CUBE))).astype(LOW)
    scr.mixed_t[b, :, here] = mixed
    scr.node[b, here, :] = tokens[b, here, :].astype(WIDE) + trans_left(mixed, packed[:, cols.msg_out])


def token_back(b, cols, packed, tokens, scr, grads):
    count = scr.slope.shape[1]
    d_out = scr.node[b]
    node_low = d_out.astype(LOW)
    grads[:, cols.msg_out] += product(scr.mixed_t[b], node_low)
    d_mixed = trans_right(packed[:, cols.msg_out], node_low) * (1.5 / count)
    scr.mixed_low[b] = d_mixed.astype(LOW)
    d_target = (d_mixed * scr.slope_sum[b]).astype(LOW)
    grads[:, cols.target] += product(d_target, tokens[b])
    return d_out + trans_left(d_target, packed[:, cols.target])


def source_back(b, cols, packed, points, neighbours, scr, grads):
    length = points.shape[1]
    count = neighbours.shape[1]
    near_t = neighbours[b]
    group = 4
    low = scr.mixed_low[b]
    for at in range(0, count, group):
        edges = range(at, at + group)
        inside = jnp.concatenate([scr.slope[b, k] * low for k in edges], axis=1)
        part = trans_right(inside, one_hot(near_t, edges, slice(0, length), length))
        if at == 0:
            scr.total[...] = part
        else:
            scr.total[...] += part
    d_source = scr.total[...].astype(LOW)
    grads[:, cols.source] += product(d_source, points[b])
    return trans_left(d_source, packed[:, cols.source])


def remote(src, dst, send, recv, to):
    return pltpu.make_async_remote_copy(
        src_ref=src, dst_ref=dst, send_sem=send, recv_sem=recv, device_id=to, device_id_type=pl.DeviceIdType.MESH
    )


class Gather:
    def __init__(self, place, packed, per, groups, sems):
        self.section, self.dp, self.rep, self.chips = place
        self.packed, self.per, self.groups = packed, per, groups
        self.core = lax.rem(self.dp, 2)
        self.chip = self.dp // 2
        self.sems = sems
        self.line = self.chips == 4

    def rows(self, dp):
        return pl.ds(pl.multiple_of(dp * self.per, 16), self.per)

    def half(self, group, which):
        start, stop = self.groups[group]
        size = (stop - start) // 2
        return pl.ds(pl.multiple_of(start + which * size, 128), size)

    def whole(self, group):
        start, stop = self.groups[group]
        return pl.ds(start, stop - start)

    def source_dp(self, k, core):
        return 2 * lax.rem(self.chip - k + self.chips, self.chips) + core

    def copy(self, kind, group, k, dp, columns, to):
        spot = self.packed.at[self.rows(dp), columns]
        at = group * self.chips + k
        return remote(spot, spot, self.sems[0].at[kind, at], self.sems[1].at[kind, at], to)

    def along(self, group, k, dp):
        far = 2 * lax.rem(self.chip + k, self.chips) + self.core
        return self.copy(0, group, k, dp, self.half(group, self.rep), (self.section, far, self.rep))

    def over_rep(self, group, k, dp, which):
        return self.copy(1, group, k, dp, self.half(group, which), (self.section, self.dp, 1 - self.rep))

    def sibling(self):
        return (self.section, 2 * self.chip + 1 - self.core, self.rep)

    def over_core(self, kind, group, k, dp, which):
        return self.copy(kind, group, k, dp, self.half(group, which), self.sibling())

    def own_core(self, group, dp):
        return self.copy(4, group, 0, dp, self.whole(group), self.sibling())

    def ends(self, k):
        return jnp.abs(lax.rem(self.chip + k, self.chips) - self.chip) == self.chips - 1

    def onward(self, group):
        to, k = 3 * (self.chip - 1), 2 * self.chip - 1
        spot = self.packed.at[self.rows(self.source_dp(2, self.core)), self.half(group, self.rep)]
        send, recv = self.sems[0].at[5, group * self.chips], self.sems[1].at[0, group * self.chips + k]
        return remote(spot, spot, send, recv, (self.section, 2 * to + self.core, self.rep))

    def inner(self):
        return (self.chip == 1) | (self.chip == 2)

    def begin(self, group):
        for k in range(1, self.chips):
            if self.line:

                @pl.when(jnp.logical_not(self.ends(k)))
                def _():
                    self.along(group, k, self.dp).start()

            else:
                self.along(group, k, self.dp).start()
        self.own_core(group, self.dp).start()

    def middle(self, group):
        order = list(range(1, self.chips))
        if self.line:
            last = jnp.where(self.chip == 0, 1, 3)
            order = [2, 4 - last, last]
        for n, k in enumerate(order):
            dp = self.source_dp(k, self.core)
            self.along(group, k, dp).wait_recv()
            if self.line and n == 0:

                @pl.when(self.inner())
                def _():
                    self.onward(group).start()

            self.over_rep(group, k, dp, self.rep).start()
            self.over_core(2, group, k, dp, self.rep).start()

    def late(self, group):
        for k in range(1, self.chips):
            dp = self.source_dp(k, self.core)
            self.over_rep(group, k, dp, 1 - self.rep).wait_recv()
            self.over_core(3, group, k, dp, 1 - self.rep).start()

    def finish(self, group):
        self.own_core(group, 2 * self.chip + 1 - self.core).wait_recv()
        for k in range(1, self.chips):
            dp = self.source_dp(k, 1 - self.core)
            self.over_core(2, group, k, dp, self.rep).wait_recv()
            self.over_core(3, group, k, dp, 1 - self.rep).wait_recv()

    def drain(self):
        for group in range(len(self.groups)):
            self.own_core(group, self.dp).wait_send()
            if self.line:

                @pl.when(self.inner())
                def _():
                    self.onward(group).wait_send()

            for k in range(1, self.chips):
                dp = self.source_dp(k, self.core)
                if self.line:

                    @pl.when(jnp.logical_not(self.ends(k)))
                    def _():
                        self.along(group, k, self.dp).wait_send()

                else:
                    self.along(group, k, self.dp).wait_send()
                self.over_rep(group, k, dp, self.rep).wait_send()
                self.over_core(2, group, k, dp, self.rep).wait_send()
                self.over_core(3, group, k, dp, 1 - self.rep).wait_send()


class Scatter:
    def __init__(self, place, grads, share, per, columns, sems, at, bufs):
        self.section, self.dp, self.rep, self.chips = place
        self.grads, self.share, self.per, self.columns = grads, share, per, columns
        self.core = lax.rem(self.dp, 2)
        self.chip = self.dp // 2
        self.sems, self.at = sems, at
        self.core_out, self.core_in, self.rep_in, self.far_in, self.end_out, self.end_in = bufs
        self.size = (columns[1] - columns[0]) // 2
        self.rep_out = self.core_out.at[:, :, : self.size]
        self.far_out = self.core_out.at[:, :, self.size :]

    def rows(self, chip, core):
        return pl.ds(pl.multiple_of((2 * chip + core) * self.per, 16), self.per)

    def half(self, which):
        return pl.ds(pl.multiple_of(self.columns[0] + which * self.size, 128), self.size)

    def local(self, which):
        return pl.ds(pl.multiple_of(which * self.size, 128), self.size)

    def pair(self, kind):
        return self.sems[0].at[self.at, kind], self.sems[1].at[self.at, kind]

    def core_copy(self):
        to = (self.section, 2 * self.chip + 1 - self.core, self.rep)
        return remote(self.core_out, self.core_in, *self.pair(0), to)

    def rep_copy(self):
        return remote(self.rep_out, self.rep_in, *self.pair(1), (self.section, self.dp, 1 - self.rep))

    def far_copy(self, k):
        to = (self.section, 2 * lax.rem(self.chip + k, self.chips) + self.core, self.rep)
        return remote(self.far_out.at[k - 1], self.far_in.at[k - 1], *self.pair(2 + k), to)

    def end_copy(self):
        return remote(self.end_out, self.end_in, *self.pair(2), (self.section, self.dp, 1 - self.rep))

    def begin(self):
        start, stop = self.columns
        for chip in range(self.chips):
            self.core_out[chip] = self.grads[self.rows(chip, 1 - self.core), start:stop].astype(LOW)
        self.core_copy().start()

    def middle(self):
        self.core_copy().wait()
        for chip in range(self.chips):
            rows = self.rows(chip, self.core)
            other = self.grads[rows, self.half(1 - self.rep)]
            self.rep_out[chip] = (other + self.core_in[chip, :, self.local(1 - self.rep)].astype(WIDE)).astype(LOW)
        self.rep_copy().start()

    def late(self):
        self.rep_copy().wait_recv()
        for k in range(self.chips):
            chip = lax.rem(self.chip + k, self.chips)
            rows = self.rows(chip, self.core)
            mine = self.grads[rows, self.half(self.rep)]
            mine = mine + self.core_in[chip, :, self.local(self.rep)].astype(WIDE)
            mine = mine + self.rep_in[chip].astype(WIDE)
            if k == 0:
                self.grads[rows, self.half(self.rep)] = mine
            else:
                self.far_out[k - 1] = mine.astype(LOW)
                self.far_copy(k).start()

    def finish(self):
        total = self.grads[self.rows(self.chip, self.core), self.half(self.rep)]
        for k in range(1, self.chips):
            self.far_copy(k).wait_recv()
            total = total + self.far_in[k - 1].astype(WIDE)
        low = total.astype(LOW)
        self.end_out[...] = low
        self.end_copy().start()
        self.share[:, self.half(self.rep)] = low

    def end(self):
        self.end_copy().wait_recv()
        self.share[:, self.half(1 - self.rep)] = self.end_in[...]
        self.rep_copy().wait_send()
        self.end_copy().wait_send()
        for k in range(1, self.chips):
            self.far_copy(k).wait_send()


class Packets:
    def __init__(self, place, scr):
        self.section, self.dp, self.rep, self.chips = place
        self.core, self.chip = lax.rem(self.dp, 2), self.dp // 2
        self.scr = scr
        self.rows = scr.d_mod.shape[0]

    def copy(self, spot, at, to):
        sems = self.scr.packet_sems
        return remote(spot, spot, sems.at[0, at], sems.at[1, at], to)

    def along(self, k, chip):
        spot = self.scr.packets.at[self.core, self.rep, chip]
        far = 2 * lax.rem(self.chip + k, self.chips) + self.core
        return self.copy(spot, k, (self.section, far, self.rep))

    def over_rep(self, rep):
        return self.copy(self.scr.packets.at[self.core, rep], 0, (self.section, self.dp, 1 - self.rep))

    def over_core(self, core):
        to = (self.section, 2 * self.chip + 1 - self.core, self.rep)
        return self.copy(self.scr.packets.at[core], self.chips, to)

    def begin(self):
        scr, width = self.scr, self.scr.node.shape[-1]
        spot = scr.packets.at[self.core, self.rep, self.chip]
        size = 2 * self.rows
        for n in range(2):
            pieces = [scr.d_mod[:, (2 * n + m) * width : (2 * n + m + 1) * width] for m in range(2)]
            spot[n * size : (n + 1) * size, :] = jnp.concatenate(pieces, axis=0).astype(LOW)
        spot[2 * size :, :] = scr.condition[...].astype(LOW)
        for k in range(1, self.chips):
            self.along(k, self.chip).start()

    def middle(self):
        for k in range(1, self.chips):
            self.along(k, lax.rem(self.chip - k + self.chips, self.chips)).wait_recv()
        self.over_rep(self.rep).start()

    def late(self):
        self.over_rep(1 - self.rep).wait_recv()
        self.over_core(self.core).start()

    def finish(self, out, per):
        self.over_core(1 - self.core).wait_recv()
        scr, width, rows = self.scr, self.scr.node.shape[-1], self.rows
        size = 2 * rows
        total = 4 * self.chips

        def gathered(piece):
            part = scr.packets[:, :, :, piece * size : (piece + 1) * size, :].astype(WIDE)
            part = part.reshape(total, 2, rows, width)
            return [part[:, m].reshape(total * rows, width).astype(LOW) for m in range(2)]

        scr.turned[...] = gathered(2)[0].T
        mine = scr.turned[pl.ds(pl.multiple_of(self.dp * per, 16), per), :]
        for n in range(2):
            for m, part in enumerate(gathered(n)):
                at = 2 * n + m
                out[:, at * width : (at + 1) * width] = product(mine, part)
        for k in range(1, self.chips):
            self.along(k, self.chip).wait_send()
        self.over_rep(self.rep).wait_send()
        self.over_core(self.core).wait_send()


def layer_call(cols, linked, sizes, packed_in, raw, points, segments, neighbours, condition, cotangent, per):
    count, length, width = points.shape
    near = neighbours.shape[1]
    per_sim = cols.base.stop - cols.base.start
    chips = sizes[DP] // 2
    part = length // 2
    groups = (
        (0, cols.msg_out.stop),
        (cols.kv.start, cols.base.stop),
        (cols.mod.start, cols.mod.stop),
        (cols.up.start, cols.up.stop),
        (cols.down.start, cols.down.stop),
    )
    summed = (
        (0, cols.gain.stop),
        (cols.target.start, cols.msg_out.stop),
        (cols.kv.start, cols.base.stop),
        (cols.up.start, cols.down.stop),
    )
    many = cols.mod.start
    rows = 8
    weights_in = list(raw) if linked else [packed_in]
    inputs = weights_in + [points, segments, neighbours, condition, cotangent]
    shape = jax.ShapeDtypeStruct
    hidden = cols.up.stop - cols.up.start
    outs = [
        shape((count, 2 * per_sim, width), LOW),
        shape((count, length, width), WIDE),
    ]
    outs.append(shape((per, many), LOW) if linked else shape((width, many), WIDE))
    outs.append(shape((per if linked else width, 4 * width), WIDE))
    scratch = dict(
        source_t=pltpu.VMEM((width, length), LOW),
        value_sum=pltpu.VMEM((width, part), WIDE),
        tokens=pltpu.VMEM((count, length, width), LOW),
        passed=pltpu.VMEM((count, length, width), LOW),
        mixed_t=pltpu.VMEM((count, width, length), LOW),
        slope=pltpu.VMEM((count, near, width, length), LOW),
        slope_sum=pltpu.VMEM((count, width, length), WIDE),
        node=pltpu.VMEM((count, length, width), WIDE),
        mixed_low=pltpu.VMEM((count, width, length), LOW),
        total=pltpu.VMEM((width, length), WIDE),
        point_out=pltpu.VMEM((count, length, width), LOW),
        point_in=pltpu.VMEM((count, length, width), LOW),
        back_in=pltpu.VMEM((count, length, width), LOW),
        modulation=pltpu.VMEM((rows, 4 * width), WIDE),
        condition=pltpu.VMEM((2 * rows, width), WIDE),
        base_unit=pltpu.VMEM((per_sim, width), WIDE),
        base_rows=pltpu.VMEM((per_sim, width), WIDE),
        base_scale=pltpu.VMEM((per_sim, 1), WIDE),
        gain_row=pltpu.VMEM((1, width), WIDE),
        d_gain=pltpu.VMEM((1, width), WIDE),
        d_base_unit=pltpu.VMEM((per_sim, width), WIDE),
        d_base=pltpu.VMEM((per_sim, width), WIDE),
        d_mod=pltpu.VMEM((rows, 4 * width), WIDE),
        lat_buf=pltpu.VMEM((2 * per_sim, width), LOW),
        lat_sem=pltpu.SemaphoreType.DMA,
        pass_sems=pltpu.SemaphoreType.DMA((2, 2 * count)),
        back_sems=pltpu.SemaphoreType.DMA((2, count)),
        point_sems=pltpu.SemaphoreType.DMA((2, count)),
    )
    scratch.update(perceiver_scratch(count, length, width, per_sim))
    bufs = []
    if linked:
        scratch.update(
            packed=pltpu.VMEM((width, cols.total), LOW),
            grads=pltpu.VMEM((width, many), WIDE),
            packets=pltpu.VMEM((2, 2, chips, 6 * rows, width), LOW),
            turned=pltpu.VMEM((width, 4 * chips * rows), LOW),
            packet_sems=pltpu.SemaphoreType.DMA((2, chips + 2)),
            gather_send=pltpu.SemaphoreType.DMA((6, len(groups) * chips)),
            gather_recv=pltpu.SemaphoreType.DMA((6, len(groups) * chips)),
            scatter_send=pltpu.SemaphoreType.DMA((len(summed), 2 + chips)),
            scatter_recv=pltpu.SemaphoreType.DMA((len(summed), 2 + chips)),
        )
        for start, stop in summed:
            size = stop - start
            bufs += [
                pltpu.VMEM((chips, per, size), LOW),
                pltpu.VMEM((chips, per, size), LOW),
                pltpu.VMEM((chips, per, size // 2), LOW),
                pltpu.VMEM((chips - 1, per, size // 2), LOW),
                pltpu.VMEM((per, size // 2), LOW),
                pltpu.VMEM((per, size // 2), LOW),
            ]
    names = list(scratch)

    def body(*refs):
        ins, refs = refs[: len(inputs)], refs[len(inputs) :]
        results, refs = refs[: len(outs)], refs[len(outs) :]
        scr = types.SimpleNamespace(**dict(zip(names, refs)))
        moved = refs[len(names) :]
        points, segments, neighbours, condition, cotangent = ins[-5:]
        latents, point_sum = results[:2]
        section, dp, rep = (lax.axis_index(name) for name in (SECTION, DP, REP))
        other = (1 - section, dp, rep)
        if linked:
            packed, grads = scr.packed, scr.grads
            core, chip = lax.rem(dp, 2), dp // 2
            partners = [other, (section, dp, 1 - rep), (section, 2 * chip + 1 - core, rep)]
            partners += [(section, 2 * lax.rem(chip + k, chips) + core, rep) for k in range(1, chips)]
        else:
            packed, grads = ins[0], results[2]
            partners = [other]
        barrier = pltpu.get_barrier_semaphore()
        for to in partners:
            pl.semaphore_signal(barrier, inc=1, device_id=to, device_id_type=pl.DeviceIdType.MESH)
        if linked:
            place = (section, dp, rep, chips)
            gather = Gather(place, packed, per, groups, (scr.gather_send, scr.gather_recv))
            msg_in, msg_out, norm_gain, mod_weight, query_base, q_weight, kv_weight, o_weight, up_weight, down_weight = ins[:10]
            mine = gather.rows(dp)
            packed[mine, cols.source] = msg_in[0, :, :width]
            packed[mine, cols.target] = msg_in[0, :, width:]
            packed[mine, cols.msg_out] = msg_out[0]
            gain = jnp.broadcast_to(norm_gain[...].astype(WIDE), (128, per)).T
            packed[mine, cols.gain] = gain.astype(LOW)
            packed[mine, cols.kv] = kv_weight[0]
            packed[mine, cols.q] = q_weight[0]
            packed[mine, cols.o] = o_weight[0]
            packed[mine, cols.base] = query_base[0]
            packed[mine, cols.mod] = mod_weight[0]
            packed[mine, cols.up] = up_weight[0]
            packed[mine, cols.down] = down_weight[0]
        pl.semaphore_wait(barrier, len(partners))
        if linked:
            for group in range(len(groups)):
                gather.begin(group)
        grads[...] = jnp.zeros_like(grads)
        for total in (scr.d_gain, scr.d_base_unit, scr.d_base, scr.d_mod, scr.condition):
            total[...] = jnp.zeros_like(total)
        for b in range(count):
            scr.condition[2 * b : 2 * b + 2, :] = condition[b].astype(WIDE)

        tokens = scr.tokens

        @pl.when(section == 0)
        def _():
            tokens[...] = points[...]

        if linked:
            gather.middle(0)
            gather.late(0)
            gather.finish(0)

        def pass_copy(n):
            b, half = n // 2, lax.rem(n, 2)
            rows = pl.ds(pl.multiple_of(half * part, part), part)
            return remote(
                scr.passed.at[b, rows, :], tokens.at[b, rows, :], scr.pass_sems.at[0, n], scr.pass_sems.at[1, n], other
            )

        def back_copy(b):
            return remote(scr.passed.at[b], scr.back_in.at[b], scr.back_sems.at[0, b], scr.back_sems.at[1, b], other)

        def point_copy(b):
            return remote(scr.point_out.at[b], scr.point_in.at[b], scr.point_sems.at[0, b], scr.point_sems.at[1, b], other)

        def forward(b, carry):
            for half in range(2):
                n = 2 * b + half

                @pl.when(section == 1)
                def _():
                    pass_copy(n).wait_recv()

                message_half(b, half, cols, packed, points, tokens, neighbours, scr)

                @pl.when(section == 0)
                def _():
                    rows = slice(half * part, (half + 1) * part)
                    scr.passed[b, rows, :] = scr.node[b, rows, :].astype(LOW)
                    pass_copy(n).start()

            if linked:

                @pl.when(b == 0)
                def _():
                    gather.middle(1)

                @pl.when(b == 1)
                def _():
                    gather.late(1)
                    gather.middle(2)

            return carry

        lax.fori_loop(0, count, forward, 0)
        if linked:
            gather.late(2)
            gather.finish(1)
            gather.middle(3)
            gather.finish(2)
            scatters = [
                Scatter(
                    place, grads, results[2], per, summed[n], (scr.scatter_send, scr.scatter_recv), n,
                    moved[6 * n : 6 * n + 6],
                )
                for n in range(len(summed))
            ]
        base = packed[:, cols.base].astype(WIDE).T
        scr.base_rows[...] = base
        unit, scale = normalised(base)
        scr.base_unit[...] = unit
        scr.base_scale[...] = scale
        scr.gain_row[...] = packed[:, cols.gain].astype(WIDE).T[:1]
        scr.modulation[...] = product(scr.condition[...].astype(LOW), packed[:, cols.mod])[:rows]

        def attention(b, carry):
            attend(b, cols, packed, segments, scr)
            if linked:

                @pl.when(b == 0)
                def _():
                    gather.late(3)
                    gather.middle(4)

                @pl.when(b == 1)
                def _():
                    gather.late(4)

            return carry

        lax.fori_loop(0, count, attention, 0)
        if linked:
            gather.finish(3)
            gather.finish(4)

        def feed(b, carry):
            feed_forward(b, cols, packed, cotangent, latents, grads, scr)
            return carry

        lax.fori_loop(0, count, feed, 0)
        if linked:
            scatters[3].begin()

        def token_step(b):
            return token_back(b, cols, packed, tokens, scr, grads)

        def attention_back(b, carry):
            attend_back(b, cols, packed, segments, grads, scr)

            @pl.when(section == 1)
            def _():
                scr.passed[b] = token_step(b).astype(LOW)
                back_copy(b).start()

            if linked:

                @pl.when(b == 0)
                def _():
                    scatters[3].middle()

            return carry

        lax.fori_loop(0, count, attention_back, 0)
        d_rows = normalised_back(scr.d_base_unit[...], scr.base_unit[...], scr.base_scale[...])
        grads[:, cols.base] = (d_rows + scr.d_base[...]).T
        grads[:, cols.gain] = jnp.broadcast_to(scr.d_gain[...], (128, width)).T
        if linked:
            packet = Packets(place, scr)
            scatters[2].begin()
            packet.begin()
            scatters[3].late()
        else:
            results[3][...] = trans_left(scr.condition[:rows].astype(LOW), scr.d_mod[...].astype(LOW))

        def backward(b, carry):
            point_sum[b] = jnp.zeros((length, width), WIDE)

            @pl.when(section == 0)
            def _():
                back_copy(b).wait_recv()
                scr.node[b] = scr.node[b] + scr.back_in[b].astype(WIDE)
                point_sum[b] = token_step(b)

            if linked:

                @pl.when(b == count - 1)
                def _():
                    scatters[1].begin()

            d_points = source_back(b, cols, packed, points, neighbours, scr, grads)
            scr.point_out[b] = (point_sum[b] + d_points).astype(LOW)
            point_copy(b).start()
            if linked:

                @pl.when(b == 0)
                def _():
                    scatters[2].middle()
                    packet.middle()

                @pl.when(b == 1)
                def _():
                    scatters[3].finish()
                    packet.late()

            return carry

        lax.fori_loop(0, count, backward, 0)
        if linked:
            scatters[0].begin()
            scatters[1].middle()
            scatters[0].middle()
            scatters[2].late()
            scatters[3].end()
            scatters[1].late()
            scatters[0].late()
            packet.finish(results[3], per)
            scatters[2].finish()
        for b in range(count):
            point_copy(b).wait_recv()
            point_sum[b] = scr.point_out[b].astype(WIDE) + scr.point_in[b].astype(WIDE)
        if linked:
            scatters[1].finish()
            scatters[0].finish()
            for n in (2, 1, 0):
                scatters[n].end()
            gather.drain()

        pltpu.make_async_copy(scr.lat_buf, latents.at[count - 1], scr.lat_sem).wait()

        @pl.when(section == 0)
        def _():
            for n in range(2 * count):
                pass_copy(n).wait_send()

        @pl.when(section == 1)
        def _():
            for b in range(count):
                back_copy(b).wait_send()

        for b in range(count):
            point_copy(b).wait_send()

    spec = pl.BlockSpec(memory_space=pltpu.VMEM)
    return pl.pallas_call(
        body,
        out_shape=outs,
        in_specs=[spec] * len(inputs),
        out_specs=[pl.BlockSpec(memory_space=pl.ANY)] + [spec] * (len(outs) - 1),
        scratch_shapes=list(scratch.values()) + bufs,
        compiler_params=pltpu.CompilerParams(
            vmem_limit_bytes=VMEM_BYTES, collective_id=0, has_side_effects=True
        ),
        cost_estimate=pl.CostEstimate(flops=10**10, bytes_accessed=1 << 24, transcendentals=0),
        name="layers",
    )(*inputs)


def finish_call(cols, latents, point_sum, share, mod_share):
    per, width = share.shape[0], point_sum.shape[-1]
    pieces = (cols.msg_out, cols.gain, cols.base, cols.q, cols.kv, cols.o, cols.up, cols.down)
    gain_at = 1

    def body(latents, point_sum, mod_share, share, latents_out, point_out, mod_out, msg_in_out, *rest):
        outs, (latents_buf, point_buf, mod_buf, sems) = rest[:-4], rest[-4:]
        arrays = ((latents, latents_buf, latents_out), (point_sum, point_buf, point_out), (mod_share, mod_buf, mod_out))
        arriving = [pltpu.make_async_copy(a, buf, sems.at[0, n]) for n, (a, buf, _) in enumerate(arrays)]
        leaving = [pltpu.make_async_copy(buf, a, sems.at[1, n]) for n, (_, buf, a) in enumerate(arrays)]
        for move in arriving:
            move.start()
        for first, then in zip(arriving, leaving):
            first.wait()
            then.start()
        msg_in_out[0, :, :width] = share[:, cols.source].astype(WIDE)
        msg_in_out[0, :, width:] = share[:, cols.target].astype(WIDE)
        for n, piece in enumerate(pieces):
            value = share[:, piece].astype(WIDE)
            if n == gain_at:
                outs[n][...] = value.T[:1]
            else:
                outs[n][0] = value
        for move in leaving:
            move.wait()

    shape = jax.ShapeDtypeStruct
    whole, local = pl.BlockSpec(memory_space=pl.ANY), pl.BlockSpec(memory_space=pltpu.VMEM)
    outs = [shape(latents.shape, LOW), shape(point_sum.shape, WIDE), shape(mod_share.shape, WIDE)]
    outs.append(shape((1, per, 2 * width), WIDE))
    for n, piece in enumerate(pieces):
        outs.append(shape((1, per) if n == gain_at else (1, per, piece.stop - piece.start), WIDE))
    latents, point_sum, mod, msg_in, msg_out, gain, base, q, kv, o, up, down = pl.pallas_call(
        body,
        out_shape=outs,
        in_specs=[whole, whole, whole, local],
        out_specs=[whole, whole, whole] + [local] * (1 + len(pieces)),
        scratch_shapes=[pltpu.VMEM(a.shape, a.dtype) for a in (latents, point_sum, mod_share)]
        + [pltpu.SemaphoreType.DMA((2, 3))],
        compiler_params=pltpu.CompilerParams(vmem_limit_bytes=VMEM_BYTES),
        cost_estimate=pl.CostEstimate(flops=10**6, bytes_accessed=1 << 23, transcendentals=0),
        name="finish",
    )(latents, point_sum, mod_share, share)
    turn = lambda array: jnp.swapaxes(array, 1, 2)
    return (latents[None], point_sum, turn(msg_in), msg_out, gain, mod[None], turn(base), q, kv, o, up, turn(down))


def on_device(
    points,
    segments,
    neighbours,
    condition,
    msg_in,
    msg_out,
    norm_gain,
    mod_weight,
    query_base,
    q_weight,
    kv_weight,
    o_weight,
    up_weight,
    down_weight,
    cotangent,
):
    count, length, width = points.shape
    per = q_weight.shape[1]
    hidden = up_weight.shape[2]
    per_sim = query_base.shape[1]
    cols = Columns(width, hidden, per_sim)
    sizes = {name: lax.axis_size(name) for name in (SECTION, DP, REP)}
    linked = per % 16 == 0 and sizes[DP] % 2 == 0 and sizes[REP] == 2
    raw = (
        jnp.swapaxes(msg_in, 1, 2),
        msg_out,
        norm_gain,
        mod_weight,
        jnp.swapaxes(query_base, 1, 2),
        q_weight,
        kv_weight,
        o_weight,
        up_weight,
        jnp.swapaxes(down_weight, 1, 2),
    )
    near_t = jnp.swapaxes(neighbours, 1, 2)
    if linked:
        outs = layer_call(cols, True, sizes, None, raw, points, segments, near_t, condition, cotangent[0], per)
        return finish_call(cols, *outs)
    turned = msg_in[0].T
    own = jnp.concatenate(
        [
            turned[:, :width],
            jnp.broadcast_to(norm_gain[0][:, None], (per, 128)),
            turned[:, width:],
            msg_out[0],
            kv_weight[0],
            q_weight[0],
            o_weight[0],
            query_base[0].T,
            up_weight[0],
            down_weight[0].T,
            mod_weight[0],
        ],
        axis=1,
    )
    packed = lax.all_gather(own, DP, axis=0, tiled=True)
    latents, point_sum, grads, mod_grads = layer_call(
        cols, False, sizes, packed, None, points, segments, near_t, condition, cotangent[0], per
    )
    grads = jnp.concatenate([grads, mod_grads], axis=1)
    share = lax.psum_scatter(grads, DP, scatter_dimension=0, tiled=True)
    share = lax.psum(share.astype(LOW), REP).astype(WIDE)
    return (
        latents[None],
        point_sum,
        jnp.concatenate([share[:, cols.source], share[:, cols.target]], axis=1).T[None],
        share[None, :, cols.msg_out],
        share[None, :, cols.gain.start],
        share[None, :, cols.mod],
        share[:, cols.base].T[None],
        share[None, :, cols.q],
        share[None, :, cols.kv],
        share[None, :, cols.o],
        share[None, :, cols.up],
        share[:, cols.down].T[None],
    )


def solution(mesh):
    placed = (
        P((DP, REP), None, None),
        P((DP, REP), None),
        P((DP, REP), None, None),
        P((DP, REP), None, None),
        P(SECTION, None, DP),
        P(SECTION, DP, None),
        P(SECTION, DP),
        P(SECTION, DP, None),
        P(SECTION, None, DP),
        P(SECTION, DP, None),
        P(SECTION, DP, None),
        P(SECTION, DP, None),
        P(SECTION, DP, None),
        P(SECTION, None, DP),
        P(SECTION, (DP, REP), None, None),
    )
    return jax.shard_map(
        on_device,
        mesh=mesh,
        in_specs=placed,
        out_specs=(
            P(SECTION, (DP, REP), None, None),
            P((DP, REP), None, None),
            P(SECTION, None, DP),
            P(SECTION, DP, None),
            P(SECTION, DP),
            P(SECTION, DP, None),
            P(SECTION, None, DP),
            P(SECTION, DP, None),
            P(SECTION, DP, None),
            P(SECTION, DP, None),
            P(SECTION, DP, None),
            P(SECTION, None, DP),
        ),
        check_vma=False,
    )
```

time: 454 us -> 141 us (0.31)
  waiting for transfers between devices: 263 us -> 0 us
  local copies, waits for them, and re-layouts: 23.4 us -> 0 us
  other arithmetic: 21 us -> 0 us
  between operations: 13.9 us -> 0.82 us
  Pallas kernels: 128 us -> 139 us
    reduce_scatter x1 -> x0, waiting for transfers between devices: 119 us -> none  [on_device(): share = lax.psum_scatter(grads, 'dp', scatter_dimension=0, tiled=True)]
    psum x2 -> x0, waiting for transfers between devices: 62.4 us -> none  [the longest x1 34.5 us: on_device(): share = lax.psum(share.astype(LOW), 'rep').astype(WIDE)]
    all_gather x1 -> x0, waiting for transfers between devices: 61.9 us -> none  [on_device(): packed = lax.all_gather(own, 'dp', axis=0, tiled=True)]
    ppermute x2 -> x0, waiting for transfers between devices: 19.3 us -> none  [the longest x1 15.5 us: on_device(): arrived = lax.ppermute(node.astype(LOW), 'section', forth)]
    pallas_call x5 -> x2, Pallas kernels: 128 us -> 139 us  [the longest x1 134 us: layer_call(): pl.pallas_call(body, out_shape=outs, in_specs=[spec] * len(inputs), out_s...]
    unnamed x26 -> x0, local copies, waits for them, and re-layouts: 10.8 us -> none
    concatenate x1 -> x0, other arithmetic: 9.58 us -> none  [on_device(): grads = jnp.concatenate([grads_msg, grads[:, cols.msg_out.stop:]], axis=1)]
    convert_element_type x6 -> x0, other arithmetic: 9.38 us -> none  [the longest x2 3.55 us: on_device(): share = lax.psum(share.astype(LOW), 'rep').astype(WIDE)]
  transfers between devices with their start and end apart: 6 -> 0, of which waited for: 6 -> 0; matrix products, arithmetic and copies ran while one was open for 3% -> 0% of each run, Pallas kernels for 0% -> 0%
where the time goes in v2:
time: 141 us; the launch traced here: 139 us
  Pallas kernels  139 us (99%)
    pallas_call x1, Pallas kernels, layer_call(): pl.pallas_call(body, out_shape=outs, in_specs=[spec] * len(inputs), out_s...  134 us
    pallas_call x1, Pallas kernels, finish_call(): pl.pallas_call(body, out_shape=outs, in_specs=[whole, whole, whole, local...  4.88 us

profile of v2, /device:TPU:2, one launch (start us, length us, event | category | flops | bytes accessed | tf_op | source)
XLA Modules:
  0.0 139.4 jit_solution(15206579087091317674)
XLA Ops:
  0.7 133.7 %layers.1 = (bf16[3,512,384]{2,1,0:T(8,128)(2,1)}, f32[3,256,384]{2,1,0:T(8,128)}, bf16[48,6144]{1,0:T(8,128)(2,1)}, f32[48,1536]{1,0:T(8,128)}) custom-call(bf16[1,48,768]{2,1,0:T(8,128)(2,1)} %bitcast.16, bf16[1,48,384]{2,1,0:T(8,128)(2,1)} %refs_1_.1, bf16[1,48]{1,0:T(2,128)(2,1)} %refs_2_.1, bf16[1,48,1536]{2,1,0:T(8,128)(2,1)} %refs_3_.1, ...), custom_call_target="tpu_custom_call" | custom-call | flops 10000000000 | bytes 16777216 | tf_op jit(solution)/shard_map/layers/pallas_call | solution.py:978
  134.3 4.9 %finish.1 = (bf16[3,512,384]{2,1,0:T(8,128)(2,1)}, f32[3,256,384]{2,1,0:T(8,128)}, f32[48,1536]{1,0:T(8,128)}, f32[1,48,768]{2,1,0:T(8,128)}, f32[1,48,384]{2,1,...) custom-call(bf16[3,512,384]{2,1,0:T(8,128)(2,1)} %get-tuple-element., ...), custom_call_target="tpu_custom_call" | custom-call | flops 1000000 | bytes 8388608 | tf_op jit(solution)/shard_map/finish/pallas_call | solution.py:1024

commit v3 on v2

--- a/solution.py
+++ b/solution.py
@@ -14,6 +14,7 @@
 TANH_THREE = 0.7978845608028654 * 0.044715
 CUBE = TANH_THREE ** (1.0 / 3.0)
 SECTION, DP, REP = "section", "dp", "rep"
+CHUNKS = 3
 LOW = jnp.bfloat16
 WIDE = jnp.float32
 VMEM_BYTES = 63 * 1024 * 1024
@@ -73,14 +74,19 @@
             ("q", width),
             ("o", width),
             ("base", per_sim),
-            ("up", hidden),
-            ("down", hidden),
-            ("mod", 4 * width),
         )
         at = 0
         for name, extent in self.pieces:
             setattr(self, name, slice(at, at + extent))
             at += extent
+        self.chunk = hidden // CHUNKS
+        self.up, self.down = [], []
+        for _ in range(CHUNKS):
+            self.up.append(slice(at, at + self.chunk))
+            self.down.append(slice(at + self.chunk, at + 2 * self.chunk))
+            at += 2 * self.chunk
+        self.mod = slice(at, at + 4 * width)
+        at += 4 * width
         self.total = at
 
 
@@ -125,7 +131,7 @@
     unit, _ = normalised(scr.node[b])
     normed = (unit * scr.gain_row[...]).astype(LOW)
     keyval = product(normed, packed[:, cols.kv]).astype(LOW)
-    scr.keyval[b] = keyval
+    scr.values[b] = keyval[:, width:]
     scr.keyval_t[b] = keyval.T
     own_col, own_row = evolution_masks(b, segments, length)
     low_row = (own_row.astype(LOW), (1.0 - own_row).astype(LOW))
@@ -153,43 +159,59 @@
             scr.attended_t[b, here, per_sim:] = out_t[HEAD_DIM:]
 
 
-def feed_forward(b, cols, packed, cotangent, latents, grads, scr):
+def residual_of(b, cols, packed, scr):
+    residual = trans_left(scr.attended_t[b], packed[:, cols.o])
+    return residual + jnp.concatenate([scr.base_rows[...]] * 2, axis=0)
+
+
+def feed_in(b, cols, packed, scr):
     width = scr.node.shape[-1]
     per_sim = scr.base_rows.shape[0]
     _, _, scale_two, shift_two = mod_rows(b, scr, width)
+    unit, _ = normalised(residual_of(b, cols, packed, scr))
+    second = jnp.concatenate(
+        [(1.0 + scale_two[s]) * unit[s * per_sim : (s + 1) * per_sim] + shift_two[s] for s in range(2)], axis=0
+    ).astype(LOW)
+    scr.second[b] = second
+    scr.second_t[:, pl.ds(pl.multiple_of(b * 2 * per_sim, 2 * per_sim), 2 * per_sim)] = second.T
+
+
+def feed_chunk(b, at, cols, packed, cotangent, scr):
+    up, down = cols.up[at], cols.down[at]
+    queries = scr.second.shape[1]
+    here = pl.ds(pl.multiple_of(b * queries, queries), queries)
+    value, steep = gelu_cubed((product(scr.second[b], packed[:, up]) * CUBE).astype(LOW))
+    hidden = value * jnp.asarray(0.5 / CUBE, LOW)
+    d_up = (product(cotangent[b], packed[:, down]) * 1.5).astype(LOW) * steep
+    scr.hidden[here, :] = hidden
+    scr.d_up[here, :] = d_up
+    if at == 0:
+        scr.d_second[b] = trans_right(d_up, packed[:, up])
+    else:
+        scr.d_second[b] += trans_right(d_up, packed[:, up])
+    if at == 0:
+        scr.lat_sum[b] = trans_right(hidden, packed[:, down])
+    elif at < CHUNKS - 1:
+        scr.lat_sum[b] += trans_right(hidden, packed[:, down])
+
+
+def feed_latents(b, cols, packed, latents, scr):
+    queries = scr.second.shape[1]
+    here = pl.ds(pl.multiple_of(b * queries, queries), queries)
+    last = trans_right(scr.hidden[here, :], packed[:, cols.down[CHUNKS - 1]])
+    scr.second[b] = (scr.lat_sum[b] + last).astype(LOW)
+    pltpu.make_async_copy(scr.second.at[b], latents.at[b], scr.lat_sems.at[b]).start()
+
+
+def feed_out(b, cols, packed, cotangent, grads, scr):
+    width = scr.node.shape[-1]
+    per_sim = scr.base_rows.shape[0]
+    _, _, scale_two, _ = mod_rows(b, scr, width)
     attended_t = scr.attended_t[b]
-    residual = trans_left(attended_t, packed[:, cols.o])
-    residual = residual + jnp.concatenate([scr.base_rows[...]] * 2, axis=0)
+    residual = residual_of(b, cols, packed, scr)
     res_unit, res_scale = normalised(residual)
-    second = jnp.concatenate(
-        [(1.0 + scale_two[s]) * res_unit[s * per_sim : (s + 1) * per_sim] + shift_two[s] for s in range(2)], axis=0
-    ).astype(LOW)
-    cot = cotangent[b]
-    scr.second_t[...] = second.T
-    scr.cot_t[...] = cot.T
-    lat = None
-    d_second = None
-    chunk = 512
-    for at in range(0, cols.up.stop - cols.up.start, chunk):
-        up = slice(cols.up.start + at, cols.up.start + at + chunk)
-        down = slice(cols.down.start + at, cols.down.start + at + chunk)
-        value, steep = gelu_cubed((product(second, packed[:, up]) * CUBE).astype(LOW))
-        hidden = value * jnp.asarray(0.5 / CUBE, LOW)
-        d_up = (product(cot, packed[:, down]) * 1.5).astype(LOW) * steep
-        part = trans_right(hidden, packed[:, down])
-        lat = part if lat is None else lat + part
-        part = trans_right(d_up, packed[:, up])
-        d_second = part if d_second is None else d_second + part
-        grads[:, down] += product(scr.cot_t[...], hidden)
-        grads[:, up] += product(scr.second_t[...], d_up)
-    out_copy = pltpu.make_async_copy(scr.lat_buf, latents.at[b], scr.lat_sem)
-
-    @pl.when(b > 0)
-    def _():
-        out_copy.wait()
-
-    scr.lat_buf[...] = (residual + lat).astype(LOW)
-    out_copy.start()
+    scr.lat_sum[b] += residual
+    d_second = scr.d_second[b]
     d_res = []
     for s in range(2):
         rows_at = slice(s * per_sim, (s + 1) * per_sim)
@@ -198,7 +220,7 @@
         scr.d_mod[pl.ds(2 * b + s, 1), 2 * width : 3 * width] = jnp.sum(d_sim * unit_sim, axis=0, keepdims=True)
         scr.d_mod[pl.ds(2 * b + s, 1), 3 * width :] = jnp.sum(d_sim, axis=0, keepdims=True)
         d_res.append(
-            cot[rows_at].astype(WIDE)
+            cotangent[b, rows_at, :].astype(WIDE)
             + normalised_back(d_sim * (1.0 + scale_two[s]), unit_sim, res_scale[rows_at])
         )
     scr.d_base[...] += d_res[0] + d_res[1]
@@ -221,13 +243,13 @@
     low_row = (own_row.astype(LOW), (1.0 - own_row).astype(LOW))
     mask = own_col > 0.5
     left_half = lax.broadcasted_iota(jnp.int32, (1, block), 1) < HEAD_DIM
-    keyval = scr.keyval[b]
+    values_all = scr.values[b]
     query = scr.query[b]
     d_att = scr.attended_t[b]
     for pair in range(HEADS // 2):
-        values = spread_heads(keyval[:, width + pair * block : width + (pair + 1) * block], own_col)
+        here = slice(pair * block, (pair + 1) * block)
+        values = spread_heads(values_all[:, here], own_col)
         query_pair = by_sim(query, pair)
-        here = slice(pair * block, (pair + 1) * block)
         d_att_pair = jnp.concatenate([d_att[here, :per_sim], d_att[here, per_sim:]], axis=0)
         d_keys, d_values = [], []
         for h in range(2):
@@ -272,17 +294,22 @@
     scr.node[b] = normalised_back(d_normed * gain, unit, node_scale)
 
 
-def perceiver_scratch(count, length, width, per_sim):
+def perceiver_scratch(count, length, width, per_sim, chunk):
     queries = 2 * per_sim
     return dict(
-        keyval=pltpu.VMEM((count, length, 2 * width), LOW),
+        values=pltpu.VMEM((count, length, width), LOW),
         keyval_t=pltpu.VMEM((count, 2 * width, length), LOW),
         query=pltpu.VMEM((count, queries, width), LOW),
         weights_t=pltpu.VMEM((count, HEADS, length, per_sim), LOW),
         attended_t=pltpu.VMEM((count, width, queries), LOW),
         overlap=pltpu.VMEM((count, 8, queries), WIDE),
-        second_t=pltpu.VMEM((width, queries), LOW),
-        cot_t=pltpu.VMEM((width, queries), LOW),
+        second=pltpu.VMEM((count, queries, width), LOW),
+        second_t=pltpu.VMEM((width, count * queries), LOW),
+        cot_t=pltpu.VMEM((width, count * queries), LOW),
+        hidden=pltpu.VMEM((count * queries, chunk), LOW),
+        d_up=pltpu.VMEM((count * queries, chunk), LOW),
+        lat_sum=pltpu.VMEM((count, queries, width), WIDE),
+        d_second=pltpu.VMEM((count, queries, width), WIDE),
         query_t=pltpu.VMEM((width, queries), LOW),
         d_keyval=pltpu.VMEM((length, 2 * width), LOW),
     )
@@ -334,7 +361,7 @@
     node_low = d_out.astype(LOW)
     grads[:, cols.msg_out] += product(scr.mixed_t[b], node_low)
     d_mixed = trans_right(packed[:, cols.msg_out], node_low) * (1.5 / count)
-    scr.mixed_low[b] = d_mixed.astype(LOW)
+    scr.mixed_t[b] = d_mixed.astype(LOW)
     d_target = (d_mixed * scr.slope_sum[b]).astype(LOW)
     grads[:, cols.target] += product(d_target, tokens[b])
     return d_out + trans_left(d_target, packed[:, cols.target])
@@ -345,7 +372,7 @@
     count = neighbours.shape[1]
     near_t = neighbours[b]
     group = 4
-    low = scr.mixed_low[b]
+    low = scr.mixed_t[b]
     for at in range(0, count, group):
         edges = range(at, at + group)
         inside = jnp.concatenate([scr.slope[b, k] * low for k in edges], axis=1)
@@ -365,17 +392,23 @@
     )
 
 
+class Packed:
+    def __init__(self, ref):
+        self.ref = ref
+
+    def __getitem__(self, index):
+        piece = self.ref[:, :, :, index[1]]
+        return piece.reshape(-1, piece.shape[-1])
+
+
 class Gather:
-    def __init__(self, place, packed, per, groups, sems):
+    def __init__(self, place, ref, groups, sems):
         self.section, self.dp, self.rep, self.chips = place
-        self.packed, self.per, self.groups = packed, per, groups
+        self.ref, self.groups = ref, groups
         self.core = lax.rem(self.dp, 2)
         self.chip = self.dp // 2
-        self.sems = sems
+        self.send, self.recv = sems
         self.line = self.chips == 4
-
-    def rows(self, dp):
-        return pl.ds(pl.multiple_of(dp * self.per, 16), self.per)
 
     def half(self, group, which):
         start, stop = self.groups[group]
@@ -386,106 +419,98 @@
         start, stop = self.groups[group]
         return pl.ds(start, stop - start)
 
-    def source_dp(self, k, core):
-        return 2 * lax.rem(self.chip - k + self.chips, self.chips) + core
-
-    def copy(self, kind, group, k, dp, columns, to):
-        spot = self.packed.at[self.rows(dp), columns]
-        at = group * self.chips + k
-        return remote(spot, spot, self.sems[0].at[kind, at], self.sems[1].at[kind, at], to)
-
-    def along(self, group, k, dp):
+    def source(self, k):
+        return lax.rem(self.chip - k + self.chips, self.chips)
+
+    def copy(self, spot, send, group, recv, to):
+        return remote(spot, spot, self.send.at[send], self.recv.at[group, recv], to)
+
+    def along(self, group, k, chip):
+        spot = self.ref.at[chip, self.core, :, self.half(group, self.rep)]
         far = 2 * lax.rem(self.chip + k, self.chips) + self.core
-        return self.copy(0, group, k, dp, self.half(group, self.rep), (self.section, far, self.rep))
-
-    def over_rep(self, group, k, dp, which):
-        return self.copy(1, group, k, dp, self.half(group, which), (self.section, self.dp, 1 - self.rep))
-
-    def sibling(self):
-        return (self.section, 2 * self.chip + 1 - self.core, self.rep)
-
-    def over_core(self, kind, group, k, dp, which):
-        return self.copy(kind, group, k, dp, self.half(group, which), self.sibling())
-
-    def own_core(self, group, dp):
-        return self.copy(4, group, 0, dp, self.whole(group), self.sibling())
+        return self.copy(spot, k - 1, group, k - 1, (self.section, far, self.rep))
+
+    def onward(self, group):
+        to, k = 3 * (self.chip - 1), 2 * self.chip - 1
+        spot = self.ref.at[self.source(2), self.core, :, self.half(group, self.rep)]
+        return self.copy(spot, self.chips - 1, group, k - 1, (self.section, 2 * to + self.core, self.rep))
+
+    def over_rep(self, group, chip):
+        spot = self.ref.at[chip, self.core, :, self.half(group, self.rep)]
+        return self.copy(spot, self.chips, group, self.chips - 1, (self.section, self.dp, 1 - self.rep))
+
+    def from_rep(self, group):
+        spot = self.ref.at[pl.ds(0, self.chips - 1), self.core, :, self.half(group, 1 - self.rep)]
+        return self.copy(spot, self.chips, group, self.chips - 1, (self.section, self.dp, 1 - self.rep))
+
+    def over_core(self, group, core):
+        spot = self.ref.at[:, core, :, self.whole(group)]
+        to = (self.section, 2 * self.chip + 1 - self.core, self.rep)
+        return self.copy(spot, self.chips + 1, group, self.chips, to)
 
     def ends(self, k):
         return jnp.abs(lax.rem(self.chip + k, self.chips) - self.chip) == self.chips - 1
 
-    def onward(self, group):
-        to, k = 3 * (self.chip - 1), 2 * self.chip - 1
-        spot = self.packed.at[self.rows(self.source_dp(2, self.core)), self.half(group, self.rep)]
-        send, recv = self.sems[0].at[5, group * self.chips], self.sems[1].at[0, group * self.chips + k]
-        return remote(spot, spot, send, recv, (self.section, 2 * to + self.core, self.rep))
-
     def inner(self):
         return (self.chip == 1) | (self.chip == 2)
 
+    def direct(self, k, act):
+        if self.line:
+
+            @pl.when(jnp.logical_not(self.ends(k)))
+            def _():
+                act()
+
+        else:
+            act()
+
     def begin(self, group):
         for k in range(1, self.chips):
-            if self.line:
-
-                @pl.when(jnp.logical_not(self.ends(k)))
-                def _():
-                    self.along(group, k, self.dp).start()
-
-            else:
-                self.along(group, k, self.dp).start()
-        self.own_core(group, self.dp).start()
-
-    def middle(self, group):
-        order = list(range(1, self.chips))
+            self.direct(k, lambda: self.along(group, k, self.chip).start())
+
+    def arrived(self, group, n):
+        last = jnp.where(self.chip == 0, 1, 3)
+        k = [2, 4 - last, last][n] if self.line else n + 1
+        chip = self.source(k)
+        self.along(group, k, chip).wait_recv()
+        if self.line and n == 0:
+
+            @pl.when(self.inner())
+            def _():
+                self.onward(group).start()
+
+        self.over_rep(group, chip).start()
+
+    def near(self, group):
+        for n in range(self.chips - 2):
+            self.arrived(group, n)
+
+    def far(self, group):
+        self.arrived(group, self.chips - 2)
+
+    def late(self, group):
+        self.from_rep(group).wait_recv()
+        self.over_core(group, self.core).start()
+
+    def finish(self, group):
+        self.over_core(group, 1 - self.core).wait_recv()
+
+    def drain(self):
+        total = self.ref.shape[-1]
+        part = pl.ds(0, total // 2)
+        home = (self.section, self.dp, 1 - self.rep)
+        for k in range(1, self.chips):
+            spot = self.ref.at[self.chip, self.core, :, part]
+            self.direct(k, lambda: self.copy(spot, k - 1, 0, k - 1, home).wait_send())
         if self.line:
-            last = jnp.where(self.chip == 0, 1, 3)
-            order = [2, 4 - last, last]
-        for n, k in enumerate(order):
-            dp = self.source_dp(k, self.core)
-            self.along(group, k, dp).wait_recv()
-            if self.line and n == 0:
-
-                @pl.when(self.inner())
-                def _():
-                    self.onward(group).start()
-
-            self.over_rep(group, k, dp, self.rep).start()
-            self.over_core(2, group, k, dp, self.rep).start()
-
-    def late(self, group):
-        for k in range(1, self.chips):
-            dp = self.source_dp(k, self.core)
-            self.over_rep(group, k, dp, 1 - self.rep).wait_recv()
-            self.over_core(3, group, k, dp, 1 - self.rep).start()
-
-    def finish(self, group):
-        self.own_core(group, 2 * self.chip + 1 - self.core).wait_recv()
-        for k in range(1, self.chips):
-            dp = self.source_dp(k, 1 - self.core)
-            self.over_core(2, group, k, dp, self.rep).wait_recv()
-            self.over_core(3, group, k, dp, 1 - self.rep).wait_recv()
-
-    def drain(self):
-        for group in range(len(self.groups)):
-            self.own_core(group, self.dp).wait_send()
-            if self.line:
-
-                @pl.when(self.inner())
-                def _():
-                    self.onward(group).wait_send()
-
-            for k in range(1, self.chips):
-                dp = self.source_dp(k, self.core)
-                if self.line:
-
-                    @pl.when(jnp.logical_not(self.ends(k)))
-                    def _():
-                        self.along(group, k, self.dp).wait_send()
-
-                else:
-                    self.along(group, k, self.dp).wait_send()
-                self.over_rep(group, k, dp, self.rep).wait_send()
-                self.over_core(2, group, k, dp, self.rep).wait_send()
-                self.over_core(3, group, k, dp, 1 - self.rep).wait_send()
+
+            @pl.when(self.inner())
+            def _():
+                self.copy(self.ref.at[self.chip, self.core, :, part], self.chips - 1, 0, 0, home).wait_send()
+
+        spot = self.ref.at[pl.ds(0, self.chips - 1), self.core, :, part]
+        self.copy(spot, self.chips, 0, 0, home).wait_send()
+        self.copy(self.ref.at[:, self.core], self.chips + 1, 0, 0, home).wait_send()
 
 
 class Scatter:
@@ -521,7 +546,10 @@
 
     def far_copy(self, k):
         to = (self.section, 2 * lax.rem(self.chip + k, self.chips) + self.core, self.rep)
-        return remote(self.far_out.at[k - 1], self.far_in.at[k - 1], *self.pair(2 + k), to)
+        return remote(self.far_out.at[k - 1], self.far_in.at[k - 1], *self.pair(3), to)
+
+    def far_all(self):
+        return remote(self.far_out.at[: self.chips - 1], self.far_in, *self.pair(3), (self.section, self.dp, 1 - self.rep))
 
     def end_copy(self):
         return remote(self.end_out, self.end_in, *self.pair(2), (self.section, self.dp, 1 - self.rep))
@@ -556,8 +584,8 @@
 
     def finish(self):
         total = self.grads[self.rows(self.chip, self.core), self.half(self.rep)]
+        self.far_all().wait_recv()
         for k in range(1, self.chips):
-            self.far_copy(k).wait_recv()
             total = total + self.far_in[k - 1].astype(WIDE)
         low = total.astype(LOW)
         self.end_out[...] = low
@@ -569,41 +597,32 @@
         self.share[:, self.half(1 - self.rep)] = self.end_in[...]
         self.rep_copy().wait_send()
         self.end_copy().wait_send()
-        for k in range(1, self.chips):
-            self.far_copy(k).wait_send()
+        self.far_all().wait_send()
 
 
 class Packets:
-    def __init__(self, place, scr):
+    def __init__(self, place, packets, sems, at):
         self.section, self.dp, self.rep, self.chips = place
         self.core, self.chip = lax.rem(self.dp, 2), self.dp // 2
-        self.scr = scr
-        self.rows = scr.d_mod.shape[0]
-
-    def copy(self, spot, at, to):
-        sems = self.scr.packet_sems
-        return remote(spot, spot, sems.at[0, at], sems.at[1, at], to)
+        self.packets, self.sems, self.at = packets, sems, at
+
+    def copy(self, spot, n, to):
+        return remote(spot, spot, self.sems.at[0, self.at, n], self.sems.at[1, self.at, n], to)
 
     def along(self, k, chip):
-        spot = self.scr.packets.at[self.core, self.rep, chip]
+        spot = self.packets.at[self.core, self.rep, chip]
         far = 2 * lax.rem(self.chip + k, self.chips) + self.core
         return self.copy(spot, k, (self.section, far, self.rep))
 
     def over_rep(self, rep):
-        return self.copy(self.scr.packets.at[self.core, rep], 0, (self.section, self.dp, 1 - self.rep))
+        return self.copy(self.packets.at[self.core, rep], 0, (self.section, self.dp, 1 - self.rep))
 
     def over_core(self, core):
         to = (self.section, 2 * self.chip + 1 - self.core, self.rep)
-        return self.copy(self.scr.packets.at[core], self.chips, to)
-
-    def begin(self):
-        scr, width = self.scr, self.scr.node.shape[-1]
-        spot = scr.packets.at[self.core, self.rep, self.chip]
-        size = 2 * self.rows
-        for n in range(2):
-            pieces = [scr.d_mod[:, (2 * n + m) * width : (2 * n + m + 1) * width] for m in range(2)]
-            spot[n * size : (n + 1) * size, :] = jnp.concatenate(pieces, axis=0).astype(LOW)
-        spot[2 * size :, :] = scr.condition[...].astype(LOW)
+        return self.copy(self.packets.at[core], self.chips, to)
+
+    def begin(self, pieces):
+        self.packets[self.core, self.rep, self.chip] = jnp.concatenate(pieces, axis=0).astype(LOW)
         for k in range(1, self.chips):
             self.along(k, self.chip).start()
 
@@ -616,27 +635,28 @@
         self.over_rep(1 - self.rep).wait_recv()
         self.over_core(self.core).start()
 
-    def finish(self, out, per):
+    def finish(self):
         self.over_core(1 - self.core).wait_recv()
-        scr, width, rows = self.scr, self.scr.node.shape[-1], self.rows
-        size = 2 * rows
-        total = 4 * self.chips
-
-        def gathered(piece):
-            part = scr.packets[:, :, :, piece * size : (piece + 1) * size, :].astype(WIDE)
-            part = part.reshape(total, 2, rows, width)
-            return [part[:, m].reshape(total * rows, width).astype(LOW) for m in range(2)]
-
-        scr.turned[...] = gathered(2)[0].T
-        mine = scr.turned[pl.ds(pl.multiple_of(self.dp * per, 16), per), :]
-        for n in range(2):
-            for m, part in enumerate(gathered(n)):
-                at = 2 * n + m
-                out[:, at * width : (at + 1) * width] = product(mine, part)
         for k in range(1, self.chips):
             self.along(k, self.chip).wait_send()
         self.over_rep(self.rep).wait_send()
         self.over_core(self.core).wait_send()
+        width = self.packets.shape[-1]
+        result = []
+        for at in range(0, self.packets.shape[3], 16):
+            part = self.packets[:, :, :, at : at + 16, :].astype(WIDE).reshape(4 * self.chips, 2, 8, width)
+            result.append([part[:, m].reshape(32 * self.chips, width).astype(LOW) for m in range(2)])
+        return result
+
+
+def mod_share(scr, late, early, place, out, per):
+    width = scr.node.shape[-1]
+    second, condition = late.finish()
+    (first,) = early.finish()
+    scr.turned[...] = condition[0].T
+    mine = scr.turned[pl.ds(pl.multiple_of(place[1] * per, 16), per), :]
+    for at, part in enumerate(first + second):
+        out[:, at * width : (at + 1) * width] = product(mine, part)
 
 
 def layer_call(cols, linked, sizes, packed_in, raw, points, segments, neighbours, condition, cotangent, per):
@@ -645,28 +665,27 @@
     per_sim = cols.base.stop - cols.base.start
     chips = sizes[DP] // 2
     part = length // 2
+    parts = tuple((cols.up[n].start, cols.down[n].stop) for n in range(CHUNKS))
     groups = (
         (0, cols.msg_out.stop),
         (cols.kv.start, cols.base.stop),
         (cols.mod.start, cols.mod.stop),
-        (cols.up.start, cols.up.stop),
-        (cols.down.start, cols.down.stop),
-    )
+    ) + parts
     summed = (
         (0, cols.gain.stop),
         (cols.target.start, cols.msg_out.stop),
-        (cols.kv.start, cols.base.stop),
-        (cols.up.start, cols.down.stop),
-    )
+        (cols.kv.start, cols.kv.stop),
+        (cols.q.start, cols.base.stop),
+    ) + parts
     many = cols.mod.start
     rows = 8
     weights_in = list(raw) if linked else [packed_in]
     inputs = weights_in + [points, segments, neighbours, condition, cotangent]
     shape = jax.ShapeDtypeStruct
-    hidden = cols.up.stop - cols.up.start
     outs = [
         shape((count, 2 * per_sim, width), LOW),
-        shape((count, length, width), WIDE),
+        shape((count, length, width), LOW),
+        shape((count, length, width), LOW),
     ]
     outs.append(shape((per, many), LOW) if linked else shape((width, many), WIDE))
     outs.append(shape((per if linked else width, 4 * width), WIDE))
@@ -679,7 +698,6 @@
         slope=pltpu.VMEM((count, near, width, length), LOW),
         slope_sum=pltpu.VMEM((count, width, length), WIDE),
         node=pltpu.VMEM((count, length, width), WIDE),
-        mixed_low=pltpu.VMEM((count, width, length), LOW),
         total=pltpu.VMEM((width, length), WIDE),
         point_out=pltpu.VMEM((count, length, width), LOW),
         point_in=pltpu.VMEM((count, length, width), LOW),
@@ -694,25 +712,26 @@
         d_base_unit=pltpu.VMEM((per_sim, width), WIDE),
         d_base=pltpu.VMEM((per_sim, width), WIDE),
         d_mod=pltpu.VMEM((rows, 4 * width), WIDE),
-        lat_buf=pltpu.VMEM((2 * per_sim, width), LOW),
-        lat_sem=pltpu.SemaphoreType.DMA,
+        lat_sems=pltpu.SemaphoreType.DMA((count,)),
         pass_sems=pltpu.SemaphoreType.DMA((2, 2 * count)),
         back_sems=pltpu.SemaphoreType.DMA((2, count)),
+        point_local=pltpu.SemaphoreType.DMA((2,)),
         point_sems=pltpu.SemaphoreType.DMA((2, count)),
     )
-    scratch.update(perceiver_scratch(count, length, width, per_sim))
+    scratch.update(perceiver_scratch(count, length, width, per_sim, cols.chunk))
     bufs = []
     if linked:
         scratch.update(
-            packed=pltpu.VMEM((width, cols.total), LOW),
+            packed=pltpu.VMEM((chips, 2, per, cols.total), LOW),
             grads=pltpu.VMEM((width, many), WIDE),
-            packets=pltpu.VMEM((2, 2, chips, 6 * rows, width), LOW),
+            packets_two=pltpu.VMEM((2, 2, chips, 4 * rows, width), LOW),
+            packets_one=pltpu.VMEM((2, 2, chips, 2 * rows, width), LOW),
             turned=pltpu.VMEM((width, 4 * chips * rows), LOW),
-            packet_sems=pltpu.SemaphoreType.DMA((2, chips + 2)),
-            gather_send=pltpu.SemaphoreType.DMA((6, len(groups) * chips)),
-            gather_recv=pltpu.SemaphoreType.DMA((6, len(groups) * chips)),
-            scatter_send=pltpu.SemaphoreType.DMA((len(summed), 2 + chips)),
-            scatter_recv=pltpu.SemaphoreType.DMA((len(summed), 2 + chips)),
+            packet_sems=pltpu.SemaphoreType.DMA((2, 2, chips + 1)),
+            gather_send=pltpu.SemaphoreType.DMA((chips + 2,)),
+            gather_recv=pltpu.SemaphoreType.DMA((len(groups), chips + 1)),
+            scatter_send=pltpu.SemaphoreType.DMA((len(summed), 4)),
+            scatter_recv=pltpu.SemaphoreType.DMA((len(summed), 4)),
         )
         for start, stop in summed:
             size = stop - start
@@ -732,46 +751,50 @@
         scr = types.SimpleNamespace(**dict(zip(names, refs)))
         moved = refs[len(names) :]
         points, segments, neighbours, condition, cotangent = ins[-5:]
-        latents, point_sum = results[:2]
+        latents, point_mine, point_other = results[:3]
         section, dp, rep = (lax.axis_index(name) for name in (SECTION, DP, REP))
         other = (1 - section, dp, rep)
         if linked:
-            packed, grads = scr.packed, scr.grads
+            packed, grads = Packed(scr.packed), scr.grads
             core, chip = lax.rem(dp, 2), dp // 2
             partners = [other, (section, dp, 1 - rep), (section, 2 * chip + 1 - core, rep)]
             partners += [(section, 2 * lax.rem(chip + k, chips) + core, rep) for k in range(1, chips)]
         else:
-            packed, grads = ins[0], results[2]
+            packed, grads = ins[0], results[3]
             partners = [other]
         barrier = pltpu.get_barrier_semaphore()
         for to in partners:
             pl.semaphore_signal(barrier, inc=1, device_id=to, device_id_type=pl.DeviceIdType.MESH)
         if linked:
             place = (section, dp, rep, chips)
-            gather = Gather(place, packed, per, groups, (scr.gather_send, scr.gather_recv))
+            gather = Gather(place, scr.packed, groups, (scr.gather_send, scr.gather_recv))
             msg_in, msg_out, norm_gain, mod_weight, query_base, q_weight, kv_weight, o_weight, up_weight, down_weight = ins[:10]
-            mine = gather.rows(dp)
-            packed[mine, cols.source] = msg_in[0, :, :width]
-            packed[mine, cols.target] = msg_in[0, :, width:]
-            packed[mine, cols.msg_out] = msg_out[0]
+            mine = scr.packed.at[chip, core]
+            mine[:, cols.source] = msg_in[0, :, :width]
+            mine[:, cols.target] = msg_in[0, :, width:]
+            mine[:, cols.msg_out] = msg_out[0]
             gain = jnp.broadcast_to(norm_gain[...].astype(WIDE), (128, per)).T
-            packed[mine, cols.gain] = gain.astype(LOW)
-            packed[mine, cols.kv] = kv_weight[0]
-            packed[mine, cols.q] = q_weight[0]
-            packed[mine, cols.o] = o_weight[0]
-            packed[mine, cols.base] = query_base[0]
-            packed[mine, cols.mod] = mod_weight[0]
-            packed[mine, cols.up] = up_weight[0]
-            packed[mine, cols.down] = down_weight[0]
+            mine[:, cols.gain] = gain.astype(LOW)
+            mine[:, cols.kv] = kv_weight[0]
+            mine[:, cols.q] = q_weight[0]
+            mine[:, cols.o] = o_weight[0]
+            mine[:, cols.base] = query_base[0]
+            mine[:, cols.mod] = mod_weight[0]
+            for n in range(CHUNKS):
+                piece = slice(n * cols.chunk, (n + 1) * cols.chunk)
+                mine[:, cols.up[n]] = up_weight[0, :, piece]
+                mine[:, cols.down[n]] = down_weight[0, :, piece]
         pl.semaphore_wait(barrier, len(partners))
         if linked:
-            for group in range(len(groups)):
-                gather.begin(group)
-        grads[...] = jnp.zeros_like(grads)
+            gather.begin(0)
+            gather.begin(1)
+        first = grads.at[:, : cols.base.stop]
+        first[...] = jnp.zeros_like(first)
         for total in (scr.d_gain, scr.d_base_unit, scr.d_base, scr.d_mod, scr.condition):
             total[...] = jnp.zeros_like(total)
         for b in range(count):
             scr.condition[2 * b : 2 * b + 2, :] = condition[b].astype(WIDE)
+            scr.cot_t[:, b * 2 * per_sim : (b + 1) * 2 * per_sim] = cotangent[b].T
 
         tokens = scr.tokens
 
@@ -780,9 +803,13 @@
             tokens[...] = points[...]
 
         if linked:
-            gather.middle(0)
+            gather.near(0)
+            gather.far(0)
+            gather.begin(2)
             gather.late(0)
             gather.finish(0)
+            gather.near(1)
+            gather.begin(3)
 
         def pass_copy(n):
             b, half = n // 2, lax.rem(n, 2)
@@ -797,7 +824,7 @@
         def point_copy(b):
             return remote(scr.point_out.at[b], scr.point_in.at[b], scr.point_sems.at[0, b], scr.point_sems.at[1, b], other)
 
-        def forward(b, carry):
+        def forward(b):
             for half in range(2):
                 n = 2 * b + half
 
@@ -813,72 +840,141 @@
                     scr.passed[b, rows, :] = scr.node[b, rows, :].astype(LOW)
                     pass_copy(n).start()
 
+                ahead = jnp.where(b == 2, 8 * half - 1, n + 2)
+                gather_at(jnp.where(section == 0, n, ahead), (1, 3, 5, 7) if half else (0, 2, 4))
+
+        def prepare():
+            base = packed[:, cols.base].astype(WIDE).T
+            scr.base_rows[...] = base
+            unit, scale = normalised(base)
+            scr.base_unit[...] = unit
+            scr.base_scale[...] = scale
+            scr.gain_row[...] = packed[:, cols.gain].astype(WIDE).T[:1]
+            scr.modulation[...] = product(scr.condition[...].astype(LOW), packed[:, cols.mod])[:rows]
+
+        def gather_step(n):
+            if n == 0:
+                gather.far(1)
+            elif n == 1:
+                gather.near(2)
+                gather.begin(4)
+            elif n == 2:
+                gather.far(2)
+            elif n == 3:
+                gather.late(1)
+                gather.near(3)
+                gather.begin(5)
+            elif n == 4:
+                gather.far(3)
+            elif n == 5:
+                gather.late(2)
+                gather.finish(1)
+                gather.near(4)
+                gather.finish(2)
+                prepare()
+            elif n == 6:
+                gather.far(4)
+                gather.late(3)
+                gather.near(5)
+            else:
+                gather.far(5)
+                gather.late(4)
+                gather.finish(3)
+
+        def gather_at(at, choices):
             if linked:
-
-                @pl.when(b == 0)
-                def _():
-                    gather.middle(1)
-
-                @pl.when(b == 1)
-                def _():
-                    gather.late(1)
-                    gather.middle(2)
+                for n in choices:
+
+                    @pl.when(at == n)
+                    def _():
+                        gather_step(n)
+
+        if linked:
+
+            @pl.when(section == 1)
+            def _():
+                gather_step(0)
+                gather_step(1)
+
+        else:
+            prepare()
+
+        def early(step, carry):
+            late_one = (step == 3) & (section == 1)
+            early_one = (step == 2) & (section == 1)
+            message = ((step < count) | late_one) & jnp.logical_not(early_one)
+            b = jnp.where(message, jnp.minimum(step, count - 1), jnp.where(early_one, 0, step - count))
+
+            @pl.when(message)
+            def _():
+                forward(b)
+
+            @pl.when(jnp.logical_not(message))
+            def _():
+                attend(b, cols, packed, segments, scr)
+                gather_at(jnp.where(section == 0, 6 + b, 6 + 2 * b), (6, 7))
 
             return carry
 
-        lax.fori_loop(0, count, forward, 0)
+        lax.fori_loop(0, 2 * count, early, 0)
         if linked:
-            gather.late(2)
-            gather.finish(1)
-            gather.middle(3)
-            gather.finish(2)
             scatters = [
                 Scatter(
-                    place, grads, results[2], per, summed[n], (scr.scatter_send, scr.scatter_recv), n,
+                    place, grads, results[3], per, summed[n], (scr.scatter_send, scr.scatter_recv), n,
                     moved[6 * n : 6 * n + 6],
                 )
                 for n in range(len(summed))
             ]
-        base = packed[:, cols.base].astype(WIDE).T
-        scr.base_rows[...] = base
-        unit, scale = normalised(base)
-        scr.base_unit[...] = unit
-        scr.base_scale[...] = scale
-        scr.gain_row[...] = packed[:, cols.gain].astype(WIDE).T[:1]
-        scr.modulation[...] = product(scr.condition[...].astype(LOW), packed[:, cols.mod])[:rows]
-
-        def attention(b, carry):
-            attend(b, cols, packed, segments, scr)
+
+        def feed_first(b, carry):
+            feed_in(b, cols, packed, scr)
+            return carry
+
+        lax.fori_loop(0, count, feed_first, 0)
+        for at in range(CHUNKS):
+            if linked and at > 0:
+                gather.finish(3 + at)
+
+            def feed_step(b, carry):
+                feed_chunk(b, at, cols, packed, cotangent, scr)
+                if linked and at == 0:
+
+                    @pl.when(b == 0)
+                    def _():
+                        gather.late(5)
+
+                return carry
+
+            lax.fori_loop(0, count, feed_step, 0)
+            grads[:, cols.down[at]] = product(scr.cot_t[...], scr.hidden[...])
+            grads[:, cols.up[at]] = product(scr.second_t[...], scr.d_up[...])
+            if linked:
+                scatters[4 + at].begin()
+                if at > 0:
+                    scatters[3 + at].middle()
+                if at > 1:
+                    scatters[2 + at].late()
+
+        if linked:
+            halves = [slice(width * n, width * (n + 1)) for n in range(4)]
+            packet_two = Packets(place, scr.packets_two, scr.packet_sems, 0)
+            packet_one = Packets(place, scr.packets_one, scr.packet_sems, 1)
+
+        def token_step(b):
+            return token_back(b, cols, packed, tokens, scr, grads)
+
+        def attention_back(b, carry):
+            feed_out(b, cols, packed, cotangent, grads, scr)
             if linked:
 
                 @pl.when(b == 0)
                 def _():
-                    gather.late(3)
-                    gather.middle(4)
-
-                @pl.when(b == 1)
+                    scatters[6].middle()
+
+                @pl.when(b == count - 1)
                 def _():
-                    gather.late(4)
-
-            return carry
-
-        lax.fori_loop(0, count, attention, 0)
-        if linked:
-            gather.finish(3)
-            gather.finish(4)
-
-        def feed(b, carry):
-            feed_forward(b, cols, packed, cotangent, latents, grads, scr)
-            return carry
-
-        lax.fori_loop(0, count, feed, 0)
-        if linked:
-            scatters[3].begin()
-
-        def token_step(b):
-            return token_back(b, cols, packed, tokens, scr, grads)
-
-        def attention_back(b, carry):
+                    packet_two.begin([scr.d_mod[:, halves[2]], scr.d_mod[:, halves[3]], scr.condition[...]])
+
             attend_back(b, cols, packed, segments, grads, scr)
 
             @pl.when(section == 1)
@@ -890,76 +986,125 @@
 
                 @pl.when(b == 0)
                 def _():
-                    scatters[3].middle()
+                    scatters[5].late()
+                    scatters[4].finish()
+
+                @pl.when(b == 1)
+                def _():
+                    scatters[6].late()
+                    scatters[5].finish()
 
             return carry
 
         lax.fori_loop(0, count, attention_back, 0)
+        if linked:
+            scatters[2].begin()
         d_rows = normalised_back(scr.d_base_unit[...], scr.base_unit[...], scr.base_scale[...])
         grads[:, cols.base] = (d_rows + scr.d_base[...]).T
         grads[:, cols.gain] = jnp.broadcast_to(scr.d_gain[...], (128, width)).T
         if linked:
-            packet = Packets(place, scr)
-            scatters[2].begin()
-            packet.begin()
-            scatters[3].late()
+            scatters[3].begin()
+            packet_one.begin([scr.d_mod[:, halves[0]], scr.d_mod[:, halves[1]]])
+            packet_two.middle()
+
+            @pl.when(section == 1)
+            def _():
+                scatters[1].begin()
+
+            scatters[6].finish()
+            scatters[2].middle()
         else:
-            results[3][...] = trans_left(scr.condition[:rows].astype(LOW), scr.d_mod[...].astype(LOW))
+            results[4][...] = trans_left(scr.condition[:rows].astype(LOW), scr.d_mod[...].astype(LOW))
 
         def backward(b, carry):
-            point_sum[b] = jnp.zeros((length, width), WIDE)
-
             @pl.when(section == 0)
             def _():
                 back_copy(b).wait_recv()
                 scr.node[b] = scr.node[b] + scr.back_in[b].astype(WIDE)
-                point_sum[b] = token_step(b)
+                scr.node[b] = token_step(b)
+
+            @pl.when(section == 1)
+            def _():
+                scr.node[b] = jnp.zeros((length, width), WIDE)
 
             if linked:
 
-                @pl.when(b == count - 1)
+                @pl.when((b == count - 1) & (section == 0))
                 def _():
                     scatters[1].begin()
 
             d_points = source_back(b, cols, packed, points, neighbours, scr, grads)
-            scr.point_out[b] = (point_sum[b] + d_points).astype(LOW)
+            scr.point_out[b] = (scr.node[b] + d_points).astype(LOW)
             point_copy(b).start()
             if linked:
 
                 @pl.when(b == 0)
                 def _():
-                    scatters[2].middle()
-                    packet.middle()
+                    scatters[3].middle()
+                    packet_one.middle()
+                    packet_two.late()
+
+                    @pl.when(section == 1)
+                    def _():
+                        scatters[1].middle()
 
                 @pl.when(b == 1)
                 def _():
-                    scatters[3].finish()
-                    packet.late()
+                    packet_one.late()
+                    scatters[2].late()
 
             return carry
 
         lax.fori_loop(0, count, backward, 0)
         if linked:
             scatters[0].begin()
-            scatters[1].middle()
+            scatters[3].late()
+
+            @pl.when(section == 0)
+            def _():
+                scatters[1].middle()
+
+        feed_latents(0, cols, packed, latents, scr)
+        if linked:
             scatters[0].middle()
-            scatters[2].late()
-            scatters[3].end()
-            scatters[1].late()
+
+            @pl.when(section == 1)
+            def _():
+                scatters[1].late()
+
+        for b in range(1, count):
+            feed_latents(b, cols, packed, latents, scr)
+        if linked:
+            scatters[2].finish()
+
+            @pl.when(section == 0)
+            def _():
+                scatters[1].late()
+
             scatters[0].late()
-            packet.finish(results[3], per)
-            scatters[2].finish()
+            scatters[3].finish()
+            for n in range(4, 4 + CHUNKS):
+                scatters[n].end()
+            mod_share(scr, packet_two, packet_one, place, results[4], per)
         for b in range(count):
             point_copy(b).wait_recv()
-            point_sum[b] = scr.point_out[b].astype(WIDE) + scr.point_in[b].astype(WIDE)
+        point_moves = [
+            pltpu.make_async_copy(scr.point_out, point_mine, scr.point_local.at[0]),
+            pltpu.make_async_copy(scr.point_in, point_other, scr.point_local.at[1]),
+        ]
+        for move in point_moves:
+            move.start()
         if linked:
             scatters[1].finish()
             scatters[0].finish()
-            for n in (2, 1, 0):
+            for n in (3, 2, 1, 0):
                 scatters[n].end()
             gather.drain()
-
-        pltpu.make_async_copy(scr.lat_buf, latents.at[count - 1], scr.lat_sem).wait()
+        for move in point_moves:
+            move.wait()
+
+        for b in range(count):
+            pltpu.make_async_copy(scr.second.at[b], latents.at[b], scr.lat_sems.at[b]).wait()
 
         @pl.when(section == 0)
         def _():
@@ -979,7 +1124,7 @@
         body,
         out_shape=outs,
         in_specs=[spec] * len(inputs),
-        out_specs=[pl.BlockSpec(memory_space=pl.ANY)] + [spec] * (len(outs) - 1),
+        out_specs=[pl.BlockSpec(memory_space=pl.ANY)] * 3 + [spec] * (len(outs) - 3),
         scratch_shapes=list(scratch.values()) + bufs,
         compiler_params=pltpu.CompilerParams(
             vmem_limit_bytes=VMEM_BYTES, collective_id=0, has_side_effects=True
@@ -989,14 +1134,14 @@
     )(*inputs)
 
 
-def finish_call(cols, latents, point_sum, share, mod_share):
-    per, width = share.shape[0], point_sum.shape[-1]
-    pieces = (cols.msg_out, cols.gain, cols.base, cols.q, cols.kv, cols.o, cols.up, cols.down)
+def finish_call(cols, latents, point_mine, point_other, share, mod_share):
+    per, width = share.shape[0], point_mine.shape[-1]
+    pieces = ([cols.msg_out], [cols.gain], [cols.base], [cols.q], [cols.kv], [cols.o], cols.up, cols.down)
     gain_at = 1
 
-    def body(latents, point_sum, mod_share, share, latents_out, point_out, mod_out, msg_in_out, *rest):
-        outs, (latents_buf, point_buf, mod_buf, sems) = rest[:-4], rest[-4:]
-        arrays = ((latents, latents_buf, latents_out), (point_sum, point_buf, point_out), (mod_share, mod_buf, mod_out))
+    def body(latents, mod_share, point_mine, point_other, share, latents_out, mod_out, point_out, msg_in_out, *rest):
+        outs, (latents_buf, mod_buf, sems) = rest[:-3], rest[-3:]
+        arrays = ((latents, latents_buf, latents_out), (mod_share, mod_buf, mod_out))
         arriving = [pltpu.make_async_copy(a, buf, sems.at[0, n]) for n, (a, buf, _) in enumerate(arrays)]
         leaving = [pltpu.make_async_copy(buf, a, sems.at[1, n]) for n, (_, buf, a) in enumerate(arrays)]
         for move in arriving:
@@ -1004,34 +1149,39 @@
         for first, then in zip(arriving, leaving):
             first.wait()
             then.start()
+        point_out[...] = point_mine[...].astype(WIDE) + point_other[...].astype(WIDE)
         msg_in_out[0, :, :width] = share[:, cols.source].astype(WIDE)
         msg_in_out[0, :, width:] = share[:, cols.target].astype(WIDE)
         for n, piece in enumerate(pieces):
-            value = share[:, piece].astype(WIDE)
-            if n == gain_at:
-                outs[n][...] = value.T[:1]
-            else:
-                outs[n][0] = value
+            at = 0
+            for place in piece:
+                value = share[:, place].astype(WIDE)
+                size = place.stop - place.start
+                if n == gain_at:
+                    outs[n][...] = value.T[:1]
+                else:
+                    outs[n][0, :, at : at + size] = value
+                at += size
         for move in leaving:
             move.wait()
 
     shape = jax.ShapeDtypeStruct
     whole, local = pl.BlockSpec(memory_space=pl.ANY), pl.BlockSpec(memory_space=pltpu.VMEM)
-    outs = [shape(latents.shape, LOW), shape(point_sum.shape, WIDE), shape(mod_share.shape, WIDE)]
+    outs = [shape(latents.shape, LOW), shape(mod_share.shape, WIDE), shape(point_mine.shape, WIDE)]
     outs.append(shape((1, per, 2 * width), WIDE))
     for n, piece in enumerate(pieces):
-        outs.append(shape((1, per) if n == gain_at else (1, per, piece.stop - piece.start), WIDE))
-    latents, point_sum, mod, msg_in, msg_out, gain, base, q, kv, o, up, down = pl.pallas_call(
+        outs.append(shape((1, per) if n == gain_at else (1, per, sum(place.stop - place.start for place in piece)), WIDE))
+    latents, mod, point_sum, msg_in, msg_out, gain, base, q, kv, o, up, down = pl.pallas_call(
         body,
         out_shape=outs,
-        in_specs=[whole, whole, whole, local],
-        out_specs=[whole, whole, whole] + [local] * (1 + len(pieces)),
-        scratch_shapes=[pltpu.VMEM(a.shape, a.dtype) for a in (latents, point_sum, mod_share)]
-        + [pltpu.SemaphoreType.DMA((2, 3))],
+        in_specs=[whole, whole, local, local, local],
+        out_specs=[whole, whole] + [local] * (2 + len(pieces)),
+        scratch_shapes=[pltpu.VMEM(a.shape, a.dtype) for a in (latents, mod_share)]
+        + [pltpu.SemaphoreType.DMA((2, 2))],
         compiler_params=pltpu.CompilerParams(vmem_limit_bytes=VMEM_BYTES),
         cost_estimate=pl.CostEstimate(flops=10**6, bytes_accessed=1 << 23, transcendentals=0),
         name="finish",
-    )(latents, point_sum, mod_share, share)
+    )(latents, mod_share, point_mine, point_other, share)
     turn = lambda array: jnp.swapaxes(array, 1, 2)
     return (latents[None], point_sum, turn(msg_in), msg_out, gain, mod[None], turn(base), q, kv, o, up, turn(down))
 
@@ -1087,14 +1237,19 @@
             q_weight[0],
             o_weight[0],
             query_base[0].T,
-            up_weight[0],
-            down_weight[0].T,
+            *sum(
+                (
+                    [up_weight[0, :, n : n + cols.chunk], down_weight[0, n : n + cols.chunk].T]
+                    for n in range(0, hidden, cols.chunk)
+                ),
+                [],
+            ),
             mod_weight[0],
         ],
         axis=1,
     )
     packed = lax.all_gather(own, DP, axis=0, tiled=True)
-    latents, point_sum, grads, mod_grads = layer_call(
+    latents, point_mine, point_other, grads, mod_grads = layer_call(
         cols, False, sizes, packed, None, points, segments, near_t, condition, cotangent[0], per
     )
     grads = jnp.concatenate([grads, mod_grads], axis=1)
@@ -1102,7 +1257,7 @@
     share = lax.psum(share.astype(LOW), REP).astype(WIDE)
     return (
         latents[None],
-        point_sum,
+        point_mine.astype(WIDE) + point_other.astype(WIDE),
         jnp.concatenate([share[:, cols.source], share[:, cols.target]], axis=1).T[None],
         share[None, :, cols.msg_out],
         share[None, :, cols.gain.start],
@@ -1111,8 +1266,8 @@
         share[None, :, cols.q],
         share[None, :, cols.kv],
         share[None, :, cols.o],
-        share[None, :, cols.up],
-        share[:, cols.down].T[None],
+        jnp.concatenate([share[None, :, piece] for piece in cols.up], axis=2),
+        jnp.concatenate([share[:, piece] for piece in cols.down], axis=1).T[None],
     )
 
 

time: 141 us -> 121 us (0.86)
  Pallas kernels: 139 us -> 120 us
    pallas_call x1, Pallas kernels: 134 us -> 114 us  [layer_call(): pl.pallas_call(body, out_shape=outs, in_specs=[spec] * len(inputs), out_s...]
where the time goes in v3:
time: 121 us; the launch traced here: 120 us
  Pallas kernels  120 us (99%)
    pallas_call x1, Pallas kernels, layer_call(): pl.pallas_call(body, out_shape=outs, in_specs=[spec] * len(inputs), out_s...  114 us
    pallas_call x1, Pallas kernels, finish_call(): pl.pallas_call(body, out_shape=outs, in_specs=[whole, whole, local, local...  5.22 us

profile of v3, /device:TPU:2, one launch (start us, length us, event | category | flops | bytes accessed | tf_op | source)
XLA Modules:
  0.0 120.4 jit_solution(9793215426145853753)
XLA Ops:
  0.7 114.4 %layers.1 = (bf16[3,512,384]{2,1,0:T(8,128)(2,1)}, bf16[3,256,384]{2,1,0:T(8,128)(2,1)}, bf16[3,256,384]{2,1,0:T(8,128)(2,1)}, bf16[48,6144]{1,0:T(8,128)(2,1)}, f32[48,1536]{1,0:T(8,128)}) custom-call(bf16[1,48,768]{2,1,0:T(8,128)(2,1)} %bitcast.16, bf16[1,48,384]{2,1,0:T(8,128)(2,1)} %refs_1_.1, bf16[1,48]{1,0:T(2,128)(2,1)} %refs_2_.1, ...), custom_call_target="tpu_custom_call" | custom-call | flops 10000000000 | bytes 16777216 | tf_op jit(solution)/shard_map/layers/pallas_call | solution.py:1123
  115.0 5.2 %finish.1 = (bf16[3,512,384]{2,1,0:T(8,128)(2,1)}, f32[48,1536]{1,0:T(8,128)}, f32[3,256,384]{2,1,0:T(8,128)}, f32[1,48,768]{2,1,0:T(8,128)}, f32[1,48,384]{2,1,...) custom-call(bf16[3,512,384]{2,1,0:T(8,128)(2,1)} %get-tuple-element., ...), custom_call_target="tpu_custom_call" | custom-call | flops 1000000 | bytes 8388608 | tf_op jit(solution)/shard_map/finish/pallas_call | solution.py:1174

commit v4 on v3

--- a/solution.py
+++ b/solution.py
@@ -138,25 +138,27 @@
     query = (product(first_rows(b, scr, width), packed[:, cols.q]).astype(LOW) * 0.125).astype(LOW)
     scr.query[b] = query
     mask = own_col > 0.5
+    ones = jnp.concatenate([jnp.broadcast_to(own_row, (8, length)), jnp.broadcast_to(1.0 - own_row, (8, length))], axis=0)
+    ones = ones.astype(LOW)
     for pair in range(HEADS // 2):
         keys = spread_heads(keyval[:, pair * block : (pair + 1) * block], own_col)
-        query_pair = by_sim(query, pair)
+        raw_pair = trans_right(jnp.concatenate(keys, axis=0), by_sim(query, pair))
         for h in range(2):
             head = 2 * pair + h
-            raw = trans_right(keys[h], query_pair)
+            raw = raw_pair[h * length : (h + 1) * length]
             top_first = jnp.max(jnp.where(mask, raw, -3e38), axis=0, keepdims=True)
             top_second = jnp.max(jnp.where(mask, -3e38, raw), axis=0, keepdims=True)
-            grown = jnp.exp(raw - jnp.where(mask, top_first, top_second))
-            sum_first = jnp.sum(jnp.where(mask, grown, 0.0), axis=0, keepdims=True)
-            sum_second = jnp.sum(jnp.where(mask, 0.0, grown), axis=0, keepdims=True)
-            share = (grown * jnp.where(mask, 1.0 / sum_first, 1.0 / sum_second)).astype(LOW)
-            scr.weights_t[b, head] = share
+            grown = jnp.exp(raw - jnp.where(mask, top_first, top_second)).astype(LOW)
+            scr.weights_t[b, head] = grown
             here = slice(head * HEAD_DIM, (head + 1) * HEAD_DIM)
             value_t = scr.keyval_t[b, width + here.start : width + here.stop, :]
-            value_sims = jnp.concatenate([value_t * low_row[0], value_t * low_row[1]], axis=0)
-            out_t = product(value_sims, share).astype(LOW)
-            scr.attended_t[b, here, :per_sim] = out_t[:HEAD_DIM]
-            scr.attended_t[b, here, per_sim:] = out_t[HEAD_DIM:]
+            value_sims = jnp.concatenate([value_t * low_row[0], value_t * low_row[1], ones], axis=0)
+            out_t = product(value_sims, grown)
+            inverse = 1.0 / out_t[2 * HEAD_DIM :]
+            scr.inverse[b, head : head + 1, :per_sim] = inverse[:1]
+            scr.inverse[b, head : head + 1, per_sim:] = inverse[8:9]
+            scr.attended_t[b, here, :per_sim] = (out_t[:HEAD_DIM] * inverse[:1]).astype(LOW)
+            scr.attended_t[b, here, per_sim:] = (out_t[HEAD_DIM : 2 * HEAD_DIM] * inverse[8:9]).astype(LOW)
 
 
 def residual_of(b, cols, packed, scr):
@@ -226,13 +228,13 @@
     scr.d_base[...] += d_res[0] + d_res[1]
     res_low = jnp.concatenate(d_res, axis=0).astype(LOW)
     grads[:, cols.o] += product(attended_t, res_low)
-    d_att = trans_right(packed[:, cols.o], res_low).astype(LOW)
-    both = d_att.astype(WIDE) * attended_t.astype(WIDE)
+    d_att = trans_right(packed[:, cols.o], res_low)
     for head in range(HEADS):
-        scr.overlap[b, head : head + 1, :] = jnp.sum(
-            both[head * HEAD_DIM : (head + 1) * HEAD_DIM], axis=0, keepdims=True
-        )
-    scr.attended_t[b] = d_att
+        there = slice(head * HEAD_DIM, (head + 1) * HEAD_DIM)
+        scaled = d_att[there] * scr.inverse[b, head : head + 1, :]
+        both = scaled * attended_t[there].astype(WIDE)
+        scr.overlap[b, head : head + 1, :] = jnp.sum(both, axis=0, keepdims=True)
+        scr.attended_t[b, there, :] = scaled.astype(LOW)
 
 
 def attend_back(b, cols, packed, segments, grads, scr):
@@ -251,25 +253,32 @@
         values = spread_heads(values_all[:, here], own_col)
         query_pair = by_sim(query, pair)
         d_att_pair = jnp.concatenate([d_att[here, :per_sim], d_att[here, per_sim:]], axis=0)
-        d_keys, d_values = [], []
+        d_share_pair = product(jnp.concatenate(values, axis=0), d_att_pair)
+        d_raws = []
         for h in range(2):
             head = 2 * pair + h
             there = slice(head * HEAD_DIM, (head + 1) * HEAD_DIM)
             both = scr.overlap[b, head : head + 1, :]
-            share = scr.weights_t[b, head]
-            d_share = product(values[h], d_att_pair)
+            d_share = d_share_pair[h * length : (h + 1) * length]
             d_raw = (
-                share.astype(WIDE) * (d_share - jnp.where(mask, both[:, :per_sim], both[:, per_sim:]))
+                scr.weights_t[b, head].astype(WIDE)
+                * (d_share - jnp.where(mask, both[:, :per_sim], both[:, per_sim:]))
             ).astype(LOW)
+            d_raws.append(d_raw)
             key_t = scr.keyval_t[b, there, :]
             key_sims = jnp.concatenate([key_t * low_row[0], key_t * low_row[1]], axis=0)
             d_q = (product(key_sims, d_raw) * 0.125).astype(LOW)
             scr.query_t[there, :per_sim] = d_q[:HEAD_DIM]
             scr.query_t[there, per_sim:] = d_q[HEAD_DIM:]
-            full = trans_right(share, d_att_pair)
-            d_values.append(jnp.where(mask, full[:, :block], full[:, block:]))
-            full = product(d_raw, query_pair)
-            d_keys.append(jnp.where(mask, full[:, :block], full[:, block:]))
+        shares = scr.weights_t[b, 2 * pair : 2 * pair + 2].reshape(2 * length, per_sim)
+        d_keys, d_values = [], []
+        for full, parts in (
+            (product(jnp.concatenate(d_raws, axis=0), query_pair), d_keys),
+            (trans_right(shares, d_att_pair), d_values),
+        ):
+            for h in range(2):
+                own = full[h * length : (h + 1) * length]
+                parts.append(jnp.where(mask, own[:, :block], own[:, block:]))
         scr.d_keyval[:, here] = jnp.where(left_half, d_keys[0], d_keys[1]).astype(LOW)
         scr.d_keyval[:, width + here.start : width + here.stop] = jnp.where(
             left_half, d_values[0], d_values[1]
@@ -303,6 +312,7 @@
         weights_t=pltpu.VMEM((count, HEADS, length, per_sim), LOW),
         attended_t=pltpu.VMEM((count, width, queries), LOW),
         overlap=pltpu.VMEM((count, 8, queries), WIDE),
+        inverse=pltpu.VMEM((count, 8, queries), WIDE),
         second=pltpu.VMEM((count, queries, width), LOW),
         second_t=pltpu.VMEM((width, count * queries), LOW),
         cot_t=pltpu.VMEM((width, count * queries), LOW),
@@ -1139,49 +1149,67 @@
     pieces = ([cols.msg_out], [cols.gain], [cols.base], [cols.q], [cols.kv], [cols.o], cols.up, cols.down)
     gain_at = 1
 
-    def body(latents, mod_share, point_mine, point_other, share, latents_out, mod_out, point_out, msg_in_out, *rest):
-        outs, (latents_buf, mod_buf, sems) = rest[:-3], rest[-3:]
-        arrays = ((latents, latents_buf, latents_out), (mod_share, mod_buf, mod_out))
-        arriving = [pltpu.make_async_copy(a, buf, sems.at[0, n]) for n, (a, buf, _) in enumerate(arrays)]
-        leaving = [pltpu.make_async_copy(buf, a, sems.at[1, n]) for n, (_, buf, a) in enumerate(arrays)]
+    shape = jax.ShapeDtypeStruct
+    outs = [shape(latents.shape, LOW), shape(mod_share.shape, WIDE), shape(point_mine.shape, WIDE)]
+    outs.append(shape((1, per, 2 * width), WIDE))
+    for n, piece in enumerate(pieces):
+        outs.append(shape((1, per) if n == gain_at else (1, per, sum(place.stop - place.start for place in piece)), WIDE))
+    inputs = (share, point_mine, point_other, latents, mod_share)
+    count = len(outs)
+
+    def body(*refs):
+        ins, refs = refs[: len(inputs)], refs[len(inputs) :]
+        results, refs = refs[:count], refs[count:]
+        held, refs = refs[: len(inputs)], refs[len(inputs) :]
+        made, sems = refs[:-1], refs[-1]
+        arriving = [pltpu.make_async_copy(a, b, sems.at[n]) for n, (a, b) in enumerate(zip(ins, held))]
         for move in arriving:
             move.start()
-        for first, then in zip(arriving, leaving):
-            first.wait()
-            then.start()
-        point_out[...] = point_mine[...].astype(WIDE) + point_other[...].astype(WIDE)
-        msg_in_out[0, :, :width] = share[:, cols.source].astype(WIDE)
-        msg_in_out[0, :, width:] = share[:, cols.target].astype(WIDE)
+        share, point_mine, point_other, latents, mod_share = held
+        sources = [latents, mod_share, *made]
+        leaving = [
+            pltpu.make_async_copy(a, b, sems.at[len(inputs) + n]) for n, (a, b) in enumerate(zip(sources, results))
+        ]
+        arriving[0].wait()
+        msg_in, parts = made[1], made[2:]
+        msg_in[0, :, :width] = share[:, cols.source].astype(WIDE)
+        msg_in[0, :, width:] = share[:, cols.target].astype(WIDE)
+        leaving[3].start()
         for n, piece in enumerate(pieces):
             at = 0
             for place in piece:
                 value = share[:, place].astype(WIDE)
                 size = place.stop - place.start
                 if n == gain_at:
-                    outs[n][...] = value.T[:1]
+                    parts[n][...] = value.T[:1]
                 else:
-                    outs[n][0, :, at : at + size] = value
+                    parts[n][0, :, at : at + size] = value
                 at += size
+            leaving[4 + n].start()
+        arriving[1].wait()
+        arriving[2].wait()
+        made[0][...] = point_mine[...].astype(WIDE) + point_other[...].astype(WIDE)
+        leaving[2].start()
+        for n in (0, 1):
+            arriving[3 + n].wait()
+            leaving[n].start()
         for move in leaving:
             move.wait()
 
-    shape = jax.ShapeDtypeStruct
-    whole, local = pl.BlockSpec(memory_space=pl.ANY), pl.BlockSpec(memory_space=pltpu.VMEM)
-    outs = [shape(latents.shape, LOW), shape(mod_share.shape, WIDE), shape(point_mine.shape, WIDE)]
-    outs.append(shape((1, per, 2 * width), WIDE))
-    for n, piece in enumerate(pieces):
-        outs.append(shape((1, per) if n == gain_at else (1, per, sum(place.stop - place.start for place in piece)), WIDE))
-    latents, mod, point_sum, msg_in, msg_out, gain, base, q, kv, o, up, down = pl.pallas_call(
+    whole = pl.BlockSpec(memory_space=pl.ANY)
+    results = pl.pallas_call(
         body,
         out_shape=outs,
-        in_specs=[whole, whole, local, local, local],
-        out_specs=[whole, whole] + [local] * (2 + len(pieces)),
-        scratch_shapes=[pltpu.VMEM(a.shape, a.dtype) for a in (latents, mod_share)]
-        + [pltpu.SemaphoreType.DMA((2, 2))],
+        in_specs=[whole] * len(inputs),
+        out_specs=[whole] * count,
+        scratch_shapes=[pltpu.VMEM(a.shape, a.dtype) for a in inputs]
+        + [pltpu.VMEM(a.shape, a.dtype) for a in outs[2:]]
+        + [pltpu.SemaphoreType.DMA((len(inputs) + count,))],
         compiler_params=pltpu.CompilerParams(vmem_limit_bytes=VMEM_BYTES),
         cost_estimate=pl.CostEstimate(flops=10**6, bytes_accessed=1 << 23, transcendentals=0),
         name="finish",
-    )(latents, mod_share, point_mine, point_other, share)
+    )(*inputs)
+    latents, mod, point_sum, msg_in, msg_out, gain, base, q, kv, o, up, down = results
     turn = lambda array: jnp.swapaxes(array, 1, 2)
     return (latents[None], point_sum, turn(msg_in), msg_out, gain, mod[None], turn(base), q, kv, o, up, turn(down))
 

time: 121 us -> 116 us (0.959)
  Pallas kernels: 120 us -> 115 us
    pallas_call x1, Pallas kernels: 114 us -> 112 us  [layer_call(): pl.pallas_call(body, out_shape=outs, in_specs=[spec] * len(inputs), out_s...]
    pallas_call x1, Pallas kernels: 5.22 us -> 3.2 us  [finish_call(): pl.pallas_call(body, out_shape=outs, in_specs=[whole] * len(inputs), out_...]
where the time goes in v4:
time: 116 us
  Pallas kernels  115 us (99%)
    pallas_call x1, Pallas kernels, layer_call(): pl.pallas_call(body, out_shape=outs, in_specs=[spec] * len(inputs), out_s...  112 us
    pallas_call x1, Pallas kernels, finish_call(): pl.pallas_call(body, out_shape=outs, in_specs=[whole] * len(inputs), out_...  3.2 us

profile of v4, /device:TPU:2, one launch (start us, length us, event | category | flops | bytes accessed | tf_op | source)
XLA Modules:
  0.0 116.2 jit_solution(13289908282101241922)
XLA Ops:
  0.7 112.2 %layers.1 = (bf16[3,512,384]{2,1,0:T(8,128)(2,1)}, bf16[3,256,384]{2,1,0:T(8,128)(2,1)}, bf16[3,256,384]{2,1,0:T(8,128)(2,1)}, bf16[48,6144]{1,0:T(8,128)(2,1)}, f32[48,1536]{1,0:T(8,128)}) custom-call(bf16[1,48,768]{2,1,0:T(8,128)(2,1)} %bitcast.16, bf16[1,48,384]{2,1,0:T(8,128)(2,1)} %refs_1_.1, bf16[1,48]{1,0:T(2,128)(2,1)} %refs_2_.1, ...), custom_call_target="tpu_custom_call" | custom-call | flops 10000000000 | bytes 16777216 | tf_op jit(solution)/shard_map/layers/pallas_call | solution.py:1133
  112.9 3.2 %finish.1 = (bf16[3,512,384]{2,1,0:T(8,128)(2,1)}, f32[48,1536]{1,0:T(8,128)}, f32[3,256,384]{2,1,0:T(8,128)}, f32[1,48,768]{2,1,0:T(8,128)}, f32[1,48,384]{2,1,...) custom-call(bf16[48,6144]{1,0:T(8,128)(2,1)} %get-tuple-element.29.r, ...), custom_call_target="tpu_custom_call" | custom-call | flops 1000000 | bytes 8388608 | tf_op jit(solution)/shard_map/finish/pallas_call | solution.py:1200

commit v5 on v4

--- a/solution.py
+++ b/solution.py
@@ -940,7 +940,7 @@
             feed_in(b, cols, packed, scr)
             return carry
 
-        lax.fori_loop(0, count, feed_first, 0)
+        lax.fori_loop(0, count, feed_first, 0, unroll=True)
         for at in range(CHUNKS):
             if linked and at > 0:
                 gather.finish(3 + at)
@@ -955,7 +955,7 @@
 
                 return carry
 
-            lax.fori_loop(0, count, feed_step, 0)
+            lax.fori_loop(0, count, feed_step, 0, unroll=True)
             grads[:, cols.down[at]] = product(scr.cot_t[...], scr.hidden[...])
             grads[:, cols.up[at]] = product(scr.second_t[...], scr.d_up[...])
             if linked:

time: 116 us -> 114 us (0.983)
  Pallas kernels: 115 us -> 113 us
    pallas_call x1, Pallas kernels: 112 us -> 110 us  [layer_call(): pl.pallas_call(body, out_shape=outs, in_specs=[spec] * len(inputs), out_s...]
where the time goes in v5:
time: 114 us
  Pallas kernels  113 us (99%)
    pallas_call x1, Pallas kernels, layer_call(): pl.pallas_call(body, out_shape=outs, in_specs=[spec] * len(inputs), out_s...  110 us
    pallas_call x1, Pallas kernels, finish_call(): pl.pallas_call(body, out_shape=outs, in_specs=[whole] * len(inputs), out_...  3.2 us

profile of v5, /device:TPU:2, one launch (start us, length us, event | category | flops | bytes accessed | tf_op | source)
XLA Modules:
  0.0 114.1 jit_solution(6326182575963938541)
XLA Ops:
  0.7 110.0 %layers.1 = (bf16[3,512,384]{2,1,0:T(8,128)(2,1)}, bf16[3,256,384]{2,1,0:T(8,128)(2,1)}, bf16[3,256,384]{2,1,0:T(8,128)(2,1)}, bf16[48,6144]{1,0:T(8,128)(2,1)}, f32[48,1536]{1,0:T(8,128)}) custom-call(bf16[1,48,768]{2,1,0:T(8,128)(2,1)} %bitcast.16, bf16[1,48,384]{2,1,0:T(8,128)(2,1)} %refs_1_.1, bf16[1,48]{1,0:T(2,128)(2,1)} %refs_2_.1, ...), custom_call_target="tpu_custom_call" | custom-call | flops 10000000000 | bytes 16777216 | tf_op jit(solution)/shard_map/layers/pallas_call | solution.py:1133
  110.7 3.2 %finish.1 = (bf16[3,512,384]{2,1,0:T(8,128)(2,1)}, f32[48,1536]{1,0:T(8,128)}, f32[3,256,384]{2,1,0:T(8,128)}, f32[1,48,768]{2,1,0:T(8,128)}, f32[1,48,384]{2,1,...) custom-call(bf16[48,6144]{1,0:T(8,128)(2,1)} %get-tuple-element.29.r, ...), custom_call_target="tpu_custom_call" | custom-call | flops 1000000 | bytes 8388608 | tf_op jit(solution)/shard_map/finish/pallas_call | solution.py:1200

commit v6 on v5

--- a/solution.py
+++ b/solution.py
@@ -80,12 +80,14 @@
             setattr(self, name, slice(at, at + extent))
             at += extent
         self.chunk = hidden // CHUNKS
-        self.up, self.down = [], []
-        for _ in range(CHUNKS):
-            self.up.append(slice(at, at + self.chunk))
-            self.down.append(slice(at + self.chunk, at + 2 * self.chunk))
+        self.order = (*range(1, CHUNKS), 0)
+        self.up, self.down = [None] * CHUNKS, [None] * CHUNKS
+        for n in self.order:
+            self.up[n] = slice(at, at + self.chunk)
+            self.down[n] = slice(at + self.chunk, at + 2 * self.chunk)
             at += 2 * self.chunk
-        self.mod = slice(at, at + 4 * width)
+        self.mod_two = slice(at, at + 2 * width)
+        self.mod_one = slice(at + 2 * width, at + 4 * width)
         at += 4 * width
         self.total = at
 
@@ -679,15 +681,16 @@
     groups = (
         (0, cols.msg_out.stop),
         (cols.kv.start, cols.base.stop),
-        (cols.mod.start, cols.mod.stop),
-    ) + parts
+        (cols.mod_one.start, cols.mod_one.stop),
+        (cols.up[0].start, cols.mod_two.stop),
+    ) + parts[1:]
     summed = (
         (0, cols.gain.stop),
         (cols.target.start, cols.msg_out.stop),
         (cols.kv.start, cols.kv.stop),
         (cols.q.start, cols.base.stop),
     ) + parts
-    many = cols.mod.start
+    many = cols.mod_two.start
     rows = 8
     weights_in = list(raw) if linked else [packed_in]
     inputs = weights_in + [points, segments, neighbours, condition, cotangent]
@@ -789,7 +792,8 @@
             mine[:, cols.q] = q_weight[0]
             mine[:, cols.o] = o_weight[0]
             mine[:, cols.base] = query_base[0]
-            mine[:, cols.mod] = mod_weight[0]
+            mine[:, cols.mod_one] = mod_weight[0, :, : 2 * width]
+            mine[:, cols.mod_two] = mod_weight[0, :, 2 * width :]
             for n in range(CHUNKS):
                 piece = slice(n * cols.chunk, (n + 1) * cols.chunk)
                 mine[:, cols.up[n]] = up_weight[0, :, piece]
@@ -860,7 +864,7 @@
             scr.base_unit[...] = unit
             scr.base_scale[...] = scale
             scr.gain_row[...] = packed[:, cols.gain].astype(WIDE).T[:1]
-            scr.modulation[...] = product(scr.condition[...].astype(LOW), packed[:, cols.mod])[:rows]
+            scr.modulation[:, : 2 * width] = product(scr.condition[...].astype(LOW), packed[:, cols.mod_one])[:rows]
 
         def gather_step(n):
             if n == 0:
@@ -935,6 +939,8 @@
                 )
                 for n in range(len(summed))
             ]
+
+        scr.modulation[:, 2 * width :] = product(scr.condition[...].astype(LOW), packed[:, cols.mod_two])[:rows]
 
         def feed_first(b, carry):
             feed_in(b, cols, packed, scr)
@@ -1267,12 +1273,16 @@
             query_base[0].T,
             *sum(
                 (
-                    [up_weight[0, :, n : n + cols.chunk], down_weight[0, n : n + cols.chunk].T]
-                    for n in range(0, hidden, cols.chunk)
+                    [
+                        up_weight[0, :, n * cols.chunk : (n + 1) * cols.chunk],
+                        down_weight[0, n * cols.chunk : (n + 1) * cols.chunk].T,
+                    ]
+                    for n in cols.order
                 ),
                 [],
             ),
-            mod_weight[0],
+            mod_weight[0, :, 2 * width :],
+            mod_weight[0, :, : 2 * width],
         ],
         axis=1,
     )
@@ -1289,7 +1299,7 @@
         jnp.concatenate([share[:, cols.source], share[:, cols.target]], axis=1).T[None],
         share[None, :, cols.msg_out],
         share[None, :, cols.gain.start],
-        share[None, :, cols.mod],
+        share[None, :, cols.mod_two.start :],
         share[:, cols.base].T[None],
         share[None, :, cols.q],
         share[None, :, cols.kv],

time: 114 us -> 116 us (1.018)
  Pallas kernels: 113 us -> 115 us
    pallas_call x1, Pallas kernels: 110 us -> 112 us  [layer_call(): pl.pallas_call(body, out_shape=outs, in_specs=[spec] * len(inputs), out_s...]
where the time goes in v6:
time: 116 us
  Pallas kernels  115 us (99%)
    pallas_call x1, Pallas kernels, layer_call(): pl.pallas_call(body, out_shape=outs, in_specs=[spec] * len(inputs), out_s...  112 us
    pallas_call x1, Pallas kernels, finish_call(): pl.pallas_call(body, out_shape=outs, in_specs=[whole] * len(inputs), out_...  3.2 us

profile of v6, /device:TPU:2, one launch (start us, length us, event | category | flops | bytes accessed | tf_op | source)
XLA Modules:
  0.0 115.8 jit_solution(8199031903059609419)
XLA Ops:
  0.7 111.8 %layers.1 = (bf16[3,512,384]{2,1,0:T(8,128)(2,1)}, bf16[3,256,384]{2,1,0:T(8,128)(2,1)}, bf16[3,256,384]{2,1,0:T(8,128)(2,1)}, bf16[48,6144]{1,0:T(8,128)(2,1)}, f32[48,1536]{1,0:T(8,128)}) custom-call(bf16[1,48,768]{2,1,0:T(8,128)(2,1)} %bitcast.16, bf16[1,48,384]{2,1,0:T(8,128)(2,1)} %refs_1_.1, bf16[1,48]{1,0:T(2,128)(2,1)} %refs_2_.1, ...), custom_call_target="tpu_custom_call" | custom-call | flops 10000000000 | bytes 16777216 | tf_op jit(solution)/shard_map/layers/pallas_call | solution.py:1139
  112.5 3.2 %finish.1 = (bf16[3,512,384]{2,1,0:T(8,128)(2,1)}, f32[48,1536]{1,0:T(8,128)}, f32[3,256,384]{2,1,0:T(8,128)}, f32[1,48,768]{2,1,0:T(8,128)}, f32[1,48,384]{2,1,...) custom-call(bf16[48,6144]{1,0:T(8,128)(2,1)} %get-tuple-element.29.r, ...), custom_call_target="tpu_custom_call" | custom-call | flops 1000000 | bytes 8388608 | tf_op jit(solution)/shard_map/finish/pallas_call | solution.py:1206
